TPU v7x, 256 devices: a whole 4x4x8 slice. The times are simulated.
256 devices in a mesh: blk: 4 (over x), width: 16 (over z, core), rep: 4 (over y).
Axes of the slice: x: 4, y: 4, z: 8, core: 2. Of those that a mesh axis runs over, the one named last changes fastest.
Arguments:
- inputs: bfloat16 [2048, 7168], P(('blk', 'rep'), 'width'), may hold values from -6 to 6
- targets: bfloat16 [2048, 7168], P(('blk', 'rep'), 'width'), may hold values from -48 to 48
- enc_weight: bfloat16 [7168, 2048], P('width', 'blk'), may hold values from -0.0625 to 0.0625
- enc_bias: float32 [2048], P('blk'), may hold values from -3 to 3
- dec_weight: bfloat16 [2048, 7168], P('blk', 'width'), may hold values from -0.125 to 0.125
- dead_mask: int32 [2048], P('blk'), may hold values 0 or 1
- aux_picks: int32 [2048, 512], P(('blk', 'rep')), may hold values from 0 to 2047, all different within a row
Outputs:
- loss: float32 [], replicated
- grad_enc: float32 [7168, 2048], P(('width', 'rep'), 'blk')
- grad_bias: float32 [2048], P(('blk', 'rep'))
- grad_dec: float32 [2048, 7168], P('blk', ('width', 'rep'))
Inputs may be any that keep to these rules, and one draw needn't show every extreme that they name: `aux_picks`: each row names 512 different latents; every latent is named by some row.
All inputs are finite; a program needn't handle non-finite values. No bound on the sum of `dead_mask` on one device may be relied on, other than what follows from the above.
Results may differ from a plain program's by a relative error of at most 0.025.
Values may be sent and summed in bfloat16 or wider, within the bound.
No kernel may reach another device: no remote copies, remote signals or barrier semaphores. Data moves between devices by JAX's collectives and lax.ppermute only.
A program may use at most 64 MiB of HBM per device.

v0:
```python
import math

import jax
import jax.numpy as jnp
from jax import lax
from jax.sharding import PartitionSpec as P


def shifted_2(block, axis, distance):
    devices = range(lax.axis_size(axis))
    route = [((i - distance) % len(devices), i) for i in devices]
    return lax.ppermute(block, axis, route)


def encode(block_x, enc_weight, enc_bias):
    partial_value = jnp.dot(block_x, enc_weight, preferred_element_type=jnp.float32)
    return lax.psum(partial_value, "width") + enc_bias[None, :]


def pick_gate(pick_rows, dead_mask, first_latent):
    lat_count = dead_mask.shape[0]
    row_count, pick_count = pick_rows.shape
    group_size = math.gcd(pick_count, 32)
    local_ids = pick_rows - first_latent
    grouped = jnp.moveaxis(local_ids.reshape(row_count, pick_count // group_size, group_size), 1, 0)
    columns = jnp.arange(lat_count, dtype=jnp.int32)[None, None, :]

    def add_group(total, group):
        hits = jnp.where(group[:, :, None] == columns, 1.0, 0.0).astype(jnp.float32)
        return (total + jnp.sum(hits, axis=1), None)

    start = jnp.zeros((row_count, lat_count), jnp.float32)
    picked, unused = lax.scan(add_group, start, grouped)
    return picked * jnp.where(dead_mask == 1, 1.0, 0.0).astype(jnp.float32)[None, :]


def forward_work(block_x, pick_rows, running, running_aux, weights):
    enc_weight, enc_bias, dec_weight, dead_mask, first_latent = weights
    preact = encode(block_x, enc_weight, enc_bias)
    latents = jnp.maximum(preact, 0.0).astype(jnp.bfloat16)
    aux_gate = pick_gate(pick_rows, dead_mask, first_latent)
    aux_latents = latents * aux_gate.astype(jnp.bfloat16)
    decoded = jnp.dot(
        jnp.concatenate([latents, aux_latents], 0), dec_weight, preferred_element_type=jnp.float32
    )
    row_count = block_x.shape[0]
    return (running + decoded[:row_count], running_aux + decoded[row_count:], preact, aux_gate)


def backward_work(grad_main, grad_aux, preact, aux_gate, dec_weight):
    stacked = jnp.concatenate([grad_main, grad_aux], 0)
    pulled = lax.dot_general(
        stacked, dec_weight, (((1,), (1,)), ((), ())), preferred_element_type=jnp.float32
    )
    row_count = grad_main.shape[0]
    partial_value = pulled[:row_count] + pulled[row_count:] * aux_gate
    summed = lax.psum(partial_value.astype(jnp.bfloat16), "width").astype(jnp.float32)
    return jnp.where(preact > 0.0, summed, 0.0)


def local(inputs, targets, enc_weight, enc_bias, dec_weight, dead_mask, aux_picks):
    cycle_size = lax.axis_size("blk")
    width_size = lax.axis_size("width")
    rep_size = lax.axis_size("rep")
    block_rows, half_width = inputs.shape
    lat_count = dec_weight.shape[0]
    first_latent = lax.axis_index("blk") * lat_count
    weights = (enc_weight, enc_bias, dec_weight, dead_mask, first_latent)
    empty = jnp.zeros((block_rows, half_width), jnp.float32)

    def forward_step(state, unused):
        block_x, pick_rows, running, running_aux = state
        running, running_aux, preact, aux_gate = forward_work(
            block_x, pick_rows, running, running_aux, weights
        )
        shifted = (
            shifted_2(block_x, "blk", 1),
            shifted_2(pick_rows, "blk", 1),
            shifted_2(running.astype(jnp.bfloat16), "blk", 1).astype(running.dtype),
            shifted_2(running_aux.astype(jnp.bfloat16), "blk", 1).astype(running_aux.dtype),
        )
        return (shifted, (block_x, preact, aux_gate))

    final, stored = lax.scan(
        forward_step, (inputs, aux_picks, empty, empty), None, length=cycle_size
    )
    recon = final[2]
    recon_aux = final[3]
    stored_x, stored_pre, stored_gate = stored
    total_tokens = block_rows * cycle_size * rep_size
    norm_scale = 1.0 / math.sqrt(total_tokens)
    error = targets.astype(jnp.float32) - recon
    error_aux = error - recon_aux
    loss_part = jnp.sum(error * error) + jnp.sum(error_aux * error_aux)
    grad_main = (-error * norm_scale).astype(jnp.bfloat16)
    grad_aux = (-error_aux * norm_scale).astype(jnp.bfloat16)

    def backward_step(state, slices):
        main_rows, aux_rows = state
        grad_pre = backward_work(main_rows, aux_rows, slices[0], slices[1], dec_weight)
        shifted = shifted_2((main_rows, aux_rows), "blk", 1)
        return (shifted, (main_rows, aux_rows, grad_pre))

    final_back, kept = lax.scan(
        backward_step, (grad_main, grad_aux), (stored_pre[:-1], stored_gate[:-1])
    )
    last_main = final_back[0]
    last_aux = final_back[1]
    last_pre = backward_work(last_main, last_aux, stored_pre[-1], stored_gate[-1], dec_weight)
    all_main = jnp.concatenate([kept[0], last_main[None]], 0).reshape(-1, half_width)
    all_aux = jnp.concatenate([kept[1], last_aux[None]], 0).reshape(-1, half_width)
    grad_pre = jnp.concatenate([kept[2], last_pre[None]], 0).reshape(-1, lat_count)
    flat_x = stored_x.reshape(-1, half_width)
    flat_pre = stored_pre.reshape(-1, lat_count)
    flat_gate = stored_gate.reshape(-1, lat_count)
    latents = jnp.maximum(flat_pre, 0.0).astype(jnp.bfloat16)
    aux_latents = latents * flat_gate.astype(jnp.bfloat16)
    contract_rows = (((0,), (0,)), ((), ()))
    enc_term = lax.dot_general(
        flat_x, grad_pre.astype(jnp.bfloat16), contract_rows, preferred_element_type=jnp.float32
    )
    dec_term = lax.dot_general(
        jnp.concatenate([latents, aux_latents], 0),
        jnp.concatenate([all_main, all_aux], 0),
        contract_rows,
        preferred_element_type=jnp.float32,
    )
    bias_term = jnp.sum(grad_pre, axis=0)
    grad_enc, grad_dec, grad_bias = (
        lax.psum_scatter(
            enc_term.astype(jnp.bfloat16), "rep", scatter_dimension=0, tiled=True
        ).astype(jnp.float32),
        lax.psum_scatter(
            dec_term.astype(jnp.bfloat16), "rep", scatter_dimension=1, tiled=True
        ).astype(jnp.float32),
        lax.psum_scatter(
            bias_term.astype(jnp.bfloat16), "rep", scatter_dimension=0, tiled=True
        ).astype(jnp.float32),
    )
    loss = lax.psum(loss_part, ("blk", "width", "rep")) / (total_tokens * half_width * width_size)
    return (loss, grad_enc, grad_bias, grad_dec)


def solution(mesh):
    in_specs = (
        P(("blk", "rep"), "width"),
        P(("blk", "rep"), "width"),
        P("width", "blk"),
        P("blk"),
        P("blk", "width"),
        P("blk"),
        P(("blk", "rep"), None),
    )
    out_specs = (P(), P(("width", "rep"), "blk"), P(("blk", "rep")), P("blk", ("width", "rep")))
    return jax.shard_map(local, mesh=mesh, in_specs=in_specs, out_specs=out_specs, check_vma=False)
```

profile of v0, /device:TPU:32, one launch (start us, length us, event | category | flops | bytes accessed | tf_op | source)
XLA Modules:
  0.0 1053.1 jit_solution(1934383743147883233)
XLA Ops:
  10.0 485.2 %while.59 = (s32[]{:T(128)}, bf16[128,448]{0,1:T(8,128)(2,1)S(1)}, s32[128,512]{0,1:T(8,128)S(1)}, f32[128,448]{0,1:T(8,128)S(1)}, f32[128,448]{0,1:T(8,128)S(1)...) while((s32[]{:T(128)}, bf16[128,448]{0,1:T(8,128)(2,1)S(1)}, ...), condition=%wide.region_5.6_spmd.clone.clone, body=%wide.region_0.5_spmd.clone.sunk.clone | while | flops 184157184 | bytes 17068676 | solution.py:84
  14.3 48.9 %while.58 = (s32[]{:T(128)}, f32[128,512]{1,0:T(8,128)S(1)}, s32[16,128,32]{1,2,0:T(8,128)S(1)}, s32[]{:T(128)}, s32[]{:T(128)}) while((s32[]{:T(128)}, f32[128,512]{1,0:T(8,128)S(1)}, s32[16,128,32]{1,2,0:T(8,128)S(1)}, s32[]{:T(128)}, s32[]{:T(128)}) %tuple.117), condition=%wide.region_4.4_spmd.clone, body=%wide.region_2.3_spmd.clone.sunk | while | flops 6356995 | bytes 1130579 | solution.py:33
  14.4 2.8 select_reduce_fusion.2
  17.5 2.8 select_reduce_fusion.2
  20.5 2.8 select_reduce_fusion.2
  23.6 2.8 select_reduce_fusion.2
  26.6 2.8 select_reduce_fusion.2
  38.9 2.8 select_reduce_fusion.2
  41.9 2.8 select_reduce_fusion.2
  45.0 2.8 select_reduce_fusion.2
  48.0 2.8 select_reduce_fusion.2
  51.1 2.8 select_reduce_fusion.2
  54.2 2.8 select_reduce_fusion.2
  57.2 2.8 select_reduce_fusion.2
  64.6 57.1 %all-reduce.9.cloned.1.call-done = f32[128,512]{1,0:T(8,128)} async-done(((f32[128,512]{1,0:T(8,128)}), f32[128,512]{1,0:T(8,128)}) %all-reduce.9.cloned.1.call-update) | async-done | bytes 262160 | tf_op jit(solution)/shard_map/while/body/eval_jaxpr/psum | solution.py:17
  126.2 4.2 collective-permute-done.4
  135.2 48.9 %while.58 = (s32[]{:T(128)}, f32[128,512]{1,0:T(8,128)S(1)}, s32[16,128,32]{1,2,0:T(8,128)S(1)}, s32[]{:T(128)}, s32[]{:T(128)}) while((s32[]{:T(128)}, f32[128,512]{1,0:T(8,128)S(1)}, s32[16,128,32]{1,2,0:T(8,128)S(1)}, s32[]{:T(128)}, s32[]{:T(128)}) %tuple.117), condition=%wide.region_4.4_spmd.clone, body=%wide.region_2.3_spmd.clone.sunk | while | flops 6356995 | bytes 1130579 | solution.py:33
  135.3 2.8 select_reduce_fusion.2
  138.4 2.8 select_reduce_fusion.2
  141.4 2.8 select_reduce_fusion.2
  144.5 2.8 select_reduce_fusion.2
  147.5 2.8 select_reduce_fusion.2
  150.6 2.8 select_reduce_fusion.2
  153.7 2.8 select_reduce_fusion.2
  165.9 2.8 select_reduce_fusion.2
  168.9 2.8 select_reduce_fusion.2
  172.0 2.8 select_reduce_fusion.2
  175.1 2.8 select_reduce_fusion.2
  178.1 2.8 select_reduce_fusion.2
  181.2 2.8 select_reduce_fusion.2
  185.5 57.3 %all-reduce.9.cloned.1.call-done = f32[128,512]{1,0:T(8,128)} async-done(((f32[128,512]{1,0:T(8,128)}), f32[128,512]{1,0:T(8,128)}) %all-reduce.9.cloned.1.call-update) | async-done | bytes 262160 | tf_op jit(solution)/shard_map/while/body/eval_jaxpr/psum | solution.py:17
  247.3 4.2 collective-permute-done.4
  256.3 48.9 %while.58 = (s32[]{:T(128)}, f32[128,512]{1,0:T(8,128)S(1)}, s32[16,128,32]{1,2,0:T(8,128)S(1)}, s32[]{:T(128)}, s32[]{:T(128)}) while((s32[]{:T(128)}, f32[128,512]{1,0:T(8,128)S(1)}, s32[16,128,32]{1,2,0:T(8,128)S(1)}, s32[]{:T(128)}, s32[]{:T(128)}) %tuple.117), condition=%wide.region_4.4_spmd.clone, body=%wide.region_2.3_spmd.clone.sunk | while | flops 6356995 | bytes 1130579 | solution.py:33
  256.4 2.8 select_reduce_fusion.2
  259.5 2.8 select_reduce_fusion.2
  262.6 2.8 select_reduce_fusion.2
  306.6 57.2 %all-reduce.9.cloned.1.call-done = f32[128,512]{1,0:T(8,128)} async-done(((f32[128,512]{1,0:T(8,128)}), f32[128,512]{1,0:T(8,128)}) %all-reduce.9.cloned.1.call-update) | async-done | bytes 262160 | tf_op jit(solution)/shard_map/while/body/eval_jaxpr/psum | solution.py:17
  368.3 4.2 collective-permute-done.4
  377.3 48.9 %while.58 = (s32[]{:T(128)}, f32[128,512]{1,0:T(8,128)S(1)}, s32[16,128,32]{1,2,0:T(8,128)S(1)}, s32[]{:T(128)}, s32[]{:T(128)}) while((s32[]{:T(128)}, f32[128,512]{1,0:T(8,128)S(1)}, s32[16,128,32]{1,2,0:T(8,128)S(1)}, s32[]{:T(128)}, s32[]{:T(128)}) %tuple.117), condition=%wide.region_4.4_spmd.clone, body=%wide.region_2.3_spmd.clone.sunk | while | flops 6356995 | bytes 1130579 | solution.py:33
  427.6 57.2 %all-reduce.9.cloned.1.call-done = f32[128,512]{1,0:T(8,128)} async-done(((f32[128,512]{1,0:T(8,128)}), f32[128,512]{1,0:T(8,128)}) %all-reduce.9.cloned.1.call-update) | async-done | bytes 262160 | tf_op jit(solution)/shard_map/while/body/eval_jaxpr/psum | solution.py:17
  489.3 4.2 collective-permute-done.4
  498.5 337.5 %while.57 = (s32[]{:T(128)}, bf16[128,448]{1,0:T(8,128)(2,1)S(1)}, bf16[128,448]{1,0:T(8,128)(2,1)S(1)}, bf16[3,128,448]{2,1,0:T(8,128)(2,1)S(1)}, bf16[3,128,44...) while((s32[]{:T(128)}, bf16[128,448]{1,0:T(8,128)(2,1)S(1)}, ...), condition=%wide.region_11.12_spmd.clone, body=%wide.region_9.11_spmd.sunk.clone | while | flops 118358016 | bytes 5472489 | solution.py:104
  502.2 105.9 %all-reduce.7.cloned.1.call-done = bf16[128,512]{1,0:T(8,128)(2,1)} async-done(((bf16[128,512]{1,0:T(8,128)(2,1)}), bf16[128,512]{1,0:T(8,128)(2,1)}) %all-reduce.7.cloned.1.call-update) | async-done | bytes 131088 | tf_op jit(solution)/shard_map/while/body/eval_jaxpr/psum | solution.py:57
  614.7 106.4 %all-reduce.7.cloned.1.call-done = bf16[128,512]{1,0:T(8,128)(2,1)} async-done(((bf16[128,512]{1,0:T(8,128)(2,1)}), bf16[128,512]{1,0:T(8,128)(2,1)}) %all-reduce.7.cloned.1.call-update) | async-done | bytes 131088 | tf_op jit(solution)/shard_map/while/body/eval_jaxpr/psum | solution.py:57
  727.7 106.8 %all-reduce.7.cloned.1.call-done = bf16[128,512]{1,0:T(8,128)(2,1)} async-done(((bf16[128,512]{1,0:T(8,128)(2,1)}), bf16[128,512]{1,0:T(8,128)(2,1)}) %all-reduce.7.cloned.1.call-update) | async-done | bytes 131088 | tf_op jit(solution)/shard_map/while/body/eval_jaxpr/psum | solution.py:57
  842.6 104.4 %all-reduce.5.cloned.1.call-done = bf16[128,512]{1,0:T(8,128)(2,1)} async-done(((bf16[128,512]{1,0:T(8,128)(2,1)}), bf16[128,512]{1,0:T(8,128)(2,1)}) %all-reduce.5.cloned.1.call-update) | async-done | bytes 131088 | tf_op jit(solution)/shard_map/psum | solution.py:57
  951.5 79.2 %psum.28 = f32[]{:T(128)} all-reduce(f32[]{:T(128)S(6)} %add.49), channel_id=1, replica_groups=mesh['blk'=4,'width'=16,'rep'=4] {'blk','width','rep'}, use_global_device_ids=true, to_apply=%region_8.9 | all-reduce | flops 1 | bytes 8 | tf_op jit(solution)/shard_map/psum | solution.py:140
  1032.6 8.5 all-reduce
  (446 shorter events, 194.5 us)
Async XLA Ops:
  10.0 111.7 %all-reduce.9.cloned.1.call-start = ((), (), s32[]{:S(2)}) async-start(), calls=%async_computation.6 | async-start | bytes 524288 | tf_op jit(solution)/shard_map/while/body/eval_jaxpr/psum | solution.py:17
  10.1 122.0 %collective-permute-start.2 = (bf16[128,448]{0,1:T(8,128)(2,1)S(1)}, bf16[128,448]{0,1:T(8,128)(2,1)S(1)}, u32[]{:S(2)}, u32[]{:S(2)}) collective-permute-start(bf16[128,448]{0,1:T(8,128)(2,1)S(1)} %copy.51), channel_id=1, source_target_pairs={{192,0},{0,64},{64,128},{128,192},{193,1},{1,65},{65,129},{129,193... | collective-permute-start | bytes 344072 | tf_op jit(solution)/shard_map/while/body/eval_jaxpr/ppermute | solution.py:12
  11.7 120.5 %collective-permute-start.3 = (s32[128,512]{0,1:T(8,128)S(1)}, s32[128,512]{0,1:T(8,128)S(1)}, u32[]{:S(2)}, u32[]{:S(2)}) collective-permute-start(s32[128,512]{0,1:T(8,128)S(1)} %copy.52), channel_id=1, source_target_pairs={{192,0},{0,64},{64,128},{128,192},{193,1},{1,65},{65,129},{129,193... | collective-permute-start | bytes 786440 | tf_op jit(solution)/shard_map/while/body/eval_jaxpr/ppermute | solution.py:12
  14.3 49.0 %copy-start.8 = (s32[512]{0:T(512)S(1)}, s32[512]{0:T(512)}, u32[]{:S(2)}) copy-start(s32[512]{0:T(512)} %get-tuple-element.664) | copy-start | bytes 6148 | tf_op jit(solution)/shard_map/while
  14.3 107.4 %copy-start.7 = (f32[512]{0:T(512)S(1)}, f32[512]{0:T(512)}, u32[]{:S(2)}) copy-start(f32[512]{0:T(512)} %get-tuple-element.662) | copy-start | bytes 6148 | tf_op jit(solution)/shard_map/while
  63.2 59.5 %copy-start = (bf16[512,448]{0,1:T(8,128)(2,1)S(1)}, bf16[512,448]{0,1:T(8,128)(2,1)}, u32[]{:S(2)}) copy-start(bf16[512,448]{0,1:T(8,128)(2,1)} %get-tuple-element.665) | copy-start | bytes 1376260 | tf_op jit(solution)/shard_map/while
  122.7 3.4 copy-start.2
  123.2 7.3 collective-permute-start.4
  124.7 7.4 collective-permute-start.5
  132.2 110.7 %all-reduce.9.cloned.1.call-start = ((), (), s32[]{:S(2)}) async-start(), calls=%async_computation.6 | async-start | bytes 524288 | tf_op jit(solution)/shard_map/while/body/eval_jaxpr/psum | solution.py:17
  132.2 121.0 %collective-permute-start.2 = (bf16[128,448]{0,1:T(8,128)(2,1)S(1)}, bf16[128,448]{0,1:T(8,128)(2,1)S(1)}, u32[]{:S(2)}, u32[]{:S(2)}) collective-permute-start(bf16[128,448]{0,1:T(8,128)(2,1)S(1)} %copy.51), channel_id=1, source_target_pairs={{192,0},{0,64},{64,128},{128,192},{193,1},{1,65},{65,129},{129,193... | collective-permute-start | bytes 344072 | tf_op jit(solution)/shard_map/while/body/eval_jaxpr/ppermute | solution.py:12
  132.6 120.7 %collective-permute-start.3 = (s32[128,512]{0,1:T(8,128)S(1)}, s32[128,512]{0,1:T(8,128)S(1)}, u32[]{:S(2)}, u32[]{:S(2)}) collective-permute-start(s32[128,512]{0,1:T(8,128)S(1)} %copy.52), channel_id=1, source_target_pairs={{192,0},{0,64},{64,128},{128,192},{193,1},{1,65},{65,129},{129,193... | collective-permute-start | bytes 786440 | tf_op jit(solution)/shard_map/while/body/eval_jaxpr/ppermute | solution.py:12
  135.2 49.0 %copy-start.8 = (s32[512]{0:T(512)S(1)}, s32[512]{0:T(512)}, u32[]{:S(2)}) copy-start(s32[512]{0:T(512)} %get-tuple-element.664) | copy-start | bytes 6148 | tf_op jit(solution)/shard_map/while
  135.2 107.7 %copy-start.7 = (f32[512]{0:T(512)S(1)}, f32[512]{0:T(512)}, u32[]{:S(2)}) copy-start(f32[512]{0:T(512)} %get-tuple-element.662) | copy-start | bytes 6148 | tf_op jit(solution)/shard_map/while
  184.1 59.8 %copy-start = (bf16[512,448]{0,1:T(8,128)(2,1)S(1)}, bf16[512,448]{0,1:T(8,128)(2,1)}, u32[]{:S(2)}) copy-start(bf16[512,448]{0,1:T(8,128)(2,1)} %get-tuple-element.665) | copy-start | bytes 1376260 | tf_op jit(solution)/shard_map/while
  243.9 3.4 copy-start.2
  244.3 7.3 collective-permute-start.4
  245.8 7.4 collective-permute-start.5
  253.3 110.5 %all-reduce.9.cloned.1.call-start = ((), (), s32[]{:S(2)}) async-start(), calls=%async_computation.6 | async-start | bytes 524288 | tf_op jit(solution)/shard_map/while/body/eval_jaxpr/psum | solution.py:17
  253.4 120.9 %collective-permute-start.2 = (bf16[128,448]{0,1:T(8,128)(2,1)S(1)}, bf16[128,448]{0,1:T(8,128)(2,1)S(1)}, u32[]{:S(2)}, u32[]{:S(2)}) collective-permute-start(bf16[128,448]{0,1:T(8,128)(2,1)S(1)} %copy.51), channel_id=1, source_target_pairs={{192,0},{0,64},{64,128},{128,192},{193,1},{1,65},{65,129},{129,193... | collective-permute-start | bytes 344072 | tf_op jit(solution)/shard_map/while/body/eval_jaxpr/ppermute | solution.py:12
  253.7 120.5 %collective-permute-start.3 = (s32[128,512]{0,1:T(8,128)S(1)}, s32[128,512]{0,1:T(8,128)S(1)}, u32[]{:S(2)}, u32[]{:S(2)}) collective-permute-start(s32[128,512]{0,1:T(8,128)S(1)} %copy.52), channel_id=1, source_target_pairs={{192,0},{0,64},{64,128},{128,192},{193,1},{1,65},{65,129},{129,193... | collective-permute-start | bytes 786440 | tf_op jit(solution)/shard_map/while/body/eval_jaxpr/ppermute | solution.py:12
  256.3 49.0 %copy-start.8 = (s32[512]{0:T(512)S(1)}, s32[512]{0:T(512)}, u32[]{:S(2)}) copy-start(s32[512]{0:T(512)} %get-tuple-element.664) | copy-start | bytes 6148 | tf_op jit(solution)/shard_map/while
  256.3 107.5 %copy-start.7 = (f32[512]{0:T(512)S(1)}, f32[512]{0:T(512)}, u32[]{:S(2)}) copy-start(f32[512]{0:T(512)} %get-tuple-element.662) | copy-start | bytes 6148 | tf_op jit(solution)/shard_map/while
  305.2 59.6 %copy-start = (bf16[512,448]{0,1:T(8,128)(2,1)S(1)}, bf16[512,448]{0,1:T(8,128)(2,1)}, u32[]{:S(2)}) copy-start(bf16[512,448]{0,1:T(8,128)(2,1)} %get-tuple-element.665) | copy-start | bytes 1376260 | tf_op jit(solution)/shard_map/while
  365.3 7.3 collective-permute-start.4
  366.8 7.4 collective-permute-start.5
  374.3 110.5 %all-reduce.9.cloned.1.call-start = ((), (), s32[]{:S(2)}) async-start(), calls=%async_computation.6 | async-start | bytes 524288 | tf_op jit(solution)/shard_map/while/body/eval_jaxpr/psum | solution.py:17
  374.3 120.9 %collective-permute-start.2 = (bf16[128,448]{0,1:T(8,128)(2,1)S(1)}, bf16[128,448]{0,1:T(8,128)(2,1)S(1)}, u32[]{:S(2)}, u32[]{:S(2)}) collective-permute-start(bf16[128,448]{0,1:T(8,128)(2,1)S(1)} %copy.51), channel_id=1, source_target_pairs={{192,0},{0,64},{64,128},{128,192},{193,1},{1,65},{65,129},{129,193... | collective-permute-start | bytes 344072 | tf_op jit(solution)/shard_map/while/body/eval_jaxpr/ppermute | solution.py:12
  374.7 120.5 %collective-permute-start.3 = (s32[128,512]{0,1:T(8,128)S(1)}, s32[128,512]{0,1:T(8,128)S(1)}, u32[]{:S(2)}, u32[]{:S(2)}) collective-permute-start(s32[128,512]{0,1:T(8,128)S(1)} %copy.52), channel_id=1, source_target_pairs={{192,0},{0,64},{64,128},{128,192},{193,1},{1,65},{65,129},{129,193... | collective-permute-start | bytes 786440 | tf_op jit(solution)/shard_map/while/body/eval_jaxpr/ppermute | solution.py:12
  377.3 49.0 %copy-start.8 = (s32[512]{0:T(512)S(1)}, s32[512]{0:T(512)}, u32[]{:S(2)}) copy-start(s32[512]{0:T(512)} %get-tuple-element.664) | copy-start | bytes 6148 | tf_op jit(solution)/shard_map/while
  377.3 107.5 %copy-start.7 = (f32[512]{0:T(512)S(1)}, f32[512]{0:T(512)}, u32[]{:S(2)}) copy-start(f32[512]{0:T(512)} %get-tuple-element.662) | copy-start | bytes 6148 | tf_op jit(solution)/shard_map/while
  426.2 59.6 %copy-start = (bf16[512,448]{0,1:T(8,128)(2,1)S(1)}, bf16[512,448]{0,1:T(8,128)(2,1)}, u32[]{:S(2)}) copy-start(bf16[512,448]{0,1:T(8,128)(2,1)} %get-tuple-element.665) | copy-start | bytes 1376260 | tf_op jit(solution)/shard_map/while
  486.2 7.3 collective-permute-start.4
  487.8 7.4 collective-permute-start.5
  498.6 109.6 %all-reduce.7.cloned.1.call-start = ((), (), s32[]{:S(2)}) async-start(), calls=%async_computation.5 | async-start | bytes 262144 | tf_op jit(solution)/shard_map/while/body/eval_jaxpr/psum | solution.py:57
  498.6 111.2 %collective-permute-start = (bf16[128,448]{1,0:T(8,128)(2,1)S(1)}, bf16[128,448]{1,0:T(8,128)(2,1)S(1)}, u32[]{:S(2)}, u32[]{:S(2)}) collective-permute-start(bf16[128,448]{1,0:T(8,128)(2,1)S(1)} %copy.73), channel_id=1, source_target_pairs={{192,0},{0,64},{64,128},{128,192},{193,1},{1,65},{65,129},{129,193... | collective-permute-start | bytes 344072 | tf_op jit(solution)/shard_map/while/body/eval_jaxpr/ppermute | solution.py:12
  499.0 110.8 %collective-permute-start.1 = (bf16[128,448]{1,0:T(8,128)(2,1)S(1)}, bf16[128,448]{1,0:T(8,128)(2,1)S(1)}, u32[]{:S(2)}, u32[]{:S(2)}) collective-permute-start(bf16[128,448]{1,0:T(8,128)(2,1)S(1)} %copy.74), channel_id=1, source_target_pairs={{192,0},{0,64},{64,128},{128,192},{193,1},{1,65},{65,129},{129,193... | collective-permute-start | bytes 344072 | tf_op jit(solution)/shard_map/while/body/eval_jaxpr/ppermute | solution.py:12
  609.8 111.3 %all-reduce.7.cloned.1.call-start = ((), (), s32[]{:S(2)}) async-start(), calls=%async_computation.5 | async-start | bytes 262144 | tf_op jit(solution)/shard_map/while/body/eval_jaxpr/psum | solution.py:57
  609.9 112.9 %collective-permute-start = (bf16[128,448]{1,0:T(8,128)(2,1)S(1)}, bf16[128,448]{1,0:T(8,128)(2,1)S(1)}, u32[]{:S(2)}, u32[]{:S(2)}) collective-permute-start(bf16[128,448]{1,0:T(8,128)(2,1)S(1)} %copy.73), channel_id=1, source_target_pairs={{192,0},{0,64},{64,128},{128,192},{193,1},{1,65},{65,129},{129,193... | collective-permute-start | bytes 344072 | tf_op jit(solution)/shard_map/while/body/eval_jaxpr/ppermute | solution.py:12
  611.4 111.4 %collective-permute-start.1 = (bf16[128,448]{1,0:T(8,128)(2,1)S(1)}, bf16[128,448]{1,0:T(8,128)(2,1)S(1)}, u32[]{:S(2)}, u32[]{:S(2)}) collective-permute-start(bf16[128,448]{1,0:T(8,128)(2,1)S(1)} %copy.74), channel_id=1, source_target_pairs={{192,0},{0,64},{64,128},{128,192},{193,1},{1,65},{65,129},{129,193... | collective-permute-start | bytes 344072 | tf_op jit(solution)/shard_map/while/body/eval_jaxpr/ppermute | solution.py:12
  722.8 111.7 %all-reduce.7.cloned.1.call-start = ((), (), s32[]{:S(2)}) async-start(), calls=%async_computation.5 | async-start | bytes 262144 | tf_op jit(solution)/shard_map/while/body/eval_jaxpr/psum | solution.py:57
  722.8 113.2 %collective-permute-start = (bf16[128,448]{1,0:T(8,128)(2,1)S(1)}, bf16[128,448]{1,0:T(8,128)(2,1)S(1)}, u32[]{:S(2)}, u32[]{:S(2)}) collective-permute-start(bf16[128,448]{1,0:T(8,128)(2,1)S(1)} %copy.73), channel_id=1, source_target_pairs={{192,0},{0,64},{64,128},{128,192},{193,1},{1,65},{65,129},{129,193... | collective-permute-start | bytes 344072 | tf_op jit(solution)/shard_map/while/body/eval_jaxpr/ppermute | solution.py:12
  724.4 111.7 %collective-permute-start.1 = (bf16[128,448]{1,0:T(8,128)(2,1)S(1)}, bf16[128,448]{1,0:T(8,128)(2,1)S(1)}, u32[]{:S(2)}, u32[]{:S(2)}) collective-permute-start(bf16[128,448]{1,0:T(8,128)(2,1)S(1)} %copy.74), channel_id=1, source_target_pairs={{192,0},{0,64},{64,128},{128,192},{193,1},{1,65},{65,129},{129,193... | collective-permute-start | bytes 344072 | tf_op jit(solution)/shard_map/while/body/eval_jaxpr/ppermute | solution.py:12
  836.1 110.9 %all-reduce.5.cloned.1.call-start = ((), (), s32[]{:S(2)}) async-start(), calls=%async_computation.2 | async-start | bytes 262144 | tf_op jit(solution)/shard_map/psum | solution.py:57
  838.0 203.6 %reduce-scatter.5.cloned.1.call-start = ((), (), s32[]{:S(2)}) async-start(), calls=%async_computation.4 | async-start | bytes 573440 | tf_op jit(solution)/shard_map/reduce_scatter | solution.py:133
  841.0 108.0 %copy-start.9 = (bf16[4,128,448]{1,2,0:T(8,128)(2,1)S(1)}, bf16[4,128,448]{1,2,0:T(8,128)(2,1)}, u32[]{:S(2)}) copy-start(bf16[4,128,448]{1,2,0:T(8,128)(2,1)} %get-tuple-element.150) | copy-start | bytes 1376260
  841.0 202.3 %reduce-scatter.3.cloned.1.call-start = ((), (), s32[]{:S(2)}) async-start(), calls=%async_computation.3 | async-start | bytes 573440 | tf_op jit(solution)/shard_map/reduce_scatter | solution.py:130
  948.9 82.4 %copy-start.10 = (u32[256]{0:T(256)S(1)}, u32[256]{0:T(256)}, u32[]{:S(2)}) copy-start(u32[256]{0:T(256)} %constant.71) | copy-start | bytes 3076
  (10 other events, 22.5 us)
Sparse Core Ops, SparseCore 0:
  14.3 107.3 all-reduce.8
  135.3 107.4 all-reduce.8
  256.4 107.3 all-reduce.8
  377.3 107.4 all-reduce.8
  502.1 106.0 all-reduce.6
  614.1 106.9 all-reduce.6
  727.1 107.2 all-reduce.6
  841.4 26.5 reduce-scatter.4
  950.3 26.7 reduce-scatter.2
Sparse Core Ops, SparseCore 1:
  839.5 107.4 all-reduce.4
where the time goes:
time: 1060 us; the launch traced here: 1050 us
  waiting for transfers between devices  676 us (64%)
  other arithmetic  212 us (20%)
  blocking collectives  87.7 us (8%)
  starting transfers between devices  29.3 us (3%)
  between operations  19.1 us (2%)
  local copies, waits for them, and re-layouts  16.6 us (2%)
    psum x4, waiting for transfers between devices, backward_work(): lax.psum(partial_value.astype(jnp.bfloat16), 'width').astype(jnp.float32)  424 us
    psum x4, waiting for transfers between devices, encode(): return lax.psum(partial_value, 'width') + enc_bias[None, :]  229 us
    reduce_sum x64, other arithmetic, add_group(): return (total + jnp.sum(hits, axis=1), None)  180 us
    psum x1, blocking collectives, local(): lax.psum(loss_part, ('blk', 'width', 'rep'))  79.2 us
    ppermute x22, starting transfers between devices, shifted_2(): return lax.ppermute(block, axis, route)  28.9 us
    ppermute x22, waiting for transfers between devices, shifted_2(): return lax.ppermute(block, axis, route)  23.6 us
  transfers between devices with their start and end apart: 32, of which 16 were waited for; matrix products, arithmetic and copies ran while one was open for 22% of the time, Pallas kernels for 0%

commit v1 on v0

v1 whole, which is shorter than its diff:
```python
import math

import jax
import jax.numpy as jnp
from jax import lax
from jax.experimental import pallas as pl
from jax.experimental.pallas import tpu as pltpu
from jax.sharding import Mesh, PartitionSpec as P

F32 = jnp.float32
BF16 = jnp.bfloat16
GROUP = ("blk", "z", "core")


def from_ahead(block, axis, distance):
    size = lax.axis_size(axis)
    return lax.ppermute(block, axis, [((i + distance) % size, i) for i in range(size)])


def swap_core(block):
    return lax.ppermute(block, "core", [(0, 1), (1, 0)])


def shift_pieces(piece, sign):
    blk, z_size, cores = (lax.axis_size(name) for name in GROUP)
    half = z_size // 2
    route = []
    for b in range(blk):
        for z in range(z_size):
            for c in range(cores):
                to = (b + sign * (2 * c + z // half)) % blk
                route.append(((b * z_size + z) * cores + c, (to * z_size + z) * cores + c))
    return lax.ppermute(piece, GROUP, route)


def gather_z(piece):
    size = lax.axis_size("z")
    copies = jnp.broadcast_to(piece[None], (size,) + piece.shape)
    return lax.all_to_all(copies, "z", 0, 0, tiled=True)


def in_core_order(mine, other, core):
    first = jnp.where(core == 0, mine, other)
    second = jnp.where(core == 0, other, mine)
    return first, second


def pick_kernel(own_ref, picks_ref, out_ref, word_ref, bit_ref):
    own = own_ref[0]
    picks = picks_ref[...]
    place = (((own - (picks >> 9)) & 3) << 9) | (picks & 511)
    turned = jnp.transpose(place)
    word_ref[...] = turned >> 5
    bit_ref[...] = jnp.left_shift(jnp.int32(1), turned & 31)
    rows = picks_ref.shape[0]
    level = lax.broadcasted_iota(jnp.int32, (32, rows), 0)

    @pl.loop(0, out_ref.shape[1] // 128)
    def _(block):
        bits = []
        for sub in range(4):
            hit = word_ref[...] == block * 4 + sub
            total = jnp.sum(jnp.where(hit, bit_ref[...], 0), axis=0, keepdims=True)
            bits.append((jnp.broadcast_to(total, (32, rows)) >> level) & 1)
        square = jnp.concatenate(bits, 0).astype(F32)
        start = pl.multiple_of(block * 128, 128)
        out_ref[:, pl.ds(start, 128)] = jnp.transpose(square).astype(BF16)


def picked_latents(picks, own, lat_all):
    rows, count = picks.shape
    return pl.pallas_call(
        pick_kernel,
        out_shape=jax.ShapeDtypeStruct((rows, lat_all), BF16),
        in_specs=[
            pl.BlockSpec(memory_space=pltpu.SMEM),
            pl.BlockSpec(memory_space=pltpu.VMEM),
        ],
        out_specs=pl.BlockSpec(memory_space=pltpu.VMEM),
        scratch_shapes=[
            pltpu.VMEM((count, rows), jnp.int32),
            pltpu.VMEM((count, rows), jnp.int32),
        ],
        cost_estimate=pl.CostEstimate(flops=20_000_000, bytes_accessed=1_000_000, transcendentals=0),
    )(own.reshape(1).astype(jnp.int32), picks)


def two_halves(value):
    high = lax.reduce_precision(value, 8, 7)
    return high.astype(BF16), (value - high).astype(BF16)


def local(inputs, targets, enc_weight, enc_bias, dec_weight, dead_mask, aux_picks):
    blk, z_size, rep = lax.axis_size("blk"), lax.axis_size("z"), lax.axis_size("rep")
    core, blk_at, rep_at = lax.axis_index("core"), lax.axis_index("blk"), lax.axis_index("rep")
    rows, width = inputs.shape
    lat = dec_weight.shape[0]
    lat_all = blk * lat
    piece = rows * blk // (2 * z_size)
    total_tokens = rows * blk * rep
    norm_scale = 1.0 / math.sqrt(total_tokens)

    x_1, x_3 = from_ahead(inputs, "blk", 1), from_ahead(inputs, "blk", 3)
    x_2 = from_ahead(inputs, "blk", 2)
    dead = dead_mask.astype(BF16)
    dead_all = jnp.concatenate([dead] + [from_ahead(dead, "blk", -j) for j in (1, 2, 3)])
    picked = picked_latents(aux_picks, blk_at, lat_all)
    x_all = jnp.concatenate([inputs, x_1, x_2, x_3], 0)
    dec_own = lax.optimization_barrier((dec_weight, x_1, x_2, x_3))[0]
    dec_all = jnp.concatenate([dec_weight] + [from_ahead(dec_own, "blk", -j) for j in (1, 2, 3)], 0)

    halves = x_all.reshape(2, 2 * rows, width)
    sent = jnp.dot(
        lax.dynamic_index_in_dim(halves, 1 - core, 0, False), enc_weight, preferred_element_type=F32
    )
    got = swap_core(sent)
    kept = jnp.dot(
        lax.dynamic_index_in_dim(halves, core, 0, False), enc_weight, preferred_element_type=F32
    )
    parts = lax.all_to_all((kept + got).reshape(z_size, piece, lat), "z", 0, 0, tiled=True)
    preact = jnp.sum(parts, axis=0) + enc_bias[None, :]
    lat_piece = shift_pieces(jnp.maximum(preact, 0.0).astype(BF16), 1)

    lat_mine = gather_z(lat_piece).reshape(2, rows, lat)
    first, second = in_core_order(lat_mine, swap_core(lat_mine), core)
    latents = jnp.concatenate([first[0], first[1], second[0], second[1]], 1)
    gate = picked * dead_all[None, :]
    both = jnp.concatenate([latents, latents * gate], 0)

    decoded = jnp.dot(both, dec_all, preferred_element_type=F32)
    error = targets.astype(F32) - decoded[:rows]
    error_aux = error - decoded[rows:]
    loss_part = jnp.sum(error * error) + jnp.sum(error_aux * error_aux)
    loss_part = (loss_part + swap_core(loss_part.reshape(1, 1))[0, 0]).reshape(1, 1)
    grads = jnp.concatenate(
        [(-error * norm_scale).astype(BF16), (-error_aux * norm_scale).astype(BF16)], 0
    )

    def pulled_half(which):
        weight = lax.dynamic_slice_in_dim(dec_all, which * 2 * lat, 2 * lat, 0)
        opened = lax.dynamic_slice_in_dim(gate, which * 2 * lat, 2 * lat, 1).astype(F32)
        pulled = lax.dot_general(grads, weight, (((1,), (1,)), ((), ())), preferred_element_type=F32)
        return pulled[:rows] + pulled[rows:] * opened

    got_pulled = swap_core(pulled_half(1 - core).astype(BF16))
    pulled_sum = pulled_half(core) + got_pulled.astype(F32)
    pulled_sum = jnp.stack([pulled_sum[:, :lat], pulled_sum[:, lat:]], 0).astype(BF16)
    loss_lanes = jnp.concatenate([part.reshape(1, 1) for part in two_halves(loss_part)], 1)
    loss_lanes = jnp.pad(loss_lanes, ((0, 0), (0, 126)))
    packet = jnp.concatenate(
        [
            pulled_sum.reshape(z_size, piece, lat),
            jnp.broadcast_to(loss_lanes[None], (z_size, piece, 128)),
        ],
        2,
    )
    dec_term = lax.dot_general(
        grads, both, (((0,), (0,)), ((), ())), preferred_element_type=F32
    ).astype(BF16)
    share = width // rep
    dec_shares = dec_term.reshape(rep, share, lat_all)

    def rep_sum(shares):
        total = lax.dynamic_index_in_dim(shares, rep_at, 0, False).astype(F32)
        for step in (1, 3, 2):
            outgoing = lax.dynamic_index_in_dim(shares, (rep_at + step) % rep, 0, False)
            total = total + from_ahead(outgoing, "rep", -step).astype(F32)
        return total

    dec_sum = rep_sum(dec_shares).astype(BF16)

    arrived = lax.all_to_all(packet, "z", 0, 0, tiled=True).astype(F32)
    arrived = jnp.sum(arrived, axis=0)
    grad_piece = jnp.where(lat_piece > 0, arrived[:, :lat], 0.0).astype(BF16)
    loss_width = arrived[0, lat] + arrived[0, lat + 1]
    grad_piece = shift_pieces(grad_piece, -1)

    def with_rows(body, rows_of_more):
        more = [row.reshape(1, -1) for row in rows_of_more]
        more = [jnp.pad(row, ((0, 0), (0, lat - row.shape[1]))) for row in more]
        filler = jnp.zeros((16 - len(more), lat), BF16)
        return jnp.concatenate([body] + more + [filler], 0)

    def loss_row(value):
        return jnp.concatenate([part.reshape(1) for part in two_halves(value)])

    own_row = loss_row(loss_width)
    dec_final = dec_sum[:, :lat].astype(F32)
    loss_blk = loss_width
    for j in (1, 3, 2):
        outgoing = with_rows(dec_sum[:, j * lat : (j + 1) * lat], [own_row])
        incoming = from_ahead(outgoing, "blk", j).astype(F32)
        dec_final = dec_final + incoming[:share]
        loss_blk = loss_blk + incoming[share, 0] + incoming[share, 1]
    grad_dec = jnp.transpose(dec_final)

    grad_mine = gather_z(grad_piece).reshape(2 * rows, lat)
    first, second = in_core_order(grad_mine, swap_core(grad_mine), core)
    grad_pre = jnp.concatenate([first, second], 0)
    enc_term = lax.dot_general(
        x_all, grad_pre, (((0,), (0,)), ((), ())), preferred_element_type=F32
    ).astype(BF16)
    bias_term = jnp.sum(grad_pre.astype(F32), axis=0).astype(BF16)
    last_row = loss_row(loss_blk)
    shares = [
        with_rows(enc_term[i * share : (i + 1) * share], [bias_term, last_row]) for i in range(rep)
    ]
    final = rep_sum(jnp.stack(shares, 0))
    grad_enc = final[:share]
    grad_bias = lax.dynamic_slice_in_dim(final[share], rep_at * (lat // rep), lat // rep, 0)
    loss = (final[share + 1, 0] + final[share + 1, 1]) / (total_tokens * width * 2 * z_size)
    return (loss, grad_enc, grad_bias, grad_dec)


def solution(mesh):
    sizes = mesh.shape
    fine = Mesh(
        mesh.devices.reshape(sizes["blk"], sizes["width"] // 2, 2, sizes["rep"]),
        ("blk", "z", "core", "rep"),
    )
    wide = ("z", "core")
    in_specs = (
        P(("blk", "rep"), wide),
        P(("blk", "rep"), wide),
        P(wide, "blk"),
        P("blk"),
        P("blk", wide),
        P("blk"),
        P(("blk", "rep"), None),
    )
    out_specs = (P(), P(wide + ("rep",), "blk"), P(("blk", "rep")), P("blk", wide + ("rep",)))
    return jax.shard_map(local, mesh=fine, in_specs=in_specs, out_specs=out_specs, check_vma=False)
```

time: 1060 us -> 170 us (0.16)
  waiting for transfers between devices: 676 us -> 43 us
  other arithmetic: 212 us -> 7.17 us
  blocking collectives: 87.7 us -> 24.7 us
  starting transfers between devices: 29.3 us -> 54.5 us
    psum x8 -> x0, waiting for transfers between devices: 652 us -> none  [the longest x4 424 us: backward_work(): lax.psum(partial_value.astype(jnp.bfloat16), 'width').astype(jnp.float32)]
    reduce_sum x66 -> x4, other arithmetic: 183 us -> 0.24 us  [the longest x2 0.16 us: local(): bias_term = jnp.sum(grad_pre.astype(F32), axis=0).astype(BF16)]
    psum x1 -> x0, blocking collectives: 79.2 us -> none  [local(): lax.psum(loss_part, ('blk', 'width', 'rep'))]
    all_to_all x0 -> x3, starting transfers between devices: none -> 27.4 us  [the longest x2 20.2 us: gather_z(): return lax.all_to_all(copies, 'z', 0, 0, tiled=True)]
    all_to_all x0 -> x1, blocking collectives: none -> 24.7 us  [local(): lax.all_to_all((kept + got).reshape(z_size, piece, lat), 'z', 0, 0, tiled...]
    ppermute x22 -> x25, waiting for transfers between devices: 23.6 us -> 37.8 us  [the longest x18 35.9 us: from_ahead(): lax.ppermute(block, axis, [((i + distance) % size, i) for i in range(size)])]
    ppermute x22 -> x25, starting transfers between devices: 28.9 us -> 27.1 us  [the longest x18 24 us: from_ahead(): lax.ppermute(block, axis, [((i + distance) % size, i) for i in range(size)])]
  transfers between devices with their start and end apart: 32 -> 28, of which waited for: 16 -> 14; matrix products, arithmetic and copies ran while one was open for 22% -> 9% of each run, Pallas kernels for 0% -> 3%
where the time goes in v1:
time: 170 us; the launch traced here: 168 us
  starting transfers between devices  54.5 us (32%)
  waiting for transfers between devices  43 us (25%)
  blocking collectives  24.7 us (15%)
  between operations  16.2 us (10%)
  local copies, waits for them, and re-layouts  12.4 us (7%)
  other arithmetic  7.17 us (4%)
  Pallas kernels  5.7 us (3%)
  matrix products  4.4 us (3%)
    ppermute x18, waiting for transfers between devices, from_ahead(): lax.ppermute(block, axis, [((i + distance) % size, i) for i in range(size)])  35.9 us
    all_to_all x1, blocking collectives, local(): lax.all_to_all((kept + got).reshape(z_size, piece, lat), 'z', 0, 0, tiled...  24.7 us
    ppermute x18, starting transfers between devices, from_ahead(): lax.ppermute(block, axis, [((i + distance) % size, i) for i in range(size)])  24 us
    all_to_all x2, starting transfers between devices, gather_z(): return lax.all_to_all(copies, 'z', 0, 0, tiled=True)  20.2 us
    all_to_all x1, starting transfers between devices, local(): arrived = lax.all_to_all(packet, 'z', 0, 0, tiled=True).astype(F32)  7.23 us
    pallas_call x1, Pallas kernels, picked_latents(): pl.pallas_call(pick_kernel, out_shape=jax.ShapeDtypeStruct((rows, lat_all...  5.7 us
  transfers between devices with their start and end apart: 28, of which 14 were waited for; matrix products, arithmetic and copies ran while one was open for 9% of the time, Pallas kernels for 3%

profile of v1, /device:TPU:32, one launch (start us, length us, event | category | flops | bytes accessed | tf_op | source)
XLA Modules:
  0.0 168.1 jit_solution(3599360345190710632)
XLA Ops:
  0.6 2.8 %collective-permute-start = (bf16[128,448]{0,1:T(8,128)(2,1)}, bf16[128,448]{0,1:T(8,128)(2,1)S(1)}, u32[]{:S(2)}, u32[]{:S(2)}) collective-permute-start(bf16[128,448]{0,1:T(8,128)(2,1)} %param.7), channel_id=1, source_target_pairs={{64,0},{128,64},{192,128},{0,192},{65,1},{129,65},{193,129},{1,193... | collective-permute-start | bytes 344072 | tf_op jit(solution)/shard_map/ppermute | solution.py:17
  3.5 0.8 collective-permute-start.1
  4.3 0.9 collective-permute-start.2
  5.2 1.0 constant_dynamic-update-slice_fusion.3
  6.1 2.6 %collective-permute-done = bf16[128,448]{0,1:T(8,128)(2,1)S(1)} collective-permute-done((bf16[128,448]{0,1:T(8,128)(2,1)}, bf16[128,448]{0,1:T(8,128)(2,1)S(1)}, u32[]{:S(2)}, u32[]{:S(2)}) %collective-permute-start) | collective-permute-done | bytes 114720 | tf_op jit(solution)/shard_map/ppermute | solution.py:17
  8.7 2.3 %collective-permute-done.1 = bf16[128,448]{0,1:T(8,128)(2,1)S(1)} collective-permute-done((bf16[128,448]{0,1:T(8,128)(2,1)}, bf16[128,448]{0,1:T(8,128)(2,1)S(1)}, u32[]{:S(2)}, u32[]{:S(2)}) %collective-permute-start.1) | collective-permute-done | bytes 114720 | tf_op jit(solution)/shard_map/ppermute | solution.py:17
  11.1 1.2 collective-permute-done.2
  12.4 1.0 constant_dynamic-slice_fusion.2
  13.8 1.9 %collective-permute-done.3 = f32[256,512]{1,0:T(8,128)S(1)} collective-permute-done((f32[256,512]{1,0:T(8,128)S(1)}, f32[256,512]{1,0:T(8,128)S(1)}, u32[]{:S(2)}, u32[]{:S(2)}) %collective-permute-start.3) | collective-permute-done | bytes 524320 | tf_op jit(solution)/shard_map/ppermute | solution.py:21
  16.1 24.7 %all_to_all.20 = f32[8,32,512]{2,1,0:T(8,128)S(1)} all-to-all(f32[8,32,512]{2,1,0:T(8,128)S(1)} %bitcast.88), channel_id=1, replica_groups=mesh['blk'=4,'z'=8,'core'=2,'rep'=4] {'z'}, dimensions={0} | all-to-all | bytes 1048576 | tf_op jit(solution)/shard_map/all_to_all | solution.py:120
  41.5 0.7 broadcast_in_dim.9
  42.3 9.6 %all-to-all-start.1 = ((bf16[8,32,512]{2,1,0:T(8,128)(2,1)}), bf16[8,32,512]{2,1,0:T(8,128)(2,1)S(1)}, u32[]{:S(2)}, u32[]{:S(2)}) async-start(bf16[8,32,512]{2,1,0:T(8,128)(2,1)} %broadcast_in_dim.9), calls=%async_computation.1 | async-start | bytes 524288 | tf_op jit(solution)/shard_map/all_to_all | solution.py:39
  51.9 1.2 collective-permute-start.10
  53.1 2.9 %collective-permute-start.6 = (bf16[512]{0:T(512)(128)(2,1)S(1)}, bf16[512]{0:T(512)(128)(2,1)S(1)}, u32[]{:S(2)}, u32[]{:S(2)}) collective-permute-start(bf16[512]{0:T(512)(128)(2,1)S(1)} %convert_element_type.121), channel_id=1, source_target_pairs={{192,0},{0,64},{64,128},{128,192},{193,1},{1,65},{65,129},{129,193... | collective-permute-start | bytes 3080 | tf_op jit(solution)/shard_map/ppermute | solution.py:17
  56.7 2.1 %collective-permute-start.11 = (bf16[512,448]{0,1:T(8,128)(2,1)S(1)}, bf16[512,448]{0,1:T(8,128)(2,1)}, u32[]{:S(2)}, u32[]{:S(2)}) collective-permute-start(bf16[512,448]{0,1:T(8,128)(2,1)S(1)} %copy-done.10), channel_id=1, source_target_pairs={{64,0},{128,64},{192,128},{0,192},{65,1},{129,65},{193,129},{1,193... | collective-permute-start | bytes 1376264 | tf_op jit(solution)/shard_map/ppermute | solution.py:17
  58.8 5.7 %shard_map.102 = bf16[128,2048]{1,0:T(8,128)(2,1)} custom-call(s32[1]{0:T(128)} %bitcast.6.own_ref, s32[128,512]{1,0:T(8,128)} %picks_ref.1), custom_call_target="tpu_custom_call" | custom-call | flops 20000000 | bytes 1000000 | tf_op jit(solution)/shard_map/pallas_call | solution.py:72
  64.5 10.1 %collective-permute-done.6 = bf16[512]{0:T(512)(128)(2,1)S(1)} collective-permute-done((bf16[512]{0:T(512)(128)(2,1)S(1)}, bf16[512]{0:T(512)(128)(2,1)S(1)}, u32[]{:S(2)}, u32[]{:S(2)}) %collective-permute-start.6) | collective-permute-done | bytes 1056 | tf_op jit(solution)/shard_map/ppermute | solution.py:17
  74.7 3.5 %collective-permute-done.8 = bf16[512]{0:T(512)(128)(2,1)S(1)} collective-permute-done((bf16[512]{0:T(512)(128)(2,1)S(1)}, bf16[512]{0:T(512)(128)(2,1)S(1)}, u32[]{:S(2)}, u32[]{:S(2)}) %collective-permute-start.8) | collective-permute-done | bytes 1056 | tf_op jit(solution)/shard_map/ppermute | solution.py:17
  78.3 1.1 constant_dynamic-update-slice_fusion.6
  79.5 1.1 constant_dynamic-update-slice_fusion.4
  81.0 0.8 copy-done.8
  81.7 0.7 fusion.49
  84.6 1.6 collective-permute-start.13
  86.2 1.7 %convolution_convert_fusion = bf16[448,2048]{1,0:T(8,128)(2,1)S(1)} fusion(bf16[128,448]{0,1:T(8,128)(2,1)S(1)} %get-tuple-element.17, bf16[128,448]{0,1:T(8,128)(2,1)S(1)} %get-tuple-element.18, bf16[128,2048]{1,0:T(8,128)(2,1)} %copy-done.8, bf16[128,512]{1,0:T(8,128)(2,1)S(1)} %get-tuple-element.42, bf16[128,512]{1,0:T(8,128)(2,1)S(1)} %get-tuple-element.41, ...), kind=kOutput, calls=%fused_computation | convolution fusion | flops 476381184 | bytes 3112960 | tf_op jit(solution)/shard_map/dot_general | solution.py:157
  88.4 0.8 fusion.8
  89.3 1.1 dynamic-slice_bitcast_fusion.2
  90.4 1.5 collective-permute-start.16
  91.9 1.7 %collective-permute-start.17 = (bf16[112,2048]{1,0:T(8,128)(2,1)}, bf16[112,2048]{1,0:T(8,128)(2,1)}, u32[]{:S(2)}, u32[]{:S(2)}) collective-permute-start(bf16[112,2048]{1,0:T(8,128)(2,1)} %get-tuple-element.16), channel_id=1, source_target_pairs={{1,0},{2,1},{3,2},{0,3},{5,4},{6,5},{7,6},{4,7},{9,8},{10,9},{11,1... | collective-permute-start | bytes 1376264 | tf_op jit(solution)/shard_map/ppermute | solution.py:17
  93.6 2.0 %collective-permute-start.18 = (bf16[112,2048]{1,0:T(8,128)(2,1)}, bf16[112,2048]{1,0:T(8,128)(2,1)}, u32[]{:S(2)}, u32[]{:S(2)}) collective-permute-start(bf16[112,2048]{1,0:T(8,128)(2,1)} %get-tuple-element.15), channel_id=1, source_target_pairs={{2,0},{3,1},{0,2},{1,3},{6,4},{7,5},{4,6},{5,7},{10,8},{11,9},{8,1... | collective-permute-start | bytes 1376264 | tf_op jit(solution)/shard_map/ppermute | solution.py:17
  98.6 1.2 fusion.11
  99.8 0.8 pad_maximum_fusion.2
  100.6 7.2 %all-to-all-start.2 = ((bf16[8,32,640]{2,1,0:T(8,128)(2,1)}), bf16[8,32,640]{2,1,0:T(8,128)(2,1)S(1)}, u32[]{:S(2)}, u32[]{:S(2)}) async-start(bf16[8,32,640]{2,1,0:T(8,128)(2,1)} %pad_maximum_fusion.2), calls=%async_computation.2 | async-start | bytes 655360 | tf_op jit(solution)/shard_map/all_to_all | solution.py:172
  107.8 6.1 %collective-permute-done.17 = bf16[112,2048]{1,0:T(8,128)(2,1)} collective-permute-done((bf16[112,2048]{1,0:T(8,128)(2,1)}, bf16[112,2048]{1,0:T(8,128)(2,1)}, u32[]{:S(2)}, u32[]{:S(2)}) %collective-permute-start.17) | collective-permute-done | bytes 458784 | tf_op jit(solution)/shard_map/ppermute | solution.py:17
  114.0 1.9 %collective-permute-done.18 = bf16[112,2048]{1,0:T(8,128)(2,1)} collective-permute-done((bf16[112,2048]{1,0:T(8,128)(2,1)}, bf16[112,2048]{1,0:T(8,128)(2,1)}, u32[]{:S(2)}, u32[]{:S(2)}) %collective-permute-start.18) | collective-permute-done | bytes 458784 | tf_op jit(solution)/shard_map/ppermute | solution.py:17
  115.8 1.7 %fusion.2 = bf16[112,2048]{1,0:T(8,128)(2,1)S(1)} fusion(bf16[112,2048]{1,0:T(8,128)(2,1)} %collective-permute-done.18, bf16[112,2048]{1,0:T(8,128)(2,1)} %collective-permute-done.17, bf16[112,2048]{1,0:T(8,128)(2,1)} %collective-permute-done.16, bf16[4,112,2048]{2,1,0:T(8,128)(2,1)} %bitcast.90, s32[]{:T(128)S(6)} %select_n.96), kind=kLoop, calls=%fused_computation.7 | loop fusion | flops 1835008 | bytes 2293764 | tf_op jit(solution)/shard_map/convert_element_type | solution.py:170
  117.6 1.9 %all-to-all-done.2 = bf16[8,32,640]{2,1,0:T(8,128)(2,1)S(1)} async-done(((bf16[8,32,640]{2,1,0:T(8,128)(2,1)}), bf16[8,32,640]{2,1,0:T(8,128)(2,1)S(1)}, u32[]{:S(2)}, u32[]{:S(2)}) %all-to-all-start.2) | async-done | bytes 327712 | tf_op jit(solution)/shard_map/all_to_all | solution.py:172
  124.0 0.7 broadcast_in_dim.13
  124.7 10.6 %all-to-all-start.3 = ((bf16[8,32,512]{2,1,0:T(8,128)(2,1)}), bf16[8,32,512]{2,1,0:T(8,128)(2,1)S(1)}, u32[]{:S(2)}, u32[]{:S(2)}) async-start(bf16[8,32,512]{2,1,0:T(8,128)(2,1)} %broadcast_in_dim.13), calls=%async_computation.3 | async-start | bytes 524288 | tf_op jit(solution)/shard_map/all_to_all | solution.py:39
  135.4 2.5 %collective-permute-start.19 = (bf16[128,512]{1,0:T(8,128)(2,1)S(1)}, bf16[128,512]{1,0:T(8,128)(2,1)S(1)}, u32[]{:S(2)}, u32[]{:S(2)}) collective-permute-start(bf16[128,512]{1,0:T(8,128)(2,1)S(1)} %get-tuple-element.56), channel_id=1, source_target_pairs={{64,0},{128,64},{192,128},{0,192},{65,1},{129,65},{193,129},{1,193... | collective-permute-start | bytes 393224 | tf_op jit(solution)/shard_map/ppermute | solution.py:17
  138.0 1.6 collective-permute-start.21
  139.6 2.1 %collective-permute-done.19 = bf16[128,512]{1,0:T(8,128)(2,1)S(1)} collective-permute-done((bf16[128,512]{1,0:T(8,128)(2,1)S(1)}, bf16[128,512]{1,0:T(8,128)(2,1)S(1)}, u32[]{:S(2)}, u32[]{:S(2)}) %collective-permute-start.19) | collective-permute-done | bytes 131104 | tf_op jit(solution)/shard_map/ppermute | solution.py:17
  142.2 3.4 %all-to-all-done.3 = bf16[8,32,512]{2,1,0:T(8,128)(2,1)S(1)} async-done(((bf16[8,32,512]{2,1,0:T(8,128)(2,1)}), bf16[8,32,512]{2,1,0:T(8,128)(2,1)S(1)}, u32[]{:S(2)}, u32[]{:S(2)}) %all-to-all-start.3) | async-done | bytes 262176 | tf_op jit(solution)/shard_map/all_to_all | solution.py:39
  153.6 1.1 collective-permute-start.22
  154.7 2.2 %collective-permute-start.23 = (bf16[128,512]{1,0:T(8,128)(2,1)S(1)}, bf16[128,512]{1,0:T(8,128)(2,1)S(1)}, u32[]{:S(2)}, u32[]{:S(2)}) collective-permute-start(bf16[128,512]{1,0:T(8,128)(2,1)S(1)} %get-tuple-element.21), channel_id=1, source_target_pairs={{1,0},{2,1},{3,2},{0,3},{5,4},{6,5},{7,6},{4,7},{9,8},{10,9},{11,1... | collective-permute-start | bytes 393224 | tf_op jit(solution)/shard_map/ppermute | solution.py:17
  156.9 0.8 fusion.21
  157.7 3.1 %collective-permute-done.22 = bf16[128,512]{1,0:T(8,128)(2,1)S(1)} collective-permute-done((bf16[128,512]{1,0:T(8,128)(2,1)S(1)}, bf16[128,512]{1,0:T(8,128)(2,1)S(1)}, u32[]{:S(2)}, u32[]{:S(2)}) %collective-permute-start.22) | collective-permute-done | bytes 131104 | tf_op jit(solution)/shard_map/ppermute | solution.py:17
  160.8 2.1 %collective-permute-done.23 = bf16[128,512]{1,0:T(8,128)(2,1)S(1)} collective-permute-done((bf16[128,512]{1,0:T(8,128)(2,1)S(1)}, bf16[128,512]{1,0:T(8,128)(2,1)S(1)}, u32[]{:S(2)}, u32[]{:S(2)}) %collective-permute-start.23) | collective-permute-done | bytes 131104 | tf_op jit(solution)/shard_map/ppermute | solution.py:17
  162.9 0.9 collective-permute-done.24
  (104 shorter events, 11.2 us)
Async XLA Ops:
  0.6 12.8 %copy-start = (bf16[448,512]{1,0:T(8,128)(2,1)S(1)}, bf16[448,512]{1,0:T(8,128)(2,1)}, u32[]{:S(2)}) copy-start(bf16[448,512]{1,0:T(8,128)(2,1)} %param.9) | copy-start | bytes 1376260
  0.6 8.0 %collective-permute-start = (bf16[128,448]{0,1:T(8,128)(2,1)}, bf16[128,448]{0,1:T(8,128)(2,1)S(1)}, u32[]{:S(2)}, u32[]{:S(2)}) collective-permute-start(bf16[128,448]{0,1:T(8,128)(2,1)} %param.7), channel_id=1, source_target_pairs={{64,0},{128,64},{192,128},{0,192},{65,1},{129,65},{193,129},{1,193... | collective-permute-start | bytes 344072 | tf_op jit(solution)/shard_map/ppermute | solution.py:17
  3.5 7.6 %collective-permute-start.1 = (bf16[128,448]{0,1:T(8,128)(2,1)}, bf16[128,448]{0,1:T(8,128)(2,1)S(1)}, u32[]{:S(2)}, u32[]{:S(2)}) collective-permute-start(bf16[128,448]{0,1:T(8,128)(2,1)} %param.7), channel_id=1, source_target_pairs={{128,0},{192,64},{0,128},{64,192},{129,1},{193,65},{1,129},{65,193... | collective-permute-start | bytes 344072 | tf_op jit(solution)/shard_map/ppermute | solution.py:17
  4.3 8.0 %collective-permute-start.2 = (bf16[128,448]{0,1:T(8,128)(2,1)}, bf16[128,448]{0,1:T(8,128)(2,1)S(1)}, u32[]{:S(2)}, u32[]{:S(2)}) collective-permute-start(bf16[128,448]{0,1:T(8,128)(2,1)} %param.7), channel_id=1, source_target_pairs={{192,0},{0,64},{64,128},{128,192},{193,1},{1,65},{65,129},{129,193... | collective-permute-start | bytes 344072 | tf_op jit(solution)/shard_map/ppermute | solution.py:17
  12.3 1.4 copy-start.6
  13.7 27.1 %copy-start.12 = (f32[512]{0:T(512)S(1)}, f32[512]{0:T(512)}, u32[]{:S(2)}) copy-start(f32[512]{0:T(512)} %param.10) | copy-start | bytes 6148
  13.7 2.0 %collective-permute-start.3 = (f32[256,512]{1,0:T(8,128)S(1)}, f32[256,512]{1,0:T(8,128)S(1)}, u32[]{:S(2)}, u32[]{:S(2)}) collective-permute-start(f32[256,512]{1,0:T(8,128)S(1)} %fusion.22), channel_id=1, source_target_pairs={{0,4},{4,0},{1,5},{5,1},{2,6},{6,2},{3,7},{7,3},{8,12},{12,8},{9,1... | collective-permute-start | bytes 1572872 | tf_op jit(solution)/shard_map/ppermute | solution.py:21
  15.7 36.2 %copy-start.10 = (bf16[512,448]{0,1:T(8,128)(2,1)S(1)}, bf16[512,448]{0,1:T(8,128)(2,1)}, u32[]{:S(2)}) copy-start(bf16[512,448]{0,1:T(8,128)(2,1)} %param.11) | copy-start | bytes 1376260
  15.7 37.3 %copy-start.13 = (s32[512]{0:T(512)S(1)}, s32[512]{0:T(512)}, u32[]{:S(2)}) copy-start(s32[512]{0:T(512)} %param.12) | copy-start | bytes 6148
  40.9 0.7 collective-permute-start.4
  42.3 35.9 %all-to-all-start.1 = ((bf16[8,32,512]{2,1,0:T(8,128)(2,1)}), bf16[8,32,512]{2,1,0:T(8,128)(2,1)S(1)}, u32[]{:S(2)}, u32[]{:S(2)}) async-start(bf16[8,32,512]{2,1,0:T(8,128)(2,1)} %broadcast_in_dim.9), calls=%async_computation.1 | async-start | bytes 524288 | tf_op jit(solution)/shard_map/all_to_all | solution.py:39
  51.9 26.4 %collective-permute-start.9 = (bf16[512,448]{0,1:T(8,128)(2,1)S(1)}, bf16[512,448]{0,1:T(8,128)(2,1)}, u32[]{:S(2)}, u32[]{:S(2)}) collective-permute-start(bf16[512,448]{0,1:T(8,128)(2,1)S(1)} %copy-done.10), channel_id=1, source_target_pairs={{192,0},{0,64},{64,128},{128,192},{193,1},{1,65},{65,129},{129,193... | collective-permute-start | bytes 1376264 | tf_op jit(solution)/shard_map/ppermute | solution.py:17
  51.9 27.5 %collective-permute-start.10 = (bf16[512,448]{0,1:T(8,128)(2,1)S(1)}, bf16[512,448]{0,1:T(8,128)(2,1)S(1)}, u32[]{:S(2)}, u32[]{:S(2)}) collective-permute-start(bf16[512,448]{0,1:T(8,128)(2,1)S(1)} %copy-done.10), channel_id=1, source_target_pairs={{128,0},{192,64},{0,128},{64,192},{129,1},{193,65},{1,129},{65,193... | collective-permute-start | bytes 1376264 | tf_op jit(solution)/shard_map/ppermute | solution.py:17
  53.1 21.5 %collective-permute-start.6 = (bf16[512]{0:T(512)(128)(2,1)S(1)}, bf16[512]{0:T(512)(128)(2,1)S(1)}, u32[]{:S(2)}, u32[]{:S(2)}) collective-permute-start(bf16[512]{0:T(512)(128)(2,1)S(1)} %convert_element_type.121), channel_id=1, source_target_pairs={{192,0},{0,64},{64,128},{128,192},{193,1},{1,65},{65,129},{129,193... | collective-permute-start | bytes 3080 | tf_op jit(solution)/shard_map/ppermute | solution.py:17
  56.0 18.7 %collective-permute-start.7 = (bf16[512]{0:T(512)(128)(2,1)S(1)}, bf16[512]{0:T(512)(128)(2,1)S(1)}, u32[]{:S(2)}, u32[]{:S(2)}) collective-permute-start(bf16[512]{0:T(512)(128)(2,1)S(1)} %convert_element_type.121), channel_id=1, source_target_pairs={{128,0},{192,64},{0,128},{64,192},{129,1},{193,65},{1,129},{65,193... | collective-permute-start | bytes 3080 | tf_op jit(solution)/shard_map/ppermute | solution.py:17
  56.7 22.8 %collective-permute-start.11 = (bf16[512,448]{0,1:T(8,128)(2,1)S(1)}, bf16[512,448]{0,1:T(8,128)(2,1)}, u32[]{:S(2)}, u32[]{:S(2)}) collective-permute-start(bf16[512,448]{0,1:T(8,128)(2,1)S(1)} %copy-done.10), channel_id=1, source_target_pairs={{64,0},{128,64},{192,128},{0,192},{65,1},{129,65},{193,129},{1,193... | collective-permute-start | bytes 1376264 | tf_op jit(solution)/shard_map/ppermute | solution.py:17
  74.6 3.6 %collective-permute-start.8 = (bf16[512]{0:T(512)(128)(2,1)S(1)}, bf16[512]{0:T(512)(128)(2,1)S(1)}, u32[]{:S(2)}, u32[]{:S(2)}) collective-permute-start(bf16[512]{0:T(512)(128)(2,1)S(1)} %convert_element_type.121), channel_id=1, source_target_pairs={{64,0},{128,64},{192,128},{0,192},{65,1},{129,65},{193,129},{1,193... | collective-permute-start | bytes 3080 | tf_op jit(solution)/shard_map/ppermute | solution.py:17
  78.2 2.4 %collective-permute-start.5 = (bf16[2,128,512]{2,1,0:T(8,128)(2,1)S(1)}, bf16[2,128,512]{2,1,0:T(8,128)(2,1)S(1)}, u32[]{:S(2)}, u32[]{:S(2)}) collective-permute-start(bf16[2,128,512]{2,1,0:T(8,128)(2,1)S(1)} %bitcast.92), channel_id=1, source_target_pairs={{0,4},{4,0},{1,5},{5,1},{2,6},{6,2},{3,7},{7,3},{8,12},{12,8},{9,1... | collective-permute-start | bytes 786440 | tf_op jit(solution)/shard_map/ppermute | solution.py:21
  79.4 1.4 copy-start.1
  80.7 1.7 %copy-start.9 = (bf16[128,512]{1,0:T(8,128)(2,1)}, bf16[128,512]{1,0:T(8,128)(2,1)S(1)}, u32[]{:S(2)}) copy-start(bf16[128,512]{1,0:T(8,128)(2,1)S(1)} %get-tuple-element.59) | copy-start | bytes 393220
  80.9 0.8 copy-start.8
  81.0 7.4 %copy-start.2 = (bf16[128,2048]{1,0:T(8,128)(2,1)}, bf16[128,2048]{1,0:T(8,128)(2,1)S(1)}, u32[]{:S(2)}) copy-start(bf16[128,2048]{1,0:T(8,128)(2,1)S(1)} %get-tuple-element.13) | copy-start | bytes 1572868
  81.7 0.9 copy-start.11
  83.3 4.6 %copy-start.4 = (bf16[128,448]{0,1:T(8,128)(2,1)}, bf16[128,448]{0,1:T(8,128)(2,1)S(1)}, u32[]{:S(2)}) copy-start(bf16[128,448]{0,1:T(8,128)(2,1)S(1)} %get-tuple-element.18) | copy-start | bytes 344068
  84.6 11.4 %collective-permute-start.13 = (f32[1,1]{1,0:T(1,128)}, f32[1,1]{1,0:T(1,128)}, u32[]{:S(2)}, u32[]{:S(2)}) collective-permute-start(f32[1,1]{1,0:T(1,128)} %bitcast.10), channel_id=1, source_target_pairs={{0,4},{4,0},{1,5},{5,1},{2,6},{6,2},{3,7},{7,3},{8,12},{12,8},{9,1... | collective-permute-start | bytes 20 | tf_op jit(solution)/shard_map/ppermute | solution.py:21
  87.9 1.3 copy-start.3
  88.4 7.2 %copy-start.5 = (bf16[128,448]{0,1:T(8,128)(2,1)S(1)}, bf16[128,448]{0,1:T(8,128)(2,1)}, u32[]{:S(2)}) copy-start(bf16[128,448]{0,1:T(8,128)(2,1)} %copy-done.4) | copy-start | bytes 344068
  89.2 9.3 %collective-permute-start.12 = (bf16[128,1024]{1,0:T(8,128)(2,1)}, bf16[128,1024]{1,0:T(8,128)(2,1)}, u32[]{:S(2)}, u32[]{:S(2)}) collective-permute-start(bf16[128,1024]{1,0:T(8,128)(2,1)} %fusion.8), channel_id=1, source_target_pairs={{0,4},{4,0},{1,5},{5,1},{2,6},{6,2},{3,7},{7,3},{8,12},{12,8},{9,1... | collective-permute-start | bytes 786440 | tf_op jit(solution)/shard_map/ppermute | solution.py:21
  90.4 17.4 %collective-permute-start.16 = (bf16[112,2048]{1,0:T(8,128)(2,1)}, bf16[112,2048]{1,0:T(8,128)(2,1)}, u32[]{:S(2)}, u32[]{:S(2)}) collective-permute-start(bf16[112,2048]{1,0:T(8,128)(2,1)} %get-tuple-element.14), channel_id=1, source_target_pairs={{3,0},{0,1},{1,2},{2,3},{7,4},{4,5},{5,6},{6,7},{11,8},{8,9},{9,10... | collective-permute-start | bytes 1376264 | tf_op jit(solution)/shard_map/ppermute | solution.py:17
  91.9 22.1 %collective-permute-start.17 = (bf16[112,2048]{1,0:T(8,128)(2,1)}, bf16[112,2048]{1,0:T(8,128)(2,1)}, u32[]{:S(2)}, u32[]{:S(2)}) collective-permute-start(bf16[112,2048]{1,0:T(8,128)(2,1)} %get-tuple-element.16), channel_id=1, source_target_pairs={{1,0},{2,1},{3,2},{0,3},{5,4},{6,5},{7,6},{4,7},{9,8},{10,9},{11,1... | collective-permute-start | bytes 1376264 | tf_op jit(solution)/shard_map/ppermute | solution.py:17
  93.6 22.2 %collective-permute-start.18 = (bf16[112,2048]{1,0:T(8,128)(2,1)}, bf16[112,2048]{1,0:T(8,128)(2,1)}, u32[]{:S(2)}, u32[]{:S(2)}) collective-permute-start(bf16[112,2048]{1,0:T(8,128)(2,1)} %get-tuple-element.15), channel_id=1, source_target_pairs={{2,0},{3,1},{0,2},{1,3},{6,4},{7,5},{4,6},{5,7},{10,8},{11,9},{8,1... | collective-permute-start | bytes 1376264 | tf_op jit(solution)/shard_map/ppermute | solution.py:17
  100.6 18.9 %all-to-all-start.2 = ((bf16[8,32,640]{2,1,0:T(8,128)(2,1)}), bf16[8,32,640]{2,1,0:T(8,128)(2,1)S(1)}, u32[]{:S(2)}, u32[]{:S(2)}) async-start(bf16[8,32,640]{2,1,0:T(8,128)(2,1)} %pad_maximum_fusion.2), calls=%async_computation.2 | async-start | bytes 655360 | tf_op jit(solution)/shard_map/all_to_all | solution.py:172
  123.2 0.8 collective-permute-start.14
  124.7 28.2 %copy-start.7 = (bf16[512,448]{0,1:T(8,128)(2,1)S(1)}, bf16[512,448]{0,1:T(8,128)(2,1)}, u32[]{:S(2)}) copy-start(bf16[512,448]{0,1:T(8,128)(2,1)} %copy-done.6) | copy-start | bytes 1376260
  124.7 20.9 %all-to-all-start.3 = ((bf16[8,32,512]{2,1,0:T(8,128)(2,1)}), bf16[8,32,512]{2,1,0:T(8,128)(2,1)S(1)}, u32[]{:S(2)}, u32[]{:S(2)}) async-start(bf16[8,32,512]{2,1,0:T(8,128)(2,1)} %broadcast_in_dim.13), calls=%async_computation.3 | async-start | bytes 524288 | tf_op jit(solution)/shard_map/all_to_all | solution.py:39
  135.4 6.2 %collective-permute-start.19 = (bf16[128,512]{1,0:T(8,128)(2,1)S(1)}, bf16[128,512]{1,0:T(8,128)(2,1)S(1)}, u32[]{:S(2)}, u32[]{:S(2)}) collective-permute-start(bf16[128,512]{1,0:T(8,128)(2,1)S(1)} %get-tuple-element.56), channel_id=1, source_target_pairs={{64,0},{128,64},{192,128},{0,192},{65,1},{129,65},{193,129},{1,193... | collective-permute-start | bytes 393224 | tf_op jit(solution)/shard_map/ppermute | solution.py:17
  137.9 7.7 %collective-permute-start.20 = (bf16[128,512]{1,0:T(8,128)(2,1)S(1)}, bf16[128,512]{1,0:T(8,128)(2,1)S(1)}, u32[]{:S(2)}, u32[]{:S(2)}) collective-permute-start(bf16[128,512]{1,0:T(8,128)(2,1)S(1)} %get-tuple-element.57), channel_id=1, source_target_pairs={{192,0},{0,64},{64,128},{128,192},{193,1},{1,65},{65,129},{129,193... | collective-permute-start | bytes 393224 | tf_op jit(solution)/shard_map/ppermute | solution.py:17
  138.0 10.8 %collective-permute-start.21 = (bf16[128,512]{1,0:T(8,128)(2,1)S(1)}, bf16[128,512]{1,0:T(8,128)(2,1)S(1)}, u32[]{:S(2)}, u32[]{:S(2)}) collective-permute-start(bf16[128,512]{1,0:T(8,128)(2,1)S(1)} %get-tuple-element.55), channel_id=1, source_target_pairs={{128,0},{192,64},{0,128},{64,192},{129,1},{193,65},{1,129},{65,193... | collective-permute-start | bytes 393224 | tf_op jit(solution)/shard_map/ppermute | solution.py:17
  145.6 7.1 %collective-permute-start.15 = (bf16[256,512]{1,0:T(8,128)(2,1)S(1)}, bf16[256,512]{1,0:T(8,128)(2,1)S(1)}, u32[]{:S(2)}, u32[]{:S(2)}) collective-permute-start(bf16[256,512]{1,0:T(8,128)(2,1)S(1)} %bitcast.94), channel_id=1, source_target_pairs={{0,4},{4,0},{1,5},{5,1},{2,6},{6,2},{3,7},{7,3},{8,12},{12,8},{9,1... | collective-permute-start | bytes 786440 | tf_op jit(solution)/shard_map/ppermute | solution.py:21
  153.6 7.2 %collective-permute-start.22 = (bf16[128,512]{1,0:T(8,128)(2,1)S(1)}, bf16[128,512]{1,0:T(8,128)(2,1)S(1)}, u32[]{:S(2)}, u32[]{:S(2)}) collective-permute-start(bf16[128,512]{1,0:T(8,128)(2,1)S(1)} %get-tuple-element.19), channel_id=1, source_target_pairs={{3,0},{0,1},{1,2},{2,3},{7,4},{4,5},{5,6},{6,7},{11,8},{8,9},{9,10... | collective-permute-start | bytes 393224 | tf_op jit(solution)/shard_map/ppermute | solution.py:17
  154.7 8.2 %collective-permute-start.23 = (bf16[128,512]{1,0:T(8,128)(2,1)S(1)}, bf16[128,512]{1,0:T(8,128)(2,1)S(1)}, u32[]{:S(2)}, u32[]{:S(2)}) collective-permute-start(bf16[128,512]{1,0:T(8,128)(2,1)S(1)} %get-tuple-element.21), channel_id=1, source_target_pairs={{1,0},{2,1},{3,2},{0,3},{5,4},{6,5},{7,6},{4,7},{9,8},{10,9},{11,1... | collective-permute-start | bytes 393224 | tf_op jit(solution)/shard_map/ppermute | solution.py:17
  156.9 6.9 %collective-permute-start.24 = (bf16[128,512]{1,0:T(8,128)(2,1)S(1)}, bf16[128,512]{1,0:T(8,128)(2,1)S(1)}, u32[]{:S(2)}, u32[]{:S(2)}) collective-permute-start(bf16[128,512]{1,0:T(8,128)(2,1)S(1)} %get-tuple-element.20), channel_id=1, source_target_pairs={{2,0},{3,1},{0,2},{1,3},{6,4},{7,5},{4,6},{5,7},{10,8},{11,9},{8,1... | collective-permute-start | bytes 393224 | tf_op jit(solution)/shard_map/ppermute | solution.py:17

commit v2 on v1

v2 whole, which is shorter than its diff:
```python
import math

import jax
import jax.numpy as jnp
from jax import lax
from jax.experimental import pallas as pl
from jax.experimental.pallas import tpu as pltpu
from jax.sharding import Mesh, PartitionSpec as P

F32 = jnp.float32
BF16 = jnp.bfloat16
GROUP = ("blk", "z", "core")


def from_ahead(block, axis, distance):
    size = lax.axis_size(axis)
    return lax.ppermute(block, axis, [((i + distance) % size, i) for i in range(size)])


def blk_move(block, slot, sign):
    blk, cores = lax.axis_size("blk"), lax.axis_size("core")
    route = []
    for b in range(blk):
        for c in range(cores):
            to = (b + sign * (slot + 2 * c)) % blk
            route.append((b * cores + c, to * cores + c))
    return lax.ppermute(block, ("blk", "core"), route)


def swap_core(block):
    return lax.ppermute(block, "core", [(0, 1), (1, 0)])


def shift_pieces(piece, sign):
    blk, z_size, cores = (lax.axis_size(name) for name in GROUP)
    half = z_size // 2
    route = []
    for b in range(blk):
        for z in range(z_size):
            for c in range(cores):
                to = (b + sign * (2 * c + z // half)) % blk
                route.append(((b * z_size + z) * cores + c, (to * z_size + z) * cores + c))
    return lax.ppermute(piece, GROUP, route)


def z_copies(piece):
    return jnp.broadcast_to(piece[None], (lax.axis_size("z"),) + piece.shape)


def exchange_z(copies):
    return lax.all_to_all(copies, "z", 0, 0, tiled=True)


def after(values, event):
    return lax.optimization_barrier((values, event))[0]


def pick_kernel(own_ref, picks_ref, out_ref, word_ref, bit_ref):
    own = own_ref[0]
    picks = picks_ref[...]
    place = (((own - (picks >> 9)) & 3) << 9) | (picks & 511)
    turned = jnp.transpose(place)
    word_ref[...] = turned >> 5
    bit_ref[...] = jnp.left_shift(jnp.int32(1), turned & 31)
    rows = picks_ref.shape[0]
    level = lax.broadcasted_iota(jnp.int32, (32, rows), 0)

    @pl.loop(0, out_ref.shape[1] // 128)
    def _(block):
        bits = []
        for sub in range(4):
            hit = word_ref[...] == block * 4 + sub
            total = jnp.sum(jnp.where(hit, bit_ref[...], 0), axis=0, keepdims=True)
            bits.append((jnp.broadcast_to(total, (32, rows)) >> level) & 1)
        square = jnp.concatenate(bits, 0).astype(F32)
        start = pl.multiple_of(block * 128, 128)
        out_ref[:, pl.ds(start, 128)] = jnp.transpose(square).astype(BF16)


def picked_latents(picks, own, lat_all):
    rows, count = picks.shape
    return pl.pallas_call(
        pick_kernel,
        out_shape=jax.ShapeDtypeStruct((rows, lat_all), BF16),
        in_specs=[
            pl.BlockSpec(memory_space=pltpu.SMEM),
            pl.BlockSpec(memory_space=pltpu.VMEM),
        ],
        out_specs=pl.BlockSpec(memory_space=pltpu.VMEM),
        scratch_shapes=[
            pltpu.VMEM((count, rows), jnp.int32),
            pltpu.VMEM((count, rows), jnp.int32),
        ],
        cost_estimate=pl.CostEstimate(flops=20_000_000_000, bytes_accessed=1_000_000, transcendentals=0),
    )(own.reshape(1).astype(jnp.int32), picks)


def two_halves(value):
    high = lax.reduce_precision(value, 8, 7)
    return [high.astype(BF16), (value - high).astype(BF16)]


def with_rows(body, rows):
    width = body.shape[1]
    rows = [jnp.pad(row, ((0, 0), (0, width - row.shape[1]))) for row in rows]
    filler = jnp.zeros((16 - len(rows), width), BF16)
    return jnp.concatenate([body] + rows + [filler], 0)


def local(inputs, targets, enc_weight, enc_bias, dec_weight, dead_mask, aux_picks):
    blk, z_size, rep = lax.axis_size("blk"), lax.axis_size("z"), lax.axis_size("rep")
    core, blk_at, rep_at = lax.axis_index("core"), lax.axis_index("blk"), lax.axis_index("rep")
    rows, width = inputs.shape
    lat = dec_weight.shape[0]
    lat_all = blk * lat
    piece = rows * blk // (2 * z_size)
    total_tokens = rows * blk * rep
    norm_scale = 1.0 / math.sqrt(total_tokens)

    def in_slots(own, slot_1, across, slot_3):
        size = own.shape[0]
        whole = jnp.zeros((4 * size,) + own.shape[1:], own.dtype)
        for block, slot in ((own, 2 * core), (slot_1, 1), (slot_3, 3), (across, 2 - 2 * core)):
            whole = lax.dynamic_update_slice_in_dim(whole, block, slot * size, 0)
        return whole

    x_1, x_3 = blk_move(inputs, 1, -1), blk_move(inputs, 3, -1)
    x_2 = from_ahead(inputs, "blk", 2)
    x_all = in_slots(inputs, x_1, x_2, x_3)
    dead = jnp.broadcast_to(dead_mask.astype(BF16)[:, None], (lat, 16))
    dec_own = jnp.concatenate([dec_weight, dead], 1)
    dec_sent = after(dec_own, x_1)
    dec_1, dec_3 = blk_move(dec_sent, 1, 1), blk_move(dec_sent, 3, 1)
    half = lat // 2
    picked = picked_latents(aux_picks, blk_at + 2 * core, lat_all)

    got = swap_core(jnp.dot(x_all[2 * rows :], enc_weight, preferred_element_type=F32))
    kept = jnp.dot(x_all[: 2 * rows], enc_weight, preferred_element_type=F32)
    parts = lax.all_to_all((kept + got).reshape(z_size, piece, lat), "z", 0, 0, tiled=True)
    preact = jnp.sum(parts, axis=0) + enc_bias[None, :]
    lat_piece = jnp.maximum(preact, 0.0).astype(BF16)
    lat_piece, picked, dec_1, dec_3 = lax.optimization_barrier((lat_piece, picked, dec_1, dec_3))
    dec_2 = [blk_move(dec_1[:half], 1, 1), blk_move(dec_3[half:], 3, 1)]
    lat_piece = shift_pieces(lat_piece, 1)
    dec_all = in_slots(dec_own, dec_1, jnp.concatenate(dec_2, 0), dec_3)
    gate = picked * dec_all[:, width][None, :]

    lat_mine = exchange_z(z_copies(lat_piece)).reshape(2, rows, lat)
    lat_other = swap_core(lat_mine)
    latents = jnp.concatenate([lat_mine[0], lat_mine[1], lat_other[0], lat_other[1]], 1)
    both = jnp.concatenate([latents, latents * gate], 0)

    decoded = jnp.dot(both, dec_all, preferred_element_type=F32)
    error = targets.astype(F32) - decoded[:rows, :width]
    error_aux = error - decoded[rows:, :width]
    squares = error * error + error_aux * error_aux
    squares = jnp.pad(squares, ((0, 0), (0, -width % 128)))
    squares = sum(squares[:, i : i + 128] for i in range(0, squares.shape[1], 128))
    loss_part = jnp.sum(squares, axis=0, keepdims=True)
    grads = jnp.concatenate(
        [(-error * norm_scale).astype(BF16), (-error_aux * norm_scale).astype(BF16)], 0
    )
    grads = jnp.pad(grads, ((0, 0), (0, dec_all.shape[1] - width)))

    def pulled_half(start):
        pulled = lax.dot_general(
            grads,
            dec_all[start : start + 2 * lat],
            (((1,), (1,)), ((), ())),
            preferred_element_type=F32,
        )
        return pulled[:rows] + pulled[rows:] * gate[:, start : start + 2 * lat].astype(F32)

    got_pulled = swap_core(pulled_half(2 * lat).astype(BF16)).astype(F32)
    pulled_sum = pulled_half(0) + got_pulled
    pulled_sum = jnp.stack([pulled_sum[:, :lat], pulled_sum[:, lat:]], 0).astype(BF16)
    loss_rows = jnp.concatenate(two_halves(loss_part), 0)
    loss_rows = jnp.pad(loss_rows, ((0, piece - 2), (0, 0)))
    packet = jnp.concatenate(
        [
            pulled_sum.reshape(z_size, piece, lat),
            jnp.broadcast_to(loss_rows[None], (z_size,) + loss_rows.shape),
        ],
        2,
    )
    arrived = lax.all_to_all(packet, "z", 0, 0, tiled=True).astype(F32)

    dec_term = lax.dot_general(
        after(grads, packet), both, (((0,), (0,)), ((), ())), preferred_element_type=F32
    ).astype(BF16)
    share = width // rep

    def rep_exchange(shares):
        own = lax.dynamic_index_in_dim(shares, rep_at, 0, False)
        parts = [own]
        for step in (1, 3, 2):
            outgoing = lax.dynamic_index_in_dim(shares, (rep_at + step) % rep, 0, False)
            parts.append(from_ahead(outgoing, "rep", -step))
        return parts

    dec_parts = rep_exchange(dec_term[:width].reshape(rep, share, lat_all))

    arrived = jnp.sum(arrived, axis=0)
    grad_piece = jnp.where(lat_piece > 0, arrived[:, :lat], 0.0).astype(BF16)
    loss_width = arrived[0:1, lat:] + arrived[1:2, lat:]
    grad_piece = shift_pieces(grad_piece, -1)
    loss_width = loss_width + swap_core(loss_width)
    grad_copies = z_copies(grad_piece)
    dec_sum = sum(part.astype(F32) for part in after(dec_parts, grad_copies)).astype(BF16)

    loss_out = two_halves(loss_width)
    dec_own_slot = lax.dynamic_slice_in_dim(dec_sum, core * 2 * lat, lat, 1)
    dec_across = lax.dynamic_slice_in_dim(dec_sum, (1 - core) * 2 * lat, lat, 1)
    incoming = [
        blk_move(with_rows(dec_sum[:, lat : 2 * lat], loss_out), 1, -1),
        blk_move(with_rows(dec_sum[:, 3 * lat :], loss_out), 3, -1),
        from_ahead(with_rows(dec_across, loss_out), "blk", 2),
    ]
    grad_mine = exchange_z(grad_copies).reshape(2 * rows, lat)
    incoming = after(incoming, grad_mine)
    dec_final = dec_own_slot.astype(F32) + sum(part[:share].astype(F32) for part in incoming)
    loss_blk = loss_width
    for part in incoming:
        both_rows = part[share : share + 2, :128].astype(F32)
        loss_blk = loss_blk + both_rows[0:1] + both_rows[1:2]
    grad_dec = jnp.transpose(dec_final)

    grad_pre = jnp.concatenate([grad_mine, swap_core(grad_mine)], 0)
    enc_term = lax.dot_general(
        x_all, grad_pre, (((0,), (0,)), ((), ())), preferred_element_type=F32
    ).astype(BF16)
    bias_term = jnp.sum(grad_pre.astype(F32), axis=0, keepdims=True).astype(BF16)
    loss_out = two_halves(loss_blk)
    quarter = lat // rep
    shares = [
        with_rows(
            enc_term[i * share : (i + 1) * share],
            [bias_term[:, i * quarter : (i + 1) * quarter]] + loss_out,
        )
        for i in range(rep)
    ]
    parts = rep_exchange(jnp.stack(shares, 0))
    grad_enc = sum(part[:share].astype(F32) for part in parts)
    last = sum(part[share : share + 3, :quarter].astype(F32) for part in parts)
    loss = jnp.sum(last[1:3]) / (total_tokens * width * 2 * z_size)
    return (loss, grad_enc, last[0], grad_dec)


def solution(mesh):
    sizes = mesh.shape
    fine = Mesh(
        mesh.devices.reshape(sizes["blk"], sizes["width"] // 2, 2, sizes["rep"]),
        ("blk", "z", "core", "rep"),
    )
    wide = ("z", "core")
    in_specs = (
        P(("blk", "rep"), wide),
        P(("blk", "rep"), wide),
        P(wide, "blk"),
        P("blk"),
        P("blk", wide),
        P("blk"),
        P(("blk", "rep"), None),
    )
    out_specs = (P(), P(wide + ("rep",), "blk"), P(("blk", "rep")), P("blk", wide + ("rep",)))
    return jax.shard_map(local, mesh=fine, in_specs=in_specs, out_specs=out_specs, check_vma=False)
```

time: 170 us -> 134 us (0.79)
  blocking collectives: 24.7 us -> 0 us
  between operations: 16.2 us -> 3.03 us
  starting transfers between devices: 54.5 us -> 64.7 us
  waiting for transfers between devices: 43 us -> 36.8 us
  local copies, waits for them, and re-layouts: 12.4 us -> 9 us
    ppermute x18 -> x8, waiting for transfers between devices: 35.9 us -> 8.57 us  [from_ahead(): lax.ppermute(block, axis, [((i + distance) % size, i) for i in range(size)])]
    all_to_all x1 -> x0, blocking collectives: 24.7 us -> none  [local(): lax.all_to_all((kept + got).reshape(z_size, piece, lat), 'z', 0, 0, tiled...]
    ppermute x0 -> x8, starting transfers between devices: none -> 11.7 us  [blk_move(): return lax.ppermute(block, ('blk', 'core'), route)]
    ppermute x0 -> x8, waiting for transfers between devices: none -> 11 us  [blk_move(): return lax.ppermute(block, ('blk', 'core'), route)]
    ppermute x18 -> x8, starting transfers between devices: 24 us -> 13.4 us  [from_ahead(): lax.ppermute(block, axis, [((i + distance) % size, i) for i in range(size)])]
    all_to_all x2 -> x3, starting transfers between devices: 20.2 us -> 26.2 us  [the longest x2 17.6 us: exchange_z(): return lax.all_to_all(copies, 'z', 0, 0, tiled=True)]
    all_to_all x2 -> x3, waiting for transfers between devices: 3.37 us -> 9.3 us  [the longest x1 9.21 us: local(): lax.all_to_all((kept + got).reshape(z_size, piece, lat), 'z', 0, 0, tiled...]
    all_to_all x1, waiting for transfers between devices: 1.85 us -> 5.8 us  [local(): arrived = lax.all_to_all(packet, 'z', 0, 0, tiled=True).astype(F32)]
  transfers between devices with their start and end apart: 28 -> 27, of which waited for: 14 -> 15; matrix products, arithmetic and copies ran while one was open for 9% -> 11% of each run, Pallas kernels for 3% -> 4%
where the time goes in v2:
time: 134 us; the launch traced here: 133 us
  starting transfers between devices  64.7 us (48%)
  waiting for transfers between devices  36.8 us (27%)
  local copies, waits for them, and re-layouts  9 us (7%)
  other arithmetic  8.67 us (6%)
  Pallas kernels  5.69 us (4%)
  matrix products  5.23 us (4%)
  between operations  3.03 us (2%)
    all_to_all x2, starting transfers between devices, exchange_z(): return lax.all_to_all(copies, 'z', 0, 0, tiled=True)  17.6 us
    ppermute x8, starting transfers between devices, from_ahead(): lax.ppermute(block, axis, [((i + distance) % size, i) for i in range(size)])  13.4 us
    ppermute x8, starting transfers between devices, blk_move(): return lax.ppermute(block, ('blk', 'core'), route)  11.7 us
    ppermute x8, waiting for transfers between devices, blk_move(): return lax.ppermute(block, ('blk', 'core'), route)  11 us
    all_to_all x1, waiting for transfers between devices, local(): lax.all_to_all((kept + got).reshape(z_size, piece, lat), 'z', 0, 0, tiled...  9.21 us
    ppermute x8, waiting for transfers between devices, from_ahead(): lax.ppermute(block, axis, [((i + distance) % size, i) for i in range(size)])  8.57 us
    all_to_all x1, starting transfers between devices, local(): lax.all_to_all((kept + got).reshape(z_size, piece, lat), 'z', 0, 0, tiled...  8.56 us
    all_to_all x1, starting transfers between devices, local(): arrived = lax.all_to_all(packet, 'z', 0, 0, tiled=True).astype(F32)  7.23 us
  transfers between devices with their start and end apart: 27, of which 15 were waited for; matrix products, arithmetic and copies ran while one was open for 11% of the time, Pallas kernels for 4%

profile of v2, /device:TPU:32, one launch (start us, length us, event | category | flops | bytes accessed | tf_op | source)
XLA Modules:
  0.0 133.1 jit_solution(14831347247804529486)
XLA Ops:
  0.7 2.8 %collective-permute-start = (bf16[128,448]{0,1:T(8,128)(2,1)}, bf16[128,448]{0,1:T(8,128)(2,1)S(1)}, u32[]{:S(2)}, u32[]{:S(2)}) collective-permute-start(bf16[128,448]{0,1:T(8,128)(2,1)} %param.7), channel_id=1, source_target_pairs={{0,192},{4,68},{64,0},{68,132},{128,64},{132,196},{192,128},{196,4... | collective-permute-start | bytes 344072 | tf_op jit(solution)/shard_map/ppermute | solution.py:27
  3.5 2.3 %collective-permute-start.2 = (bf16[128,448]{0,1:T(8,128)(2,1)}, bf16[128,448]{0,1:T(8,128)(2,1)S(1)}, u32[]{:S(2)}, u32[]{:S(2)}) collective-permute-start(bf16[128,448]{0,1:T(8,128)(2,1)} %param.7), channel_id=1, source_target_pairs={{128,0},{192,64},{0,128},{64,192},{129,1},{193,65},{1,129},{65,193... | collective-permute-start | bytes 344072 | tf_op jit(solution)/shard_map/ppermute | solution.py:17
  5.8 1.0 constant_dynamic-update-slice_fusion.6
  6.8 0.9 collective-permute-done
  7.7 4.0 %collective-permute-done.1 = bf16[128,448]{0,1:T(8,128)(2,1)S(1)} collective-permute-done((bf16[128,448]{0,1:T(8,128)(2,1)}, bf16[128,448]{0,1:T(8,128)(2,1)S(1)}, u32[]{:S(2)}, u32[]{:S(2)}) %collective-permute-start.1) | collective-permute-done | bytes 114720 | tf_op jit(solution)/shard_map/ppermute | solution.py:27
  12.5 1.9 %pad_maximum_fusion.2 = (bf16[512,464]{0,1:T(8,128)(2,1)}, bf16[2048,464]{0,1:T(8,128)(2,1)S(1)}) fusion(bf16[512,16]{0,1:T(8,128)(2,1)S(1)} %broadcast_in_dim.14, bf16[512,448]{0,1:T(8,128)(2,1)} %param.11, bf16[2048,464]{0,1:T(8,128)(2,1)S(1)} %broadcast_in_dim.16, s32[]{:T(128)S(6)} %select_n.61), kind=kLoop, calls=%fused_computation.25 | loop fusion | flops 950272 | bytes 1425412 | tf_op jit(solution)/shard_map/concatenate | solution.py:131
  14.4 3.2 %collective-permute-start.5 = (bf16[512,464]{0,1:T(8,128)(2,1)}, bf16[512,464]{0,1:T(8,128)(2,1)}, u32[]{:S(2)}, u32[]{:S(2)}) collective-permute-start(bf16[512,464]{0,1:T(8,128)(2,1)} %get-tuple-element.17), channel_id=1, source_target_pairs={{0,192},{4,68},{64,0},{68,132},{128,64},{132,196},{192,128},{196,4... | collective-permute-start | bytes 1425416 | tf_op jit(solution)/shard_map/ppermute | solution.py:27
  17.7 2.2 %convolution_add_fusion = f32[256,512]{1,0:T(8,128)} fusion(f32[256,512]{1,0:T(8,128)} %collective-permute-done.3, bf16[448,512]{1,0:T(8,128)(2,1)S(1)} %copy-done, bf16[512,448]{0,1:T(8,128)(2,1)S(1)} %constant_dynamic-update-slice_fusion.3), kind=kOutput, calls=%fused_computation.2 | convolution fusion | flops 117571584 | bytes 1736704 | tf_op jit(solution)/shard_map/dot_general | solution.py:138
  19.8 8.6 %all-to-all-start = ((f32[8,32,512]{2,1,0:T(8,128)}), f32[8,32,512]{2,1,0:T(8,128)S(1)}, u32[]{:S(2)}, u32[]{:S(2)}) async-start(f32[8,32,512]{2,1,0:T(8,128)} %bitcast), calls=%async_computation | async-start | bytes 1048576 | tf_op jit(solution)/shard_map/all_to_all | solution.py:139
  28.4 5.7 %shard_map.102 = bf16[128,2048]{1,0:T(8,128)(2,1)} custom-call(s32[1]{0:T(128)} %bitcast.1.own_ref, s32[128,512]{1,0:T(8,128)} %picks_ref.1), custom_call_target="tpu_custom_call" | custom-call | flops 20000000000 | bytes 1000000 | tf_op jit(solution)/shard_map/pallas_call | solution.py:82
  34.1 9.2 %all-to-all-done = f32[8,32,512]{2,1,0:T(8,128)S(1)} async-done(((f32[8,32,512]{2,1,0:T(8,128)}), f32[8,32,512]{2,1,0:T(8,128)S(1)}, u32[]{:S(2)}, u32[]{:S(2)}) %all-to-all-start) | async-done | bytes 524320 | tf_op jit(solution)/shard_map/all_to_all | solution.py:139
  43.4 0.7 collective-permute-start.6
  44.1 0.7 broadcast_in_dim.15
  44.8 9.6 %all-to-all-start.1 = ((bf16[8,32,512]{2,1,0:T(8,128)(2,1)}), bf16[8,32,512]{2,1,0:T(8,128)(2,1)S(1)}, u32[]{:S(2)}, u32[]{:S(2)}) async-start(bf16[8,32,512]{2,1,0:T(8,128)(2,1)} %broadcast_in_dim.15), calls=%async_computation.1 | async-start | bytes 524288 | tf_op jit(solution)/shard_map/all_to_all | solution.py:51
  54.5 1.0 slice.196
  55.6 1.0 slice.197
  56.5 3.3 %collective-permute-start.9 = (bf16[256,464]{0,1:T(8,128)(2,1)S(1)}, bf16[256,464]{0,1:T(8,128)(2,1)S(1)}, u32[]{:S(2)}, u32[]{:S(2)}) collective-permute-start(bf16[256,464]{0,1:T(8,128)(2,1)S(1)} %slice.197), channel_id=1, source_target_pairs={{0,192},{4,68},{64,0},{68,132},{128,64},{132,196},{192,128},{196,4... | collective-permute-start | bytes 712712 | tf_op jit(solution)/shard_map/ppermute | solution.py:27
  59.8 1.1 constant_dynamic-update-slice_fusion.1
  60.9 1.1 constant_dynamic-update-slice_fusion
  62.0 0.9 collective-permute-done.8
  62.9 1.1 collective-permute-done.9
  64.0 1.8 %collective-permute-start.7 = (bf16[2,128,512]{2,1,0:T(8,128)(2,1)S(1)}, bf16[2,128,512]{2,1,0:T(8,128)(2,1)S(1)}, u32[]{:S(2)}, u32[]{:S(2)}) collective-permute-start(bf16[2,128,512]{2,1,0:T(8,128)(2,1)S(1)} %bitcast.54), channel_id=1, source_target_pairs={{0,4},{4,0},{1,5},{5,1},{2,6},{6,2},{3,7},{7,3},{8,12},{12,8},{9,1... | collective-permute-start | bytes 786440 | tf_op jit(solution)/shard_map/ppermute | solution.py:31
  65.9 1.1 collective-permute-done.7
  67.0 1.2 maximum_multiply_fusion
  68.3 0.7 fusion.35
  71.8 0.8 pad_maximum_fusion.3
  72.6 7.2 %all-to-all-start.2 = ((bf16[8,32,640]{2,1,0:T(8,128)(2,1)}), bf16[8,32,640]{2,1,0:T(8,128)(2,1)S(1)}, u32[]{:S(2)}, u32[]{:S(2)}) async-start(bf16[8,32,640]{2,1,0:T(8,128)(2,1)} %pad_maximum_fusion.3), calls=%async_computation.2 | async-start | bytes 655360 | tf_op jit(solution)/shard_map/all_to_all | solution.py:186
  80.9 1.8 %collective-permute-start.14 = (bf16[112,2048]{1,0:T(8,128)(2,1)S(1)}, bf16[112,2048]{1,0:T(8,128)(2,1)}, u32[]{:S(2)}, u32[]{:S(2)}) collective-permute-start(bf16[112,2048]{1,0:T(8,128)(2,1)S(1)} %get-tuple-element.38), channel_id=1, source_target_pairs={{3,0},{0,1},{1,2},{2,3},{7,4},{4,5},{5,6},{6,7},{11,8},{8,9},{9,10... | collective-permute-start | bytes 1376264 | tf_op jit(solution)/shard_map/ppermute | solution.py:17
  82.7 1.7 %collective-permute-start.15 = (bf16[112,2048]{1,0:T(8,128)(2,1)S(1)}, bf16[112,2048]{1,0:T(8,128)(2,1)}, u32[]{:S(2)}, u32[]{:S(2)}) collective-permute-start(bf16[112,2048]{1,0:T(8,128)(2,1)S(1)} %get-tuple-element.37), channel_id=1, source_target_pairs={{1,0},{2,1},{3,2},{0,3},{5,4},{6,5},{7,6},{4,7},{9,8},{10,9},{11,1... | collective-permute-start | bytes 1376264 | tf_op jit(solution)/shard_map/ppermute | solution.py:17
  84.4 2.0 %collective-permute-start.16 = (bf16[112,2048]{1,0:T(8,128)(2,1)S(1)}, bf16[112,2048]{1,0:T(8,128)(2,1)}, u32[]{:S(2)}, u32[]{:S(2)}) collective-permute-start(bf16[112,2048]{1,0:T(8,128)(2,1)S(1)} %get-tuple-element.36), channel_id=1, source_target_pairs={{2,0},{3,1},{0,2},{1,3},{6,4},{7,5},{4,6},{5,7},{10,8},{11,9},{8,1... | collective-permute-start | bytes 1376264 | tf_op jit(solution)/shard_map/ppermute | solution.py:17
  86.4 5.8 %all-to-all-done.2 = bf16[8,32,640]{2,1,0:T(8,128)(2,1)S(1)} async-done(((bf16[8,32,640]{2,1,0:T(8,128)(2,1)}), bf16[8,32,640]{2,1,0:T(8,128)(2,1)S(1)}, u32[]{:S(2)}, u32[]{:S(2)}) %all-to-all-start.2) | async-done | bytes 327712 | tf_op jit(solution)/shard_map/all_to_all | solution.py:186
  92.4 0.7 collective-permute-start.11
  93.5 0.7 broadcast_in_dim.19
  94.2 8.0 %all-to-all-start.3 = ((bf16[8,32,512]{2,1,0:T(8,128)(2,1)}), bf16[8,32,512]{2,1,0:T(8,128)(2,1)S(1)}, u32[]{:S(2)}, u32[]{:S(2)}) async-start(bf16[8,32,512]{2,1,0:T(8,128)(2,1)} %broadcast_in_dim.19), calls=%async_computation.3 | async-start | bytes 524288 | tf_op jit(solution)/shard_map/all_to_all | solution.py:51
  102.2 1.7 %collective-permute-done.15 = bf16[112,2048]{1,0:T(8,128)(2,1)} collective-permute-done((bf16[112,2048]{1,0:T(8,128)(2,1)S(1)}, bf16[112,2048]{1,0:T(8,128)(2,1)}, u32[]{:S(2)}, u32[]{:S(2)}) %collective-permute-start.15) | collective-permute-done | bytes 458784 | tf_op jit(solution)/shard_map/ppermute | solution.py:17
  103.9 1.9 %collective-permute-done.16 = bf16[112,2048]{1,0:T(8,128)(2,1)} collective-permute-done((bf16[112,2048]{1,0:T(8,128)(2,1)S(1)}, bf16[112,2048]{1,0:T(8,128)(2,1)}, u32[]{:S(2)}, u32[]{:S(2)}) %collective-permute-start.16) | collective-permute-done | bytes 458784 | tf_op jit(solution)/shard_map/ppermute | solution.py:17
  105.8 1.6 %add_convert_fusion = bf16[112,2048]{1,0:T(8,128)(2,1)S(1)} fusion(bf16[112,2048]{1,0:T(8,128)(2,1)} %collective-permute-done.16, bf16[112,2048]{1,0:T(8,128)(2,1)} %collective-permute-done.15, bf16[112,2048]{1,0:T(8,128)(2,1)} %collective-permute-done.14, bf16[112,2048]{1,0:T(8,128)(2,1)S(1)} %get-tuple-element.23), kind=kLoop, calls=%fused_computation.8 | loop fusion | flops 1835008 | bytes 2293760 | tf_op jit(solution)/shard_map/convert_element_type | solution.py:209
  107.5 2.2 %collective-permute-start.17 = (bf16[128,512]{1,0:T(8,128)(2,1)S(1)}, bf16[128,512]{1,0:T(8,128)(2,1)S(1)}, u32[]{:S(2)}, u32[]{:S(2)}) collective-permute-start(bf16[128,512]{1,0:T(8,128)(2,1)S(1)} %get-tuple-element.66), channel_id=1, source_target_pairs={{0,192},{4,68},{64,0},{68,132},{128,64},{132,196},{192,128},{196,4... | collective-permute-start | bytes 393224 | tf_op jit(solution)/shard_map/ppermute | solution.py:27
  109.7 1.6 %collective-permute-start.19 = (bf16[128,512]{1,0:T(8,128)(2,1)S(1)}, bf16[128,512]{1,0:T(8,128)(2,1)S(1)}, u32[]{:S(2)}, u32[]{:S(2)}) collective-permute-start(bf16[128,512]{1,0:T(8,128)(2,1)S(1)} %get-tuple-element.65), channel_id=1, source_target_pairs={{128,0},{192,64},{0,128},{64,192},{129,1},{193,65},{1,129},{65,193... | collective-permute-start | bytes 393224 | tf_op jit(solution)/shard_map/ppermute | solution.py:17
  111.4 2.5 %collective-permute-start.12 = (bf16[256,512]{1,0:T(8,128)(2,1)S(1)}, bf16[256,512]{1,0:T(8,128)(2,1)S(1)}, u32[]{:S(2)}, u32[]{:S(2)}) collective-permute-start(bf16[256,512]{1,0:T(8,128)(2,1)S(1)} %bitcast.55), channel_id=1, source_target_pairs={{0,4},{4,0},{1,5},{5,1},{2,6},{6,2},{3,7},{7,3},{8,12},{12,8},{9,1... | collective-permute-start | bytes 786440 | tf_op jit(solution)/shard_map/ppermute | solution.py:31
  113.8 4.2 %collective-permute-done.18 = bf16[128,512]{1,0:T(8,128)(2,1)S(1)} collective-permute-done((bf16[128,512]{1,0:T(8,128)(2,1)S(1)}, bf16[128,512]{1,0:T(8,128)(2,1)S(1)}, u32[]{:S(2)}, u32[]{:S(2)}) %collective-permute-start.18) | collective-permute-done | bytes 131104 | tf_op jit(solution)/shard_map/ppermute | solution.py:27
  119.7 1.2 collective-permute-start.20
  120.9 2.1 %collective-permute-start.21 = (bf16[128,512]{1,0:T(8,128)(2,1)S(1)}, bf16[128,512]{1,0:T(8,128)(2,1)S(1)}, u32[]{:S(2)}, u32[]{:S(2)}) collective-permute-start(bf16[128,512]{1,0:T(8,128)(2,1)S(1)} %get-tuple-element.45), channel_id=1, source_target_pairs={{1,0},{2,1},{3,2},{0,3},{5,4},{6,5},{7,6},{4,7},{9,8},{10,9},{11,1... | collective-permute-start | bytes 393224 | tf_op jit(solution)/shard_map/ppermute | solution.py:17
  123.0 0.7 collective-permute-start.22
  123.7 0.7 add_bitcast_fusion
  124.5 2.9 %collective-permute-done.20 = bf16[128,512]{1,0:T(8,128)(2,1)S(1)} collective-permute-done((bf16[128,512]{1,0:T(8,128)(2,1)S(1)}, bf16[128,512]{1,0:T(8,128)(2,1)S(1)}, u32[]{:S(2)}, u32[]{:S(2)}) %collective-permute-start.20) | collective-permute-done | bytes 131104 | tf_op jit(solution)/shard_map/ppermute | solution.py:17
  127.3 2.1 %collective-permute-done.22 = bf16[128,512]{1,0:T(8,128)(2,1)S(1)} collective-permute-done((bf16[128,512]{1,0:T(8,128)(2,1)S(1)}, bf16[128,512]{1,0:T(8,128)(2,1)S(1)}, u32[]{:S(2)}, u32[]{:S(2)}) %collective-permute-start.22) | collective-permute-done | bytes 131104 | tf_op jit(solution)/shard_map/ppermute | solution.py:17
  131.2 0.8 fusion.23
  (105 shorter events, 8.3 us)
Async XLA Ops:
  0.6 11.2 %copy-start = (bf16[448,512]{1,0:T(8,128)(2,1)S(1)}, bf16[448,512]{1,0:T(8,128)(2,1)}, u32[]{:S(2)}) copy-start(bf16[448,512]{1,0:T(8,128)(2,1)} %param.9) | copy-start | bytes 1376260
  0.6 11.6 %copy-start.7 = (s32[512]{0:T(512)S(1)}, s32[512]{0:T(512)}, u32[]{:S(2)}) copy-start(s32[512]{0:T(512)} %param.12) | copy-start | bytes 6148
  0.7 7.0 %collective-permute-start = (bf16[128,448]{0,1:T(8,128)(2,1)}, bf16[128,448]{0,1:T(8,128)(2,1)S(1)}, u32[]{:S(2)}, u32[]{:S(2)}) collective-permute-start(bf16[128,448]{0,1:T(8,128)(2,1)} %param.7), channel_id=1, source_target_pairs={{0,192},{4,68},{64,0},{68,132},{128,64},{132,196},{192,128},{196,4... | collective-permute-start | bytes 344072 | tf_op jit(solution)/shard_map/ppermute | solution.py:27
  3.5 8.2 %collective-permute-start.1 = (bf16[128,448]{0,1:T(8,128)(2,1)}, bf16[128,448]{0,1:T(8,128)(2,1)S(1)}, u32[]{:S(2)}, u32[]{:S(2)}) collective-permute-start(bf16[128,448]{0,1:T(8,128)(2,1)} %param.7), channel_id=1, source_target_pairs={{0,64},{4,196},{64,128},{68,4},{128,192},{132,68},{192,0},{196,132... | collective-permute-start | bytes 344072 | tf_op jit(solution)/shard_map/ppermute | solution.py:27
  3.5 8.2 %collective-permute-start.2 = (bf16[128,448]{0,1:T(8,128)(2,1)}, bf16[128,448]{0,1:T(8,128)(2,1)S(1)}, u32[]{:S(2)}, u32[]{:S(2)}) collective-permute-start(bf16[128,448]{0,1:T(8,128)(2,1)} %param.7), channel_id=1, source_target_pairs={{128,0},{192,64},{0,128},{64,192},{129,1},{193,65},{1,129},{65,193... | collective-permute-start | bytes 344072 | tf_op jit(solution)/shard_map/ppermute | solution.py:17
  12.1 5.5 %collective-permute-start.3 = (f32[256,512]{1,0:T(8,128)S(1)}, f32[256,512]{1,0:T(8,128)}, u32[]{:S(2)}, u32[]{:S(2)}) collective-permute-start(f32[256,512]{1,0:T(8,128)S(1)} %fusion.19), channel_id=1, source_target_pairs={{0,4},{4,0},{1,5},{5,1},{2,6},{6,2},{3,7},{7,3},{8,12},{12,8},{9,1... | collective-permute-start | bytes 1572872 | tf_op jit(solution)/shard_map/ppermute | solution.py:31
  14.4 29.0 %collective-permute-start.4 = (bf16[512,464]{0,1:T(8,128)(2,1)}, bf16[512,464]{0,1:T(8,128)(2,1)}, u32[]{:S(2)}, u32[]{:S(2)}) collective-permute-start(bf16[512,464]{0,1:T(8,128)(2,1)} %get-tuple-element.17), channel_id=1, source_target_pairs={{0,64},{4,196},{64,128},{68,4},{128,192},{132,68},{192,0},{196,132... | collective-permute-start | bytes 1425416 | tf_op jit(solution)/shard_map/ppermute | solution.py:27
  14.4 29.0 %collective-permute-start.5 = (bf16[512,464]{0,1:T(8,128)(2,1)}, bf16[512,464]{0,1:T(8,128)(2,1)}, u32[]{:S(2)}, u32[]{:S(2)}) collective-permute-start(bf16[512,464]{0,1:T(8,128)(2,1)} %get-tuple-element.17), channel_id=1, source_target_pairs={{0,192},{4,68},{64,0},{68,132},{128,64},{132,196},{192,128},{196,4... | collective-permute-start | bytes 1425416 | tf_op jit(solution)/shard_map/ppermute | solution.py:27
  19.8 23.5 %all-to-all-start = ((f32[8,32,512]{2,1,0:T(8,128)}), f32[8,32,512]{2,1,0:T(8,128)S(1)}, u32[]{:S(2)}, u32[]{:S(2)}) async-start(f32[8,32,512]{2,1,0:T(8,128)} %bitcast), calls=%async_computation | async-start | bytes 1048576 | tf_op jit(solution)/shard_map/all_to_all | solution.py:139
  28.4 14.9 %copy-start.6 = (f32[512]{0:T(512)S(1)}, f32[512]{0:T(512)}, u32[]{:S(2)}) copy-start(f32[512]{0:T(512)} %param.10) | copy-start | bytes 6148
  43.4 0.7 collective-permute-start.6
  44.8 19.2 %all-to-all-start.1 = ((bf16[8,32,512]{2,1,0:T(8,128)(2,1)}), bf16[8,32,512]{2,1,0:T(8,128)(2,1)S(1)}, u32[]{:S(2)}, u32[]{:S(2)}) async-start(bf16[8,32,512]{2,1,0:T(8,128)(2,1)} %broadcast_in_dim.15), calls=%async_computation.1 | async-start | bytes 524288 | tf_op jit(solution)/shard_map/all_to_all | solution.py:51
  55.5 7.4 %collective-permute-start.8 = (bf16[256,464]{0,1:T(8,128)(2,1)S(1)}, bf16[256,464]{0,1:T(8,128)(2,1)S(1)}, u32[]{:S(2)}, u32[]{:S(2)}) collective-permute-start(bf16[256,464]{0,1:T(8,128)(2,1)S(1)} %slice.196), channel_id=1, source_target_pairs={{0,64},{4,196},{64,128},{68,4},{128,192},{132,68},{192,0},{196,132... | collective-permute-start | bytes 712712 | tf_op jit(solution)/shard_map/ppermute | solution.py:27
  56.5 7.4 %collective-permute-start.9 = (bf16[256,464]{0,1:T(8,128)(2,1)S(1)}, bf16[256,464]{0,1:T(8,128)(2,1)S(1)}, u32[]{:S(2)}, u32[]{:S(2)}) collective-permute-start(bf16[256,464]{0,1:T(8,128)(2,1)S(1)} %slice.197), channel_id=1, source_target_pairs={{0,192},{4,68},{64,0},{68,132},{128,64},{132,196},{192,128},{196,4... | collective-permute-start | bytes 712712 | tf_op jit(solution)/shard_map/ppermute | solution.py:27
  64.0 3.0 %collective-permute-start.7 = (bf16[2,128,512]{2,1,0:T(8,128)(2,1)S(1)}, bf16[2,128,512]{2,1,0:T(8,128)(2,1)S(1)}, u32[]{:S(2)}, u32[]{:S(2)}) collective-permute-start(bf16[2,128,512]{2,1,0:T(8,128)(2,1)S(1)} %bitcast.54), channel_id=1, source_target_pairs={{0,4},{4,0},{1,5},{5,1},{2,6},{6,2},{3,7},{7,3},{8,12},{12,8},{9,1... | collective-permute-start | bytes 786440 | tf_op jit(solution)/shard_map/ppermute | solution.py:31
  65.9 3.1 %copy-start.1 = (bf16[4,32,512]{2,1,0:T(8,128)(2,1)}, bf16[4,32,512]{2,1,0:T(8,128)(2,1)S(1)}, u32[]{:S(2)}) copy-start(bf16[4,32,512]{2,1,0:T(8,128)(2,1)S(1)} %get-tuple-element.59) | copy-start | bytes 393220
  68.3 0.8 copy-start.3
  68.3 1.0 copy-start.5
  70.0 1.6 %collective-permute-start.10 = (bf16[128,1024]{1,0:T(8,128)(2,1)S(1)}, bf16[128,1024]{1,0:T(8,128)(2,1)S(1)}, u32[]{:S(2)}, u32[]{:S(2)}) collective-permute-start(bf16[128,1024]{1,0:T(8,128)(2,1)S(1)} %fusion.5), channel_id=1, source_target_pairs={{0,4},{4,0},{1,5},{5,1},{2,6},{6,2},{3,7},{7,3},{8,12},{12,8},{9,1... | collective-permute-start | bytes 786440 | tf_op jit(solution)/shard_map/ppermute | solution.py:31
  71.7 8.1 %copy-start.2 = (bf16[4,32,512]{2,1,0:T(8,128)(2,1)S(1)}, bf16[4,32,512]{2,1,0:T(8,128)(2,1)}, u32[]{:S(2)}) copy-start(bf16[4,32,512]{2,1,0:T(8,128)(2,1)} %copy-done.1) | copy-start | bytes 393220
  71.7 8.1 %copy-start.4 = (bf16[128,2048]{1,0:T(8,128)(2,1)S(1)}, bf16[128,2048]{1,0:T(8,128)(2,1)}, u32[]{:S(2)}) copy-start(bf16[128,2048]{1,0:T(8,128)(2,1)} %copy-done.3) | copy-start | bytes 1572868
  72.6 19.6 %all-to-all-start.2 = ((bf16[8,32,640]{2,1,0:T(8,128)(2,1)}), bf16[8,32,640]{2,1,0:T(8,128)(2,1)S(1)}, u32[]{:S(2)}, u32[]{:S(2)}) async-start(bf16[8,32,640]{2,1,0:T(8,128)(2,1)} %pad_maximum_fusion.3), calls=%async_computation.2 | async-start | bytes 655360 | tf_op jit(solution)/shard_map/all_to_all | solution.py:186
  80.9 21.3 %collective-permute-start.14 = (bf16[112,2048]{1,0:T(8,128)(2,1)S(1)}, bf16[112,2048]{1,0:T(8,128)(2,1)}, u32[]{:S(2)}, u32[]{:S(2)}) collective-permute-start(bf16[112,2048]{1,0:T(8,128)(2,1)S(1)} %get-tuple-element.38), channel_id=1, source_target_pairs={{3,0},{0,1},{1,2},{2,3},{7,4},{4,5},{5,6},{6,7},{11,8},{8,9},{9,10... | collective-permute-start | bytes 1376264 | tf_op jit(solution)/shard_map/ppermute | solution.py:17
  82.7 21.1 %collective-permute-start.15 = (bf16[112,2048]{1,0:T(8,128)(2,1)S(1)}, bf16[112,2048]{1,0:T(8,128)(2,1)}, u32[]{:S(2)}, u32[]{:S(2)}) collective-permute-start(bf16[112,2048]{1,0:T(8,128)(2,1)S(1)} %get-tuple-element.37), channel_id=1, source_target_pairs={{1,0},{2,1},{3,2},{0,3},{5,4},{6,5},{7,6},{4,7},{9,8},{10,9},{11,1... | collective-permute-start | bytes 1376264 | tf_op jit(solution)/shard_map/ppermute | solution.py:17
  84.4 21.4 %collective-permute-start.16 = (bf16[112,2048]{1,0:T(8,128)(2,1)S(1)}, bf16[112,2048]{1,0:T(8,128)(2,1)}, u32[]{:S(2)}, u32[]{:S(2)}) collective-permute-start(bf16[112,2048]{1,0:T(8,128)(2,1)S(1)} %get-tuple-element.36), channel_id=1, source_target_pairs={{2,0},{3,1},{0,2},{1,3},{6,4},{7,5},{4,6},{5,7},{10,8},{11,9},{8,1... | collective-permute-start | bytes 1376264 | tf_op jit(solution)/shard_map/ppermute | solution.py:17
  92.2 1.2 collective-permute-start.13
  92.4 1.1 collective-permute-start.11
  94.2 17.2 %all-to-all-start.3 = ((bf16[8,32,512]{2,1,0:T(8,128)(2,1)}), bf16[8,32,512]{2,1,0:T(8,128)(2,1)S(1)}, u32[]{:S(2)}, u32[]{:S(2)}) async-start(bf16[8,32,512]{2,1,0:T(8,128)(2,1)} %broadcast_in_dim.19), calls=%async_computation.3 | async-start | bytes 524288 | tf_op jit(solution)/shard_map/all_to_all | solution.py:51
  105.8 12.5 %copy-start.8 = (pred[1,512]{1,0:T(4,128)(4,1)S(1)}, pred[1,512]{1,0:T(4,128)(4,1)}, u32[]{:S(2)}) copy-start(pred[1,512]{1,0:T(4,128)(4,1)} %constant.102.clone.1) | copy-start | bytes 1540
  107.5 6.3 %collective-permute-start.17 = (bf16[128,512]{1,0:T(8,128)(2,1)S(1)}, bf16[128,512]{1,0:T(8,128)(2,1)S(1)}, u32[]{:S(2)}, u32[]{:S(2)}) collective-permute-start(bf16[128,512]{1,0:T(8,128)(2,1)S(1)} %get-tuple-element.66), channel_id=1, source_target_pairs={{0,192},{4,68},{64,0},{68,132},{128,64},{132,196},{192,128},{196,4... | collective-permute-start | bytes 393224 | tf_op jit(solution)/shard_map/ppermute | solution.py:27
  109.7 8.3 %collective-permute-start.18 = (bf16[128,512]{1,0:T(8,128)(2,1)S(1)}, bf16[128,512]{1,0:T(8,128)(2,1)S(1)}, u32[]{:S(2)}, u32[]{:S(2)}) collective-permute-start(bf16[128,512]{1,0:T(8,128)(2,1)S(1)} %get-tuple-element.67), channel_id=1, source_target_pairs={{0,64},{4,196},{64,128},{68,4},{128,192},{132,68},{192,0},{196,132... | collective-permute-start | bytes 393224 | tf_op jit(solution)/shard_map/ppermute | solution.py:27
  109.7 8.3 %collective-permute-start.19 = (bf16[128,512]{1,0:T(8,128)(2,1)S(1)}, bf16[128,512]{1,0:T(8,128)(2,1)S(1)}, u32[]{:S(2)}, u32[]{:S(2)}) collective-permute-start(bf16[128,512]{1,0:T(8,128)(2,1)S(1)} %get-tuple-element.65), channel_id=1, source_target_pairs={{128,0},{192,64},{0,128},{64,192},{129,1},{193,65},{1,129},{65,193... | collective-permute-start | bytes 393224 | tf_op jit(solution)/shard_map/ppermute | solution.py:17
  111.4 6.8 %collective-permute-start.12 = (bf16[256,512]{1,0:T(8,128)(2,1)S(1)}, bf16[256,512]{1,0:T(8,128)(2,1)S(1)}, u32[]{:S(2)}, u32[]{:S(2)}) collective-permute-start(bf16[256,512]{1,0:T(8,128)(2,1)S(1)} %bitcast.55), channel_id=1, source_target_pairs={{0,4},{4,0},{1,5},{5,1},{2,6},{6,2},{3,7},{7,3},{8,12},{12,8},{9,1... | collective-permute-start | bytes 786440 | tf_op jit(solution)/shard_map/ppermute | solution.py:31
  119.7 7.7 %collective-permute-start.20 = (bf16[128,512]{1,0:T(8,128)(2,1)S(1)}, bf16[128,512]{1,0:T(8,128)(2,1)S(1)}, u32[]{:S(2)}, u32[]{:S(2)}) collective-permute-start(bf16[128,512]{1,0:T(8,128)(2,1)S(1)} %get-tuple-element.46), channel_id=1, source_target_pairs={{3,0},{0,1},{1,2},{2,3},{7,4},{4,5},{5,6},{6,7},{11,8},{8,9},{9,10... | collective-permute-start | bytes 393224 | tf_op jit(solution)/shard_map/ppermute | solution.py:17
  120.9 6.4 %collective-permute-start.21 = (bf16[128,512]{1,0:T(8,128)(2,1)S(1)}, bf16[128,512]{1,0:T(8,128)(2,1)S(1)}, u32[]{:S(2)}, u32[]{:S(2)}) collective-permute-start(bf16[128,512]{1,0:T(8,128)(2,1)S(1)} %get-tuple-element.45), channel_id=1, source_target_pairs={{1,0},{2,1},{3,2},{0,3},{5,4},{6,5},{7,6},{4,7},{9,8},{10,9},{11,1... | collective-permute-start | bytes 393224 | tf_op jit(solution)/shard_map/ppermute | solution.py:17
  123.0 6.5 %collective-permute-start.22 = (bf16[128,512]{1,0:T(8,128)(2,1)S(1)}, bf16[128,512]{1,0:T(8,128)(2,1)S(1)}, u32[]{:S(2)}, u32[]{:S(2)}) collective-permute-start(bf16[128,512]{1,0:T(8,128)(2,1)S(1)} %get-tuple-element.44), channel_id=1, source_target_pairs={{2,0},{3,1},{0,2},{1,3},{6,4},{7,5},{4,6},{5,7},{10,8},{11,9},{8,1... | collective-permute-start | bytes 393224 | tf_op jit(solution)/shard_map/ppermute | solution.py:17

commit v3 on v2

--- a/solution.py
+++ b/solution.py
@@ -91,7 +91,7 @@
             pltpu.VMEM((count, rows), jnp.int32),
             pltpu.VMEM((count, rows), jnp.int32),
         ],
-        cost_estimate=pl.CostEstimate(flops=20_000_000_000, bytes_accessed=1_000_000, transcendentals=0),
+        cost_estimate=pl.CostEstimate(flops=20_000_000, bytes_accessed=1_000_000, transcendentals=0),
     )(own.reshape(1).astype(jnp.int32), picks)
 
 
@@ -126,12 +126,12 @@
 
     x_1, x_3 = blk_move(inputs, 1, -1), blk_move(inputs, 3, -1)
     x_2 = from_ahead(inputs, "blk", 2)
-    x_all = in_slots(inputs, x_1, x_2, x_3)
     dead = jnp.broadcast_to(dead_mask.astype(BF16)[:, None], (lat, 16))
     dec_own = jnp.concatenate([dec_weight, dead], 1)
-    dec_sent = after(dec_own, x_1)
+    dec_sent, x_2 = lax.optimization_barrier((dec_own, x_2))
+    x_all = in_slots(inputs, x_1, x_2, x_3)
     dec_1, dec_3 = blk_move(dec_sent, 1, 1), blk_move(dec_sent, 3, 1)
-    half = lat // 2
+    half = dec_own.shape[1] // 32 * 16
     picked = picked_latents(aux_picks, blk_at + 2 * core, lat_all)
 
     got = swap_core(jnp.dot(x_all[2 * rows :], enc_weight, preferred_element_type=F32))
@@ -139,10 +139,11 @@
     parts = lax.all_to_all((kept + got).reshape(z_size, piece, lat), "z", 0, 0, tiled=True)
     preact = jnp.sum(parts, axis=0) + enc_bias[None, :]
     lat_piece = jnp.maximum(preact, 0.0).astype(BF16)
-    lat_piece, picked, dec_1, dec_3 = lax.optimization_barrier((lat_piece, picked, dec_1, dec_3))
-    dec_2 = [blk_move(dec_1[:half], 1, 1), blk_move(dec_3[half:], 3, 1)]
+    lat_piece, picked = lax.optimization_barrier((lat_piece, picked))
+    dec_1, dec_3 = after((dec_1, dec_3), lat_piece)
+    dec_2 = [blk_move(dec_1[:, :half], 1, 1), blk_move(dec_3[:, half:], 3, 1)]
     lat_piece = shift_pieces(lat_piece, 1)
-    dec_all = in_slots(dec_own, dec_1, jnp.concatenate(dec_2, 0), dec_3)
+    dec_all = in_slots(dec_own, dec_1, jnp.concatenate(dec_2, 1), dec_3)
     gate = picked * dec_all[:, width][None, :]
 
     lat_mine = exchange_z(z_copies(lat_piece)).reshape(2, rows, lat)
@@ -216,6 +217,7 @@
         blk_move(with_rows(dec_sum[:, 3 * lat :], loss_out), 3, -1),
         from_ahead(with_rows(dec_across, loss_out), "blk", 2),
     ]
+
     grad_mine = exchange_z(grad_copies).reshape(2 * rows, lat)
     incoming = after(incoming, grad_mine)
     dec_final = dec_own_slot.astype(F32) + sum(part[:share].astype(F32) for part in incoming)
@@ -224,22 +226,18 @@
         both_rows = part[share : share + 2, :128].astype(F32)
         loss_blk = loss_blk + both_rows[0:1] + both_rows[1:2]
     grad_dec = jnp.transpose(dec_final)
-
     grad_pre = jnp.concatenate([grad_mine, swap_core(grad_mine)], 0)
     enc_term = lax.dot_general(
         x_all, grad_pre, (((0,), (0,)), ((), ())), preferred_element_type=F32
     ).astype(BF16)
     bias_term = jnp.sum(grad_pre.astype(F32), axis=0, keepdims=True).astype(BF16)
-    loss_out = two_halves(loss_blk)
+
     quarter = lat // rep
-    shares = [
-        with_rows(
-            enc_term[i * share : (i + 1) * share],
-            [bias_term[:, i * quarter : (i + 1) * quarter]] + loss_out,
-        )
-        for i in range(rep)
-    ]
-    parts = rep_exchange(jnp.stack(shares, 0))
+    more = [bias_term.reshape(rep, 1, quarter)]
+    more += [jnp.broadcast_to(row[None], (rep,) + row.shape) for row in two_halves(loss_blk)]
+    more = [jnp.pad(row, ((0, 0), (0, 0), (0, lat - row.shape[2]))) for row in more]
+    more.append(jnp.zeros((rep, 13, lat), BF16))
+    parts = rep_exchange(jnp.concatenate([enc_term.reshape(rep, share, lat)] + more, 1))
     grad_enc = sum(part[:share].astype(F32) for part in parts)
     last = sum(part[share : share + 3, :quarter].astype(F32) for part in parts)
     loss = jnp.sum(last[1:3]) / (total_tokens * width * 2 * z_size)

time: 134 us -> 128 us (0.955)
  starting transfers between devices: 64.7 us -> 59.6 us
  waiting for transfers between devices: 36.8 us -> 39.1 us
  other arithmetic: 8.67 us -> 7.19 us
    ppermute x8, starting transfers between devices: 11.7 us -> 9.55 us  [blk_move(): return lax.ppermute(block, ('blk', 'core'), route)]
    concatenate x1 -> x0, other arithmetic: 1.92 us -> none  [local(): dec_own = jnp.concatenate([dec_weight, dead], 1)]
    ppermute x5, starting transfers between devices: 4.94 us -> 3.02 us  [swap_core(): return lax.ppermute(block, 'core', [(0, 1), (1, 0)])]
    all_to_all x1, waiting for transfers between devices: 9.21 us -> 7.41 us  [local(): lax.all_to_all((kept + got).reshape(z_size, piece, lat), 'z', 0, 0, tiled...]
    all_to_all x2, waiting for transfers between devices: 0.09 us -> 1.75 us  [exchange_z(): return lax.all_to_all(copies, 'z', 0, 0, tiled=True)]
    ppermute x5, waiting for transfers between devices: 2.07 us -> 3.7 us  [swap_core(): return lax.ppermute(block, 'core', [(0, 1), (1, 0)])]
  transfers between devices with their start and end apart: 27 -> 27, of which waited for: 15 -> 19; matrix products, arithmetic and copies ran while one was open for 11% -> 10% of each run, Pallas kernels for 4% -> 4%
where the time goes in v3:
time: 128 us; the launch traced here: 127 us
  starting transfers between devices  59.6 us (47%)
  waiting for transfers between devices  39.1 us (31%)
  local copies, waits for them, and re-layouts  8.78 us (7%)
  other arithmetic  7.19 us (6%)
  Pallas kernels  5.69 us (4%)
  matrix products  4.16 us (3%)
  between operations  3 us (2%)
    all_to_all x2, starting transfers between devices, exchange_z(): return lax.all_to_all(copies, 'z', 0, 0, tiled=True)  17.6 us
    ppermute x8, starting transfers between devices, from_ahead(): lax.ppermute(block, axis, [((i + distance) % size, i) for i in range(size)])  12.7 us
    ppermute x8, waiting for transfers between devices, blk_move(): return lax.ppermute(block, ('blk', 'core'), route)  11.3 us
    ppermute x8, starting transfers between devices, blk_move(): return lax.ppermute(block, ('blk', 'core'), route)  9.55 us
    ppermute x8, waiting for transfers between devices, from_ahead(): lax.ppermute(block, axis, [((i + distance) % size, i) for i in range(size)])  9.39 us
    all_to_all x1, starting transfers between devices, local(): lax.all_to_all((kept + got).reshape(z_size, piece, lat), 'z', 0, 0, tiled...  8.57 us
    all_to_all x1, waiting for transfers between devices, local(): lax.all_to_all((kept + got).reshape(z_size, piece, lat), 'z', 0, 0, tiled...  7.41 us
    all_to_all x1, starting transfers between devices, local(): arrived = lax.all_to_all(packet, 'z', 0, 0, tiled=True).astype(F32)  6.76 us
  transfers between devices with their start and end apart: 27, of which 19 were waited for; matrix products, arithmetic and copies ran while one was open for 10% of the time, Pallas kernels for 4%

profile of v3, /device:TPU:32, one launch (start us, length us, event | category | flops | bytes accessed | tf_op | source)
XLA Modules:
  0.0 127.5 jit_solution(10016070576179402281)
XLA Ops:
  0.7 3.1 %collective-permute-start.2 = (bf16[128,448]{0,1:T(8,128)(2,1)}, bf16[128,448]{0,1:T(8,128)(2,1)S(1)}, u32[]{:S(2)}, u32[]{:S(2)}) collective-permute-start(bf16[128,448]{0,1:T(8,128)(2,1)} %param.7), channel_id=1, source_target_pairs={{128,0},{192,64},{0,128},{64,192},{129,1},{193,65},{1,129},{65,193... | collective-permute-start | bytes 344072 | tf_op jit(solution)/shard_map/ppermute | solution.py:17
  3.8 1.1 collective-permute-start
  4.9 0.9 collective-permute-start.1
  5.8 0.7 convert_element_type.172
  6.7 0.9 constant_dynamic-update-slice_fusion.2
  8.0 1.9 %collective-permute-done = bf16[128,448]{0,1:T(8,128)(2,1)S(1)} collective-permute-done((bf16[128,448]{0,1:T(8,128)(2,1)}, bf16[128,448]{0,1:T(8,128)(2,1)S(1)}, u32[]{:S(2)}, u32[]{:S(2)}) %collective-permute-start) | collective-permute-done | bytes 114720 | tf_op jit(solution)/shard_map/ppermute | solution.py:27
  9.9 1.2 collective-permute-done.1
  11.6 1.9 %collective-permute-done.3 = f32[256,512]{1,0:T(8,128)S(1)} collective-permute-done((f32[256,512]{1,0:T(8,128)S(1)}, f32[256,512]{1,0:T(8,128)S(1)}, u32[]{:S(2)}, u32[]{:S(2)}) %collective-permute-start.3) | collective-permute-done | bytes 524320 | tf_op jit(solution)/shard_map/ppermute | solution.py:31
  13.5 1.1 convolution_add_fusion
  14.7 8.6 %all-to-all-start = ((f32[8,32,512]{2,1,0:T(8,128)}), f32[8,32,512]{2,1,0:T(8,128)S(1)}, u32[]{:S(2)}, u32[]{:S(2)}) async-start(f32[8,32,512]{2,1,0:T(8,128)} %bitcast), calls=%async_computation | async-start | bytes 1048576 | tf_op jit(solution)/shard_map/all_to_all | solution.py:139
  23.5 3.0 %collective-permute-start.7 = (bf16[512,464]{0,1:T(8,128)(2,1)}, bf16[512,464]{0,1:T(8,128)(2,1)}, u32[]{:S(2)}, u32[]{:S(2)}) collective-permute-start(bf16[512,464]{0,1:T(8,128)(2,1)} %get-tuple-element.21), channel_id=1, source_target_pairs={{0,192},{4,68},{64,0},{68,132},{128,64},{132,196},{192,128},{196,4... | collective-permute-start | bytes 1425416 | tf_op jit(solution)/shard_map/ppermute | solution.py:27
  26.5 5.7 %shard_map.102 = bf16[128,2048]{1,0:T(8,128)(2,1)} custom-call(s32[1]{0:T(128)} %bitcast.1.own_ref, s32[128,512]{1,0:T(8,128)} %picks_ref.1), custom_call_target="tpu_custom_call" | custom-call | flops 20000000 | bytes 1000000 | tf_op jit(solution)/shard_map/pallas_call | solution.py:82
  32.2 7.4 %all-to-all-done = f32[8,32,512]{2,1,0:T(8,128)S(1)} async-done(((f32[8,32,512]{2,1,0:T(8,128)}), f32[8,32,512]{2,1,0:T(8,128)S(1)}, u32[]{:S(2)}, u32[]{:S(2)}) %all-to-all-start) | async-done | bytes 524320 | tf_op jit(solution)/shard_map/all_to_all | solution.py:139
  40.3 0.7 broadcast_in_dim.22
  41.1 9.6 %all-to-all-start.1 = ((bf16[8,32,512]{2,1,0:T(8,128)(2,1)}), bf16[8,32,512]{2,1,0:T(8,128)(2,1)}, u32[]{:S(2)}, u32[]{:S(2)}) async-start(bf16[8,32,512]{2,1,0:T(8,128)(2,1)} %broadcast_in_dim.22), calls=%async_computation.1 | async-start | bytes 524288 | tf_op jit(solution)/shard_map/all_to_all | solution.py:51
  50.8 1.0 slice.174
  52.3 1.0 slice.173
  53.2 1.6 %collective-permute-start.8 = (bf16[512,224]{0,1:T(8,128)(2,1)S(1)}, bf16[512,224]{0,1:T(8,128)(2,1)S(1)}, u32[]{:S(2)}, u32[]{:S(2)}) collective-permute-start(bf16[512,224]{0,1:T(8,128)(2,1)S(1)} %slice.173), channel_id=1, source_target_pairs={{0,64},{4,196},{64,128},{68,4},{128,192},{132,68},{192,0},{196,132... | collective-permute-start | bytes 688136 | tf_op jit(solution)/shard_map/ppermute | solution.py:27
  54.9 1.1 constant_dynamic-update-slice_fusion.1
  56.0 1.1 constant_dynamic-update-slice_fusion
  57.1 4.6 %collective-permute-done.8 = bf16[512,224]{0,1:T(8,128)(2,1)S(1)} collective-permute-done((bf16[512,224]{0,1:T(8,128)(2,1)S(1)}, bf16[512,224]{0,1:T(8,128)(2,1)S(1)}, u32[]{:S(2)}, u32[]{:S(2)}) %collective-permute-start.8) | collective-permute-done | bytes 229408 | tf_op jit(solution)/shard_map/ppermute | solution.py:27
  62.5 1.0 fusion.40
  64.4 0.7 fusion.37
  66.8 0.8 collective-permute-done.10
  67.9 0.8 pad_maximum_fusion.2
  68.7 6.8 %all-to-all-start.2 = ((bf16[8,32,640]{2,1,0:T(8,128)(2,1)}), bf16[8,32,640]{2,1,0:T(8,128)(2,1)S(1)}, u32[]{:S(2)}, u32[]{:S(2)}) async-start(bf16[8,32,640]{2,1,0:T(8,128)(2,1)} %pad_maximum_fusion.2), calls=%async_computation.2 | async-start | bytes 655360 | tf_op jit(solution)/shard_map/all_to_all | solution.py:187
  76.5 1.8 %collective-permute-start.14 = (bf16[112,2048]{1,0:T(8,128)(2,1)S(1)}, bf16[112,2048]{1,0:T(8,128)(2,1)}, u32[]{:S(2)}, u32[]{:S(2)}) collective-permute-start(bf16[112,2048]{1,0:T(8,128)(2,1)S(1)} %get-tuple-element.40), channel_id=1, source_target_pairs={{3,0},{0,1},{1,2},{2,3},{7,4},{4,5},{5,6},{6,7},{11,8},{8,9},{9,10... | collective-permute-start | bytes 1376264 | tf_op jit(solution)/shard_map/ppermute | solution.py:17
  78.4 1.7 %collective-permute-start.15 = (bf16[112,2048]{1,0:T(8,128)(2,1)S(1)}, bf16[112,2048]{1,0:T(8,128)(2,1)}, u32[]{:S(2)}, u32[]{:S(2)}) collective-permute-start(bf16[112,2048]{1,0:T(8,128)(2,1)S(1)} %get-tuple-element.39), channel_id=1, source_target_pairs={{1,0},{2,1},{3,2},{0,3},{5,4},{6,5},{7,6},{4,7},{9,8},{10,9},{11,1... | collective-permute-start | bytes 1376264 | tf_op jit(solution)/shard_map/ppermute | solution.py:17
  80.0 2.0 %collective-permute-start.16 = (bf16[112,2048]{1,0:T(8,128)(2,1)S(1)}, bf16[112,2048]{1,0:T(8,128)(2,1)}, u32[]{:S(2)}, u32[]{:S(2)}) collective-permute-start(bf16[112,2048]{1,0:T(8,128)(2,1)S(1)} %get-tuple-element.38), channel_id=1, source_target_pairs={{2,0},{3,1},{0,2},{1,3},{6,4},{7,5},{4,6},{5,7},{10,8},{11,9},{8,1... | collective-permute-start | bytes 1376264 | tf_op jit(solution)/shard_map/ppermute | solution.py:17
  82.0 5.6 %all-to-all-done.2 = bf16[8,32,640]{2,1,0:T(8,128)(2,1)S(1)} async-done(((bf16[8,32,640]{2,1,0:T(8,128)(2,1)}), bf16[8,32,640]{2,1,0:T(8,128)(2,1)S(1)}, u32[]{:S(2)}, u32[]{:S(2)}) %all-to-all-start.2) | async-done | bytes 327712 | tf_op jit(solution)/shard_map/all_to_all | solution.py:187
  88.9 0.7 broadcast_in_dim.25
  89.6 8.0 %all-to-all-start.3 = ((bf16[8,32,512]{2,1,0:T(8,128)(2,1)}), bf16[8,32,512]{2,1,0:T(8,128)(2,1)S(1)}, u32[]{:S(2)}, u32[]{:S(2)}) async-start(bf16[8,32,512]{2,1,0:T(8,128)(2,1)} %broadcast_in_dim.25), calls=%async_computation.3 | async-start | bytes 524288 | tf_op jit(solution)/shard_map/all_to_all | solution.py:51
  97.6 1.7 %collective-permute-done.15 = bf16[112,2048]{1,0:T(8,128)(2,1)} collective-permute-done((bf16[112,2048]{1,0:T(8,128)(2,1)S(1)}, bf16[112,2048]{1,0:T(8,128)(2,1)}, u32[]{:S(2)}, u32[]{:S(2)}) %collective-permute-start.15) | collective-permute-done | bytes 458784 | tf_op jit(solution)/shard_map/ppermute | solution.py:17
  99.3 1.9 %collective-permute-done.16 = bf16[112,2048]{1,0:T(8,128)(2,1)} collective-permute-done((bf16[112,2048]{1,0:T(8,128)(2,1)S(1)}, bf16[112,2048]{1,0:T(8,128)(2,1)}, u32[]{:S(2)}, u32[]{:S(2)}) %collective-permute-start.16) | collective-permute-done | bytes 458784 | tf_op jit(solution)/shard_map/ppermute | solution.py:17
  101.2 1.6 %add_convert_fusion = bf16[112,2048]{1,0:T(8,128)(2,1)S(1)} fusion(bf16[112,2048]{1,0:T(8,128)(2,1)} %collective-permute-done.16, bf16[112,2048]{1,0:T(8,128)(2,1)} %collective-permute-done.15, bf16[112,2048]{1,0:T(8,128)(2,1)} %collective-permute-done.14, bf16[112,2048]{1,0:T(8,128)(2,1)S(1)} %get-tuple-element.25), kind=kLoop, calls=%fused_computation.8 | loop fusion | flops 1835008 | bytes 2293760 | tf_op jit(solution)/shard_map/convert_element_type | solution.py:210
  102.9 1.1 collective-permute-start.17
  104.0 1.0 collective-permute-start.18
  105.6 1.2 all-to-all-done.3
  106.8 2.5 %collective-permute-start.12 = (bf16[256,512]{1,0:T(8,128)(2,1)S(1)}, bf16[256,512]{1,0:T(8,128)(2,1)S(1)}, u32[]{:S(2)}, u32[]{:S(2)}) collective-permute-start(bf16[256,512]{1,0:T(8,128)(2,1)S(1)} %bitcast.57), channel_id=1, source_target_pairs={{0,4},{4,0},{1,5},{5,1},{2,6},{6,2},{3,7},{7,3},{8,12},{12,8},{9,1... | collective-permute-start | bytes 786440 | tf_op jit(solution)/shard_map/ppermute | solution.py:31
  109.3 1.4 %collective-permute-done.17 = bf16[128,512]{1,0:T(8,128)(2,1)S(1)} collective-permute-done((bf16[128,512]{1,0:T(8,128)(2,1)S(1)}, bf16[128,512]{1,0:T(8,128)(2,1)S(1)}, u32[]{:S(2)}, u32[]{:S(2)}) %collective-permute-start.17) | collective-permute-done | bytes 131104 | tf_op jit(solution)/shard_map/ppermute | solution.py:27
  110.6 2.3 %collective-permute-done.18 = bf16[128,512]{1,0:T(8,128)(2,1)S(1)} collective-permute-done((bf16[128,512]{1,0:T(8,128)(2,1)S(1)}, bf16[128,512]{1,0:T(8,128)(2,1)S(1)}, u32[]{:S(2)}, u32[]{:S(2)}) %collective-permute-start.18) | collective-permute-done | bytes 131104 | tf_op jit(solution)/shard_map/ppermute | solution.py:27
  114.0 1.3 collective-permute-start.20
  115.3 2.1 %collective-permute-start.21 = (bf16[128,512]{1,0:T(8,128)(2,1)S(1)}, bf16[128,512]{1,0:T(8,128)(2,1)S(1)}, u32[]{:S(2)}, u32[]{:S(2)}) collective-permute-start(bf16[128,512]{1,0:T(8,128)(2,1)S(1)} %get-tuple-element.47), channel_id=1, source_target_pairs={{1,0},{2,1},{3,2},{0,3},{5,4},{6,5},{7,6},{4,7},{9,8},{10,9},{11,1... | collective-permute-start | bytes 393224 | tf_op jit(solution)/shard_map/ppermute | solution.py:17
  117.6 0.7 add_bitcast_fusion
  118.3 2.8 %collective-permute-done.20 = bf16[128,512]{1,0:T(8,128)(2,1)S(1)} collective-permute-done((bf16[128,512]{1,0:T(8,128)(2,1)S(1)}, bf16[128,512]{1,0:T(8,128)(2,1)S(1)}, u32[]{:S(2)}, u32[]{:S(2)}) %collective-permute-start.20) | collective-permute-done | bytes 131104 | tf_op jit(solution)/shard_map/ppermute | solution.py:17
  121.2 0.9 collective-permute-done.21
  122.0 1.8 %collective-permute-done.22 = bf16[128,512]{1,0:T(8,128)(2,1)S(1)} collective-permute-done((bf16[128,512]{1,0:T(8,128)(2,1)S(1)}, bf16[128,512]{1,0:T(8,128)(2,1)S(1)}, u32[]{:S(2)}, u32[]{:S(2)}) %collective-permute-start.22) | collective-permute-done | bytes 131104 | tf_op jit(solution)/shard_map/ppermute | solution.py:17
  125.6 0.8 fusion.23
  (108 shorter events, 11.6 us)
Async XLA Ops:
  0.6 10.6 %copy-start = (bf16[448,512]{1,0:T(8,128)(2,1)S(1)}, bf16[448,512]{1,0:T(8,128)(2,1)}, u32[]{:S(2)}) copy-start(bf16[448,512]{1,0:T(8,128)(2,1)} %param.9) | copy-start | bytes 1376260
  0.6 6.1 %copy-start.10 = (bf16[512,448]{0,1:T(8,128)(2,1)S(1)}, bf16[512,448]{0,1:T(8,128)(2,1)}, u32[]{:S(2)}) copy-start(bf16[512,448]{0,1:T(8,128)(2,1)} %param.11) | copy-start | bytes 1376260
  0.7 7.4 %collective-permute-start.2 = (bf16[128,448]{0,1:T(8,128)(2,1)}, bf16[128,448]{0,1:T(8,128)(2,1)S(1)}, u32[]{:S(2)}, u32[]{:S(2)}) collective-permute-start(bf16[128,448]{0,1:T(8,128)(2,1)} %param.7), channel_id=1, source_target_pairs={{128,0},{192,64},{0,128},{64,192},{129,1},{193,65},{1,129},{65,193... | collective-permute-start | bytes 344072 | tf_op jit(solution)/shard_map/ppermute | solution.py:17
  3.8 6.1 %collective-permute-start = (bf16[128,448]{0,1:T(8,128)(2,1)}, bf16[128,448]{0,1:T(8,128)(2,1)S(1)}, u32[]{:S(2)}, u32[]{:S(2)}) collective-permute-start(bf16[128,448]{0,1:T(8,128)(2,1)} %param.7), channel_id=1, source_target_pairs={{0,192},{4,68},{64,0},{68,132},{128,64},{132,196},{192,128},{196,4... | collective-permute-start | bytes 344072 | tf_op jit(solution)/shard_map/ppermute | solution.py:27
  4.9 6.2 %collective-permute-start.1 = (bf16[128,448]{0,1:T(8,128)(2,1)}, bf16[128,448]{0,1:T(8,128)(2,1)S(1)}, u32[]{:S(2)}, u32[]{:S(2)}) collective-permute-start(bf16[128,448]{0,1:T(8,128)(2,1)} %param.7), channel_id=1, source_target_pairs={{0,64},{4,196},{64,128},{68,4},{128,192},{132,68},{192,0},{196,132... | collective-permute-start | bytes 344072 | tf_op jit(solution)/shard_map/ppermute | solution.py:27
  6.5 1.2 copy-start.11
  11.5 28.1 %copy-start.13 = (f32[512]{0:T(512)S(1)}, f32[512]{0:T(512)}, u32[]{:S(2)}) copy-start(f32[512]{0:T(512)} %param.10) | copy-start | bytes 6148
  11.5 2.0 %collective-permute-start.3 = (f32[256,512]{1,0:T(8,128)S(1)}, f32[256,512]{1,0:T(8,128)S(1)}, u32[]{:S(2)}, u32[]{:S(2)}) collective-permute-start(f32[256,512]{1,0:T(8,128)S(1)} %fusion.19), channel_id=1, source_target_pairs={{0,4},{4,0},{1,5},{5,1},{2,6},{6,2},{3,7},{7,3},{8,12},{12,8},{9,1... | collective-permute-start | bytes 1572872 | tf_op jit(solution)/shard_map/ppermute | solution.py:31
  14.7 24.9 %all-to-all-start = ((f32[8,32,512]{2,1,0:T(8,128)}), f32[8,32,512]{2,1,0:T(8,128)S(1)}, u32[]{:S(2)}, u32[]{:S(2)}) async-start(f32[8,32,512]{2,1,0:T(8,128)} %bitcast), calls=%async_computation | async-start | bytes 1048576 | tf_op jit(solution)/shard_map/all_to_all | solution.py:139
  23.2 27.5 %collective-permute-start.6 = (bf16[512,464]{0,1:T(8,128)(2,1)}, bf16[512,464]{0,1:T(8,128)(2,1)}, u32[]{:S(2)}, u32[]{:S(2)}) collective-permute-start(bf16[512,464]{0,1:T(8,128)(2,1)} %get-tuple-element.21), channel_id=1, source_target_pairs={{0,64},{4,196},{64,128},{68,4},{128,192},{132,68},{192,0},{196,132... | collective-permute-start | bytes 1425416 | tf_op jit(solution)/shard_map/ppermute | solution.py:27
  23.5 27.3 %collective-permute-start.7 = (bf16[512,464]{0,1:T(8,128)(2,1)}, bf16[512,464]{0,1:T(8,128)(2,1)}, u32[]{:S(2)}, u32[]{:S(2)}) collective-permute-start(bf16[512,464]{0,1:T(8,128)(2,1)} %get-tuple-element.21), channel_id=1, source_target_pairs={{0,192},{4,68},{64,0},{68,132},{128,64},{132,196},{192,128},{196,4... | collective-permute-start | bytes 1425416 | tf_op jit(solution)/shard_map/ppermute | solution.py:27
  39.7 0.7 collective-permute-start.4
  41.1 21.3 %all-to-all-start.1 = ((bf16[8,32,512]{2,1,0:T(8,128)(2,1)}), bf16[8,32,512]{2,1,0:T(8,128)(2,1)}, u32[]{:S(2)}, u32[]{:S(2)}) async-start(bf16[8,32,512]{2,1,0:T(8,128)(2,1)} %broadcast_in_dim.22), calls=%async_computation.1 | async-start | bytes 524288 | tf_op jit(solution)/shard_map/all_to_all | solution.py:51
  51.7 10.0 %collective-permute-start.9 = (bf16[512,240]{0,1:T(8,128)(2,1)S(1)}, bf16[512,240]{0,1:T(8,128)(2,1)S(1)}, u32[]{:S(2)}, u32[]{:S(2)}) collective-permute-start(bf16[512,240]{0,1:T(8,128)(2,1)S(1)} %slice.174), channel_id=1, source_target_pairs={{0,192},{4,68},{64,0},{68,132},{128,64},{132,196},{192,128},{196,4... | collective-permute-start | bytes 737288 | tf_op jit(solution)/shard_map/ppermute | solution.py:27
  53.2 8.5 %collective-permute-start.8 = (bf16[512,224]{0,1:T(8,128)(2,1)S(1)}, bf16[512,224]{0,1:T(8,128)(2,1)S(1)}, u32[]{:S(2)}, u32[]{:S(2)}) collective-permute-start(bf16[512,224]{0,1:T(8,128)(2,1)S(1)} %slice.173), channel_id=1, source_target_pairs={{0,64},{4,196},{64,128},{68,4},{128,192},{132,68},{192,0},{196,132... | collective-permute-start | bytes 688136 | tf_op jit(solution)/shard_map/ppermute | solution.py:27
  54.9 9.2 %copy-start.1 = (bf16[128,2048]{1,0:T(8,128)(2,1)S(1)}, bf16[128,2048]{1,0:T(8,128)(2,1)}, u32[]{:S(2)}) copy-start(bf16[128,2048]{1,0:T(8,128)(2,1)} %shard_map.102) | copy-start | bytes 1572868
  62.3 1.7 %collective-permute-start.5 = (bf16[2,128,512]{2,1,0:T(8,128)(2,1)}, bf16[2,128,512]{2,1,0:T(8,128)(2,1)S(1)}, u32[]{:S(2)}, u32[]{:S(2)}) collective-permute-start(bf16[2,128,512]{2,1,0:T(8,128)(2,1)} %bitcast.4), channel_id=1, source_target_pairs={{0,4},{4,0},{1,5},{5,1},{2,6},{6,2},{3,7},{7,3},{8,12},{12,8},{9,1... | collective-permute-start | bytes 786440 | tf_op jit(solution)/shard_map/ppermute | solution.py:31
  63.5 1.6 %copy-start.2 = (bf16[4,32,512]{2,1,0:T(8,128)(2,1)}, bf16[4,32,512]{2,1,0:T(8,128)(2,1)S(1)}, u32[]{:S(2)}) copy-start(bf16[4,32,512]{2,1,0:T(8,128)(2,1)S(1)} %get-tuple-element.57) | copy-start | bytes 393220
  64.1 1.0 copy-start.4
  64.1 1.0 copy-start.6
  64.3 0.8 copy-start.8
  64.3 1.0 copy-start.12
  66.0 1.6 %collective-permute-start.10 = (bf16[128,1024]{1,0:T(8,128)(2,1)S(1)}, bf16[128,1024]{1,0:T(8,128)(2,1)S(1)}, u32[]{:S(2)}, u32[]{:S(2)}) collective-permute-start(bf16[128,1024]{1,0:T(8,128)(2,1)S(1)} %fusion.5), channel_id=1, source_target_pairs={{0,4},{4,0},{1,5},{5,1},{2,6},{6,2},{3,7},{7,3},{8,12},{12,8},{9,1... | collective-permute-start | bytes 786440 | tf_op jit(solution)/shard_map/ppermute | solution.py:31
  67.8 7.7 %copy-start.3 = (bf16[4,32,512]{2,1,0:T(8,128)(2,1)S(1)}, bf16[4,32,512]{2,1,0:T(8,128)(2,1)}, u32[]{:S(2)}) copy-start(bf16[4,32,512]{2,1,0:T(8,128)(2,1)} %copy-done.2) | copy-start | bytes 393220
  67.8 7.7 %copy-start.5 = (bf16[128,512]{1,0:T(8,128)(2,1)S(1)}, bf16[128,512]{1,0:T(8,128)(2,1)}, u32[]{:S(2)}) copy-start(bf16[128,512]{1,0:T(8,128)(2,1)} %copy-done.4) | copy-start | bytes 393220
  67.8 7.7 %copy-start.7 = (bf16[128,512]{1,0:T(8,128)(2,1)S(1)}, bf16[128,512]{1,0:T(8,128)(2,1)}, u32[]{:S(2)}) copy-start(bf16[128,512]{1,0:T(8,128)(2,1)} %copy-done.6) | copy-start | bytes 393220
  67.8 7.7 %copy-start.9 = (bf16[128,2048]{1,0:T(8,128)(2,1)S(1)}, bf16[128,2048]{1,0:T(8,128)(2,1)}, u32[]{:S(2)}) copy-start(bf16[128,2048]{1,0:T(8,128)(2,1)} %copy-done.8) | copy-start | bytes 1572868
  68.7 18.9 %all-to-all-start.2 = ((bf16[8,32,640]{2,1,0:T(8,128)(2,1)}), bf16[8,32,640]{2,1,0:T(8,128)(2,1)S(1)}, u32[]{:S(2)}, u32[]{:S(2)}) async-start(bf16[8,32,640]{2,1,0:T(8,128)(2,1)} %pad_maximum_fusion.2), calls=%async_computation.2 | async-start | bytes 655360 | tf_op jit(solution)/shard_map/all_to_all | solution.py:187
  76.5 21.1 %collective-permute-start.14 = (bf16[112,2048]{1,0:T(8,128)(2,1)S(1)}, bf16[112,2048]{1,0:T(8,128)(2,1)}, u32[]{:S(2)}, u32[]{:S(2)}) collective-permute-start(bf16[112,2048]{1,0:T(8,128)(2,1)S(1)} %get-tuple-element.40), channel_id=1, source_target_pairs={{3,0},{0,1},{1,2},{2,3},{7,4},{4,5},{5,6},{6,7},{11,8},{8,9},{9,10... | collective-permute-start | bytes 1376264 | tf_op jit(solution)/shard_map/ppermute | solution.py:17
  78.4 20.9 %collective-permute-start.15 = (bf16[112,2048]{1,0:T(8,128)(2,1)S(1)}, bf16[112,2048]{1,0:T(8,128)(2,1)}, u32[]{:S(2)}, u32[]{:S(2)}) collective-permute-start(bf16[112,2048]{1,0:T(8,128)(2,1)S(1)} %get-tuple-element.39), channel_id=1, source_target_pairs={{1,0},{2,1},{3,2},{0,3},{5,4},{6,5},{7,6},{4,7},{9,8},{10,9},{11,1... | collective-permute-start | bytes 1376264 | tf_op jit(solution)/shard_map/ppermute | solution.py:17
  80.0 21.2 %collective-permute-start.16 = (bf16[112,2048]{1,0:T(8,128)(2,1)S(1)}, bf16[112,2048]{1,0:T(8,128)(2,1)}, u32[]{:S(2)}, u32[]{:S(2)}) collective-permute-start(bf16[112,2048]{1,0:T(8,128)(2,1)S(1)} %get-tuple-element.38), channel_id=1, source_target_pairs={{2,0},{3,1},{0,2},{1,3},{6,4},{7,5},{4,6},{5,7},{10,8},{11,9},{8,1... | collective-permute-start | bytes 1376264 | tf_op jit(solution)/shard_map/ppermute | solution.py:17
  87.6 1.2 collective-permute-start.13
  87.8 1.1 collective-permute-start.11
  89.6 17.2 %all-to-all-start.3 = ((bf16[8,32,512]{2,1,0:T(8,128)(2,1)}), bf16[8,32,512]{2,1,0:T(8,128)(2,1)S(1)}, u32[]{:S(2)}, u32[]{:S(2)}) async-start(bf16[8,32,512]{2,1,0:T(8,128)(2,1)} %broadcast_in_dim.25), calls=%async_computation.3 | async-start | bytes 524288 | tf_op jit(solution)/shard_map/all_to_all | solution.py:51
  102.9 7.7 %collective-permute-start.17 = (bf16[128,512]{1,0:T(8,128)(2,1)S(1)}, bf16[128,512]{1,0:T(8,128)(2,1)S(1)}, u32[]{:S(2)}, u32[]{:S(2)}) collective-permute-start(bf16[128,512]{1,0:T(8,128)(2,1)S(1)} %get-tuple-element.61), channel_id=1, source_target_pairs={{0,192},{4,68},{64,0},{68,132},{128,64},{132,196},{192,128},{196,4... | collective-permute-start | bytes 393224 | tf_op jit(solution)/shard_map/ppermute | solution.py:27
  104.0 8.8 %collective-permute-start.18 = (bf16[128,512]{1,0:T(8,128)(2,1)S(1)}, bf16[128,512]{1,0:T(8,128)(2,1)S(1)}, u32[]{:S(2)}, u32[]{:S(2)}) collective-permute-start(bf16[128,512]{1,0:T(8,128)(2,1)S(1)} %get-tuple-element.62), channel_id=1, source_target_pairs={{0,64},{4,196},{64,128},{68,4},{128,192},{132,68},{192,0},{196,132... | collective-permute-start | bytes 393224 | tf_op jit(solution)/shard_map/ppermute | solution.py:27
  105.0 7.9 %collective-permute-start.19 = (bf16[128,512]{1,0:T(8,128)(2,1)S(1)}, bf16[128,512]{1,0:T(8,128)(2,1)S(1)}, u32[]{:S(2)}, u32[]{:S(2)}) collective-permute-start(bf16[128,512]{1,0:T(8,128)(2,1)S(1)} %get-tuple-element.60), channel_id=1, source_target_pairs={{128,0},{192,64},{0,128},{64,192},{129,1},{193,65},{1,129},{65,193... | collective-permute-start | bytes 393224 | tf_op jit(solution)/shard_map/ppermute | solution.py:17
  106.8 6.2 %collective-permute-start.12 = (bf16[256,512]{1,0:T(8,128)(2,1)S(1)}, bf16[256,512]{1,0:T(8,128)(2,1)S(1)}, u32[]{:S(2)}, u32[]{:S(2)}) collective-permute-start(bf16[256,512]{1,0:T(8,128)(2,1)S(1)} %bitcast.57), channel_id=1, source_target_pairs={{0,4},{4,0},{1,5},{5,1},{2,6},{6,2},{3,7},{7,3},{8,12},{12,8},{9,1... | collective-permute-start | bytes 786440 | tf_op jit(solution)/shard_map/ppermute | solution.py:31
  114.0 7.1 %collective-permute-start.20 = (bf16[128,512]{1,0:T(8,128)(2,1)S(1)}, bf16[128,512]{1,0:T(8,128)(2,1)S(1)}, u32[]{:S(2)}, u32[]{:S(2)}) collective-permute-start(bf16[128,512]{1,0:T(8,128)(2,1)S(1)} %get-tuple-element.48), channel_id=1, source_target_pairs={{3,0},{0,1},{1,2},{2,3},{7,4},{4,5},{5,6},{6,7},{11,8},{8,9},{9,10... | collective-permute-start | bytes 393224 | tf_op jit(solution)/shard_map/ppermute | solution.py:17
  115.3 6.8 %collective-permute-start.21 = (bf16[128,512]{1,0:T(8,128)(2,1)S(1)}, bf16[128,512]{1,0:T(8,128)(2,1)S(1)}, u32[]{:S(2)}, u32[]{:S(2)}) collective-permute-start(bf16[128,512]{1,0:T(8,128)(2,1)S(1)} %get-tuple-element.47), channel_id=1, source_target_pairs={{1,0},{2,1},{3,2},{0,3},{5,4},{6,5},{7,6},{4,7},{9,8},{10,9},{11,1... | collective-permute-start | bytes 393224 | tf_op jit(solution)/shard_map/ppermute | solution.py:17
  117.3 6.5 %collective-permute-start.22 = (bf16[128,512]{1,0:T(8,128)(2,1)S(1)}, bf16[128,512]{1,0:T(8,128)(2,1)S(1)}, u32[]{:S(2)}, u32[]{:S(2)}) collective-permute-start(bf16[128,512]{1,0:T(8,128)(2,1)S(1)} %get-tuple-element.46), channel_id=1, source_target_pairs={{2,0},{3,1},{0,2},{1,3},{6,4},{7,5},{4,6},{5,7},{10,8},{11,9},{8,1... | collective-permute-start | bytes 393224 | tf_op jit(solution)/shard_map/ppermute | solution.py:17

commit v4 on v3

--- a/solution.py
+++ b/solution.py
@@ -103,7 +103,7 @@
 def with_rows(body, rows):
     width = body.shape[1]
     rows = [jnp.pad(row, ((0, 0), (0, width - row.shape[1]))) for row in rows]
-    filler = jnp.zeros((16 - len(rows), width), BF16)
+    filler = jnp.zeros((8 - len(rows), width), BF16)
     return jnp.concatenate([body] + rows + [filler], 0)
 
 
@@ -126,6 +126,7 @@
 
     x_1, x_3 = blk_move(inputs, 1, -1), blk_move(inputs, 3, -1)
     x_2 = from_ahead(inputs, "blk", 2)
+    enc_far = swap_core(enc_weight)
     dead = jnp.broadcast_to(dead_mask.astype(BF16)[:, None], (lat, 16))
     dec_own = jnp.concatenate([dec_weight, dead], 1)
     dec_sent, x_2 = lax.optimization_barrier((dec_own, x_2))
@@ -134,15 +135,19 @@
     half = dec_own.shape[1] // 32 * 16
     picked = picked_latents(aux_picks, blk_at + 2 * core, lat_all)
 
-    got = swap_core(jnp.dot(x_all[2 * rows :], enc_weight, preferred_element_type=F32))
-    kept = jnp.dot(x_all[: 2 * rows], enc_weight, preferred_element_type=F32)
-    parts = lax.all_to_all((kept + got).reshape(z_size, piece, lat), "z", 0, 0, tiled=True)
+    x_far = swap_core(x_all[2 * rows :])
+    summed = jnp.dot(x_all[: 2 * rows], enc_weight, preferred_element_type=F32)
+    summed = summed + jnp.dot(x_far, enc_far, preferred_element_type=F32)
+    parts = exchange_z(summed.reshape(z_size, piece, lat))
     preact = jnp.sum(parts, axis=0) + enc_bias[None, :]
     lat_piece = jnp.maximum(preact, 0.0).astype(BF16)
     lat_piece, picked = lax.optimization_barrier((lat_piece, picked))
     dec_1, dec_3 = after((dec_1, dec_3), lat_piece)
-    dec_2 = [blk_move(dec_1[:, :half], 1, 1), blk_move(dec_3[:, half:], 3, 1)]
     lat_piece = shift_pieces(lat_piece, 1)
+    lat_piece, passed_1, passed_3 = lax.optimization_barrier(
+        (lat_piece, dec_1[:, :half], dec_3[:, half:])
+    )
+    dec_2 = [blk_move(passed_1, 1, 1), blk_move(passed_3, 3, 1)]
     dec_all = in_slots(dec_own, dec_1, jnp.concatenate(dec_2, 1), dec_3)
     gate = picked * dec_all[:, width][None, :]
 
@@ -205,8 +210,9 @@
     grad_piece = jnp.where(lat_piece > 0, arrived[:, :lat], 0.0).astype(BF16)
     loss_width = arrived[0:1, lat:] + arrived[1:2, lat:]
     grad_piece = shift_pieces(grad_piece, -1)
+    grad_copies = z_copies(grad_piece)
+    loss_width = after(loss_width, grad_copies)
     loss_width = loss_width + swap_core(loss_width)
-    grad_copies = z_copies(grad_piece)
     dec_sum = sum(part.astype(F32) for part in after(dec_parts, grad_copies)).astype(BF16)
 
     loss_out = two_halves(loss_width)
@@ -236,7 +242,7 @@
     more = [bias_term.reshape(rep, 1, quarter)]
     more += [jnp.broadcast_to(row[None], (rep,) + row.shape) for row in two_halves(loss_blk)]
     more = [jnp.pad(row, ((0, 0), (0, 0), (0, lat - row.shape[2]))) for row in more]
-    more.append(jnp.zeros((rep, 13, lat), BF16))
+    more.append(jnp.zeros((rep, 5, lat), BF16))
     parts = rep_exchange(jnp.concatenate([enc_term.reshape(rep, share, lat)] + more, 1))
     grad_enc = sum(part[:share].astype(F32) for part in parts)
     last = sum(part[share : share + 3, :quarter].astype(F32) for part in parts)

time: 128 us -> 127 us (level); the launches traced: 127 us -> 125 us
  starting transfers between devices: 59.6 us -> 57.1 us
    all_to_all x2 -> x3, waiting for transfers between devices: 1.75 us -> 11.5 us  [exchange_z(): return lax.all_to_all(copies, 'z', 0, 0, tiled=True)]
    all_to_all x1 -> x0, starting transfers between devices: 8.57 us -> none  [local(): lax.all_to_all((kept + got).reshape(z_size, piece, lat), 'z', 0, 0, tiled...]
    all_to_all x1 -> x0, waiting for transfers between devices: 7.41 us -> none  [local(): lax.all_to_all((kept + got).reshape(z_size, piece, lat), 'z', 0, 0, tiled...]
    all_to_all x2 -> x3, starting transfers between devices: 17.6 us -> 24.2 us  [exchange_z(): return lax.all_to_all(copies, 'z', 0, 0, tiled=True)]
    ppermute x8, waiting for transfers between devices: 9.39 us -> 6.96 us  [from_ahead(): lax.ppermute(block, axis, [((i + distance) % size, i) for i in range(size)])]
    ppermute x8, waiting for transfers between devices: 11.3 us -> 12.5 us  [blk_move(): return lax.ppermute(block, ('blk', 'core'), route)]
    ppermute x5 -> x6, starting transfers between devices: 3.02 us -> 3.9 us  [swap_core(): return lax.ppermute(block, 'core', [(0, 1), (1, 0)])]
    ppermute x5 -> x6, waiting for transfers between devices: 3.7 us -> 2.88 us  [swap_core(): return lax.ppermute(block, 'core', [(0, 1), (1, 0)])]
  transfers between devices with their start and end apart: 27 -> 28, of which waited for: 19 -> 16; matrix products, arithmetic and copies ran while one was open for 10% -> 9% of each run, Pallas kernels for 4% -> 5%
where the time goes in v4:
time: 127 us; the launch traced here: 125 us
  starting transfers between devices  57.1 us (45%)
  waiting for transfers between devices  39.7 us (31%)
  local copies, waits for them, and re-layouts  8.04 us (6%)
  other arithmetic  7.19 us (6%)
  Pallas kernels  5.69 us (4%)
  matrix products  4.19 us (3%)
  between operations  2.92 us (2%)
    all_to_all x3, starting transfers between devices, exchange_z(): return lax.all_to_all(copies, 'z', 0, 0, tiled=True)  24.2 us
    ppermute x8, waiting for transfers between devices, blk_move(): return lax.ppermute(block, ('blk', 'core'), route)  12.5 us
    ppermute x8, starting transfers between devices, from_ahead(): lax.ppermute(block, axis, [((i + distance) % size, i) for i in range(size)])  12.3 us
    all_to_all x3, waiting for transfers between devices, exchange_z(): return lax.all_to_all(copies, 'z', 0, 0, tiled=True)  11.5 us
    ppermute x8, starting transfers between devices, blk_move(): return lax.ppermute(block, ('blk', 'core'), route)  9.4 us
    ppermute x8, waiting for transfers between devices, from_ahead(): lax.ppermute(block, axis, [((i + distance) % size, i) for i in range(size)])  6.96 us
    all_to_all x1, starting transfers between devices, local(): arrived = lax.all_to_all(packet, 'z', 0, 0, tiled=True).astype(F32)  5.91 us
    all_to_all x1, waiting for transfers between devices, local(): arrived = lax.all_to_all(packet, 'z', 0, 0, tiled=True).astype(F32)  5.79 us
  transfers between devices with their start and end apart: 28, of which 16 were waited for; matrix products, arithmetic and copies ran while one was open for 9% of the time, Pallas kernels for 5%

profile of v4, /device:TPU:32, one launch (start us, length us, event | category | flops | bytes accessed | tf_op | source)
XLA Modules:
  0.0 124.8 jit_solution(15590668757744285774)
XLA Ops:
  0.6 3.1 %collective-permute-start.2 = (bf16[128,448]{0,1:T(8,128)(2,1)}, bf16[128,448]{0,1:T(8,128)(2,1)S(1)}, u32[]{:S(2)}, u32[]{:S(2)}) collective-permute-start(bf16[128,448]{0,1:T(8,128)(2,1)} %param.7), channel_id=1, source_target_pairs={{128,0},{192,64},{0,128},{64,192},{129,1},{193,65},{1,129},{65,193... | collective-permute-start | bytes 344072 | tf_op jit(solution)/shard_map/ppermute | solution.py:17
  3.8 1.1 collective-permute-start
  4.9 0.9 collective-permute-start.1
  6.0 0.7 convert_element_type.172
  6.9 0.9 constant_dynamic-update-slice_fusion.2
  8.0 1.9 %collective-permute-done = bf16[128,448]{0,1:T(8,128)(2,1)S(1)} collective-permute-done((bf16[128,448]{0,1:T(8,128)(2,1)}, bf16[128,448]{0,1:T(8,128)(2,1)S(1)}, u32[]{:S(2)}, u32[]{:S(2)}) %collective-permute-start) | collective-permute-done | bytes 114720 | tf_op jit(solution)/shard_map/ppermute | solution.py:27
  9.9 1.2 collective-permute-done.1
  11.3 1.5 %collective-permute-done.3 = bf16[256,448]{0,1:T(8,128)(2,1)S(1)} collective-permute-done((bf16[256,448]{0,1:T(8,128)(2,1)S(1)}, bf16[256,448]{0,1:T(8,128)(2,1)S(1)}, u32[]{:S(2)}, u32[]{:S(2)}) %collective-permute-start.3) | collective-permute-done | bytes 229408 | tf_op jit(solution)/shard_map/ppermute | solution.py:31
  13.1 1.1 convolution_add_fusion
  14.3 8.6 %all-to-all-start = ((f32[8,32,512]{2,1,0:T(8,128)}), f32[8,32,512]{2,1,0:T(8,128)S(1)}, u32[]{:S(2)}, u32[]{:S(2)}) async-start(f32[8,32,512]{2,1,0:T(8,128)} %bitcast), calls=%async_computation | async-start | bytes 1048576 | tf_op jit(solution)/shard_map/all_to_all | solution.py:51
  23.1 3.0 %collective-permute-start.7 = (bf16[512,464]{0,1:T(8,128)(2,1)}, bf16[512,464]{0,1:T(8,128)(2,1)S(1)}, u32[]{:S(2)}, u32[]{:S(2)}) collective-permute-start(bf16[512,464]{0,1:T(8,128)(2,1)} %get-tuple-element.24), channel_id=1, source_target_pairs={{0,192},{4,68},{64,0},{68,132},{128,64},{132,196},{192,128},{196,4... | collective-permute-start | bytes 1425416 | tf_op jit(solution)/shard_map/ppermute | solution.py:27
  26.1 5.7 %shard_map.102 = bf16[128,2048]{1,0:T(8,128)(2,1)} custom-call(s32[1]{0:T(128)} %bitcast.1.own_ref, s32[128,512]{1,0:T(8,128)} %picks_ref.1), custom_call_target="tpu_custom_call" | custom-call | flops 20000000 | bytes 1000000 | tf_op jit(solution)/shard_map/pallas_call | solution.py:82
  31.8 7.4 %all-to-all-done = f32[8,32,512]{2,1,0:T(8,128)S(1)} async-done(((f32[8,32,512]{2,1,0:T(8,128)}), f32[8,32,512]{2,1,0:T(8,128)S(1)}, u32[]{:S(2)}, u32[]{:S(2)}) %all-to-all-start) | async-done | bytes 524320 | tf_op jit(solution)/shard_map/all_to_all | solution.py:51
  39.3 0.7 collective-permute-start.5
  40.0 0.7 slice.170
  40.7 1.6 %slice.169 = bf16[512,224]{0,1:T(8,128)(2,1)} slice(bf16[512,464]{0,1:T(8,128)(2,1)} %collective-permute-done.6), slice={[0:512], [0:224]} | slice | bytes 458752 | tf_op jit(solution)/shard_map/slice | solution.py:148
  42.3 0.7 broadcast_in_dim.22
  43.1 7.2 %all-to-all-start.1 = ((bf16[8,32,512]{2,1,0:T(8,128)(2,1)}), bf16[8,32,512]{2,1,0:T(8,128)(2,1)}, u32[]{:S(2)}, u32[]{:S(2)}) async-start(bf16[8,32,512]{2,1,0:T(8,128)(2,1)} %broadcast_in_dim.22), calls=%async_computation.1 | async-start | bytes 524288 | tf_op jit(solution)/shard_map/all_to_all | solution.py:51
  50.9 1.5 %collective-permute-start.9 = (bf16[512,224]{0,1:T(8,128)(2,1)}, bf16[512,224]{0,1:T(8,128)(2,1)S(1)}, u32[]{:S(2)}, u32[]{:S(2)}) collective-permute-start(bf16[512,224]{0,1:T(8,128)(2,1)} %slice.169), channel_id=1, source_target_pairs={{0,64},{4,196},{64,128},{68,4},{128,192},{132,68},{192,0},{196,132... | collective-permute-start | bytes 688136 | tf_op jit(solution)/shard_map/ppermute | solution.py:27
  52.4 1.1 constant_dynamic-update-slice_fusion.1
  53.6 6.8 %collective-permute-done.9 = bf16[512,224]{0,1:T(8,128)(2,1)S(1)} collective-permute-done((bf16[512,224]{0,1:T(8,128)(2,1)}, bf16[512,224]{0,1:T(8,128)(2,1)S(1)}, u32[]{:S(2)}, u32[]{:S(2)}) %collective-permute-start.9) | collective-permute-done | bytes 229408 | tf_op jit(solution)/shard_map/ppermute | solution.py:27
  60.6 1.4 %all-to-all-done.1 = bf16[8,32,512]{2,1,0:T(8,128)(2,1)} async-done(((bf16[8,32,512]{2,1,0:T(8,128)(2,1)}), bf16[8,32,512]{2,1,0:T(8,128)(2,1)}, u32[]{:S(2)}, u32[]{:S(2)}) %all-to-all-start.1) | async-done | bytes 262176 | tf_op jit(solution)/shard_map/all_to_all | solution.py:51
  62.1 1.0 fusion.38
  64.0 0.7 fusion.35
  66.5 0.8 collective-permute-done.11
  67.5 0.8 pad_maximum_fusion.2
  68.3 5.9 %all-to-all-start.2 = ((bf16[8,32,640]{2,1,0:T(8,128)(2,1)}), bf16[8,32,640]{2,1,0:T(8,128)(2,1)S(1)}, u32[]{:S(2)}, u32[]{:S(2)}) async-start(bf16[8,32,640]{2,1,0:T(8,128)(2,1)} %pad_maximum_fusion.2), calls=%async_computation.2 | async-start | bytes 655360 | tf_op jit(solution)/shard_map/all_to_all | solution.py:192
  75.2 1.7 %collective-permute-start.15 = (bf16[112,2048]{1,0:T(8,128)(2,1)S(1)}, bf16[112,2048]{1,0:T(8,128)(2,1)}, u32[]{:S(2)}, u32[]{:S(2)}) collective-permute-start(bf16[112,2048]{1,0:T(8,128)(2,1)S(1)} %get-tuple-element.48), channel_id=1, source_target_pairs={{3,0},{0,1},{1,2},{2,3},{7,4},{4,5},{5,6},{6,7},{11,8},{8,9},{9,10... | collective-permute-start | bytes 1376264 | tf_op jit(solution)/shard_map/ppermute | solution.py:17
  76.9 1.7 %collective-permute-start.16 = (bf16[112,2048]{1,0:T(8,128)(2,1)S(1)}, bf16[112,2048]{1,0:T(8,128)(2,1)}, u32[]{:S(2)}, u32[]{:S(2)}) collective-permute-start(bf16[112,2048]{1,0:T(8,128)(2,1)S(1)} %get-tuple-element.47), channel_id=1, source_target_pairs={{1,0},{2,1},{3,2},{0,3},{5,4},{6,5},{7,6},{4,7},{9,8},{10,9},{11,1... | collective-permute-start | bytes 1376264 | tf_op jit(solution)/shard_map/ppermute | solution.py:17
  78.5 2.0 %collective-permute-start.17 = (bf16[112,2048]{1,0:T(8,128)(2,1)S(1)}, bf16[112,2048]{1,0:T(8,128)(2,1)}, u32[]{:S(2)}, u32[]{:S(2)}) collective-permute-start(bf16[112,2048]{1,0:T(8,128)(2,1)S(1)} %get-tuple-element.46), channel_id=1, source_target_pairs={{2,0},{3,1},{0,2},{1,3},{6,4},{7,5},{4,6},{5,7},{10,8},{11,9},{8,1... | collective-permute-start | bytes 1376264 | tf_op jit(solution)/shard_map/ppermute | solution.py:17
  80.5 5.8 %all-to-all-done.2 = bf16[8,32,640]{2,1,0:T(8,128)(2,1)S(1)} async-done(((bf16[8,32,640]{2,1,0:T(8,128)(2,1)}), bf16[8,32,640]{2,1,0:T(8,128)(2,1)S(1)}, u32[]{:S(2)}, u32[]{:S(2)}) %all-to-all-start.2) | async-done | bytes 327712 | tf_op jit(solution)/shard_map/all_to_all | solution.py:192
  86.4 0.7 collective-permute-start.12
  87.1 0.7 broadcast_in_dim.25
  87.8 8.4 %all-to-all-start.3 = ((bf16[8,32,512]{2,1,0:T(8,128)(2,1)}), bf16[8,32,512]{2,1,0:T(8,128)(2,1)S(1)}, u32[]{:S(2)}, u32[]{:S(2)}) async-start(bf16[8,32,512]{2,1,0:T(8,128)(2,1)} %broadcast_in_dim.25), calls=%async_computation.3 | async-start | bytes 524288 | tf_op jit(solution)/shard_map/all_to_all | solution.py:51
  96.2 1.9 %collective-permute-start.14 = (f32[1,128]{1,0:T(1,128)S(1)}, f32[1,128]{1,0:T(1,128)S(1)}, u32[]{:S(2)}, u32[]{:S(2)}) collective-permute-start(f32[1,128]{1,0:T(1,128)S(1)} %slice_add_fusion.2), channel_id=1, source_target_pairs={{0,4},{4,0},{1,5},{5,1},{2,6},{6,2},{3,7},{7,3},{8,12},{12,8},{9,1... | collective-permute-start | bytes 1544 | tf_op jit(solution)/shard_map/ppermute | solution.py:31
  98.0 1.6 %collective-permute-done.17 = bf16[112,2048]{1,0:T(8,128)(2,1)} collective-permute-done((bf16[112,2048]{1,0:T(8,128)(2,1)S(1)}, bf16[112,2048]{1,0:T(8,128)(2,1)}, u32[]{:S(2)}, u32[]{:S(2)}) %collective-permute-start.17) | collective-permute-done | bytes 458784 | tf_op jit(solution)/shard_map/ppermute | solution.py:17
  99.7 1.6 %add_convert_fusion = bf16[112,2048]{1,0:T(8,128)(2,1)S(1)} fusion(bf16[112,2048]{1,0:T(8,128)(2,1)} %collective-permute-done.17, bf16[112,2048]{1,0:T(8,128)(2,1)} %collective-permute-done.16, bf16[112,2048]{1,0:T(8,128)(2,1)} %collective-permute-done.15, bf16[112,2048]{1,0:T(8,128)(2,1)S(1)} %get-tuple-element.33), kind=kLoop, calls=%fused_computation.8 | loop fusion | flops 1835008 | bytes 2293760 | tf_op jit(solution)/shard_map/convert_element_type | solution.py:216
  101.8 1.8 %collective-permute-start.19 = (bf16[120,512]{1,0:T(8,128)(2,1)S(1)}, bf16[120,512]{1,0:T(8,128)(2,1)S(1)}, u32[]{:S(2)}, u32[]{:S(2)}) collective-permute-start(bf16[120,512]{1,0:T(8,128)(2,1)S(1)} %get-tuple-element.70), channel_id=1, source_target_pairs={{0,64},{4,196},{64,128},{68,4},{128,192},{132,68},{192,0},{196,132... | collective-permute-start | bytes 368648 | tf_op jit(solution)/shard_map/ppermute | solution.py:27
  103.8 2.7 %all-to-all-done.3 = bf16[8,32,512]{2,1,0:T(8,128)(2,1)S(1)} async-done(((bf16[8,32,512]{2,1,0:T(8,128)(2,1)}), bf16[8,32,512]{2,1,0:T(8,128)(2,1)S(1)}, u32[]{:S(2)}, u32[]{:S(2)}) %all-to-all-start.3) | async-done | bytes 262176 | tf_op jit(solution)/shard_map/all_to_all | solution.py:51
  106.4 1.4 %collective-permute-start.13 = (bf16[256,512]{1,0:T(8,128)(2,1)S(1)}, bf16[256,512]{1,0:T(8,128)(2,1)S(1)}, u32[]{:S(2)}, u32[]{:S(2)}) collective-permute-start(bf16[256,512]{1,0:T(8,128)(2,1)S(1)} %bitcast.58), channel_id=1, source_target_pairs={{0,4},{4,0},{1,5},{5,1},{2,6},{6,2},{3,7},{7,3},{8,12},{12,8},{9,1... | collective-permute-start | bytes 786440 | tf_op jit(solution)/shard_map/ppermute | solution.py:31
  107.8 2.6 %collective-permute-done.19 = bf16[120,512]{1,0:T(8,128)(2,1)S(1)} collective-permute-done((bf16[120,512]{1,0:T(8,128)(2,1)S(1)}, bf16[120,512]{1,0:T(8,128)(2,1)S(1)}, u32[]{:S(2)}, u32[]{:S(2)}) %collective-permute-start.19) | collective-permute-done | bytes 122912 | tf_op jit(solution)/shard_map/ppermute | solution.py:27
  111.4 1.2 collective-permute-start.21
  112.6 2.1 %collective-permute-start.22 = (bf16[120,512]{1,0:T(8,128)(2,1)S(1)}, bf16[120,512]{1,0:T(8,128)(2,1)S(1)}, u32[]{:S(2)}, u32[]{:S(2)}) collective-permute-start(bf16[120,512]{1,0:T(8,128)(2,1)S(1)} %get-tuple-element.55), channel_id=1, source_target_pairs={{1,0},{2,1},{3,2},{0,3},{5,4},{6,5},{7,6},{4,7},{9,8},{10,9},{11,1... | collective-permute-start | bytes 368648 | tf_op jit(solution)/shard_map/ppermute | solution.py:17
  115.2 0.7 add_bitcast_fusion
  115.9 2.1 %collective-permute-done.21 = bf16[120,512]{1,0:T(8,128)(2,1)S(1)} collective-permute-done((bf16[120,512]{1,0:T(8,128)(2,1)S(1)}, bf16[120,512]{1,0:T(8,128)(2,1)S(1)}, u32[]{:S(2)}, u32[]{:S(2)}) %collective-permute-start.21) | collective-permute-done | bytes 122912 | tf_op jit(solution)/shard_map/ppermute | solution.py:17
  118.0 1.4 %collective-permute-done.22 = bf16[120,512]{1,0:T(8,128)(2,1)S(1)} collective-permute-done((bf16[120,512]{1,0:T(8,128)(2,1)S(1)}, bf16[120,512]{1,0:T(8,128)(2,1)S(1)}, u32[]{:S(2)}, u32[]{:S(2)}) %collective-permute-start.22) | collective-permute-done | bytes 122912 | tf_op jit(solution)/shard_map/ppermute | solution.py:17
  119.4 1.7 %collective-permute-done.23 = bf16[120,512]{1,0:T(8,128)(2,1)S(1)} collective-permute-done((bf16[120,512]{1,0:T(8,128)(2,1)S(1)}, bf16[120,512]{1,0:T(8,128)(2,1)S(1)}, u32[]{:S(2)}, u32[]{:S(2)}) %collective-permute-start.23) | collective-permute-done | bytes 122912 | tf_op jit(solution)/shard_map/ppermute | solution.py:17
  122.9 0.8 fusion.21
  (99 shorter events, 9.3 us)
Async XLA Ops:
  0.6 6.3 %copy-start.3 = (bf16[512,448]{0,1:T(8,128)(2,1)S(1)}, bf16[512,448]{0,1:T(8,128)(2,1)}, u32[]{:S(2)}) copy-start(bf16[512,448]{0,1:T(8,128)(2,1)} %param.11) | copy-start | bytes 1376260
  0.6 7.4 %collective-permute-start.2 = (bf16[128,448]{0,1:T(8,128)(2,1)}, bf16[128,448]{0,1:T(8,128)(2,1)S(1)}, u32[]{:S(2)}, u32[]{:S(2)}) collective-permute-start(bf16[128,448]{0,1:T(8,128)(2,1)} %param.7), channel_id=1, source_target_pairs={{128,0},{192,64},{0,128},{64,192},{129,1},{193,65},{1,129},{65,193... | collective-permute-start | bytes 344072 | tf_op jit(solution)/shard_map/ppermute | solution.py:17
  3.8 6.1 %collective-permute-start = (bf16[128,448]{0,1:T(8,128)(2,1)}, bf16[128,448]{0,1:T(8,128)(2,1)S(1)}, u32[]{:S(2)}, u32[]{:S(2)}) collective-permute-start(bf16[128,448]{0,1:T(8,128)(2,1)} %param.7), channel_id=1, source_target_pairs={{0,192},{4,68},{64,0},{68,132},{128,64},{132,196},{192,128},{196,4... | collective-permute-start | bytes 344072 | tf_op jit(solution)/shard_map/ppermute | solution.py:27
  4.9 6.2 %collective-permute-start.1 = (bf16[128,448]{0,1:T(8,128)(2,1)}, bf16[128,448]{0,1:T(8,128)(2,1)S(1)}, u32[]{:S(2)}, u32[]{:S(2)}) collective-permute-start(bf16[128,448]{0,1:T(8,128)(2,1)} %param.7), channel_id=1, source_target_pairs={{0,64},{4,196},{64,128},{68,4},{128,192},{132,68},{192,0},{196,132... | collective-permute-start | bytes 344072 | tf_op jit(solution)/shard_map/ppermute | solution.py:27
  5.8 7.0 %collective-permute-start.4 = (bf16[448,512]{1,0:T(8,128)(2,1)}, bf16[448,512]{1,0:T(8,128)(2,1)S(1)}, u32[]{:S(2)}, u32[]{:S(2)}) collective-permute-start(bf16[448,512]{1,0:T(8,128)(2,1)} %param.9), channel_id=1, source_target_pairs={{0,4},{4,0},{1,5},{5,1},{2,6},{6,2},{3,7},{7,3},{8,12},{12,8},{9,1... | collective-permute-start | bytes 1376264 | tf_op jit(solution)/shard_map/ppermute | solution.py:31
  6.7 1.2 copy-start.5
  6.9 6.2 %copy-start.4 = (bf16[448,512]{1,0:T(8,128)(2,1)S(1)}, bf16[448,512]{1,0:T(8,128)(2,1)}, u32[]{:S(2)}) copy-start(bf16[448,512]{1,0:T(8,128)(2,1)} %param.9) | copy-start | bytes 1376260
  11.2 1.6 %collective-permute-start.3 = (bf16[256,448]{0,1:T(8,128)(2,1)S(1)}, bf16[256,448]{0,1:T(8,128)(2,1)S(1)}, u32[]{:S(2)}, u32[]{:S(2)}) collective-permute-start(bf16[256,448]{0,1:T(8,128)(2,1)S(1)} %slice.221), channel_id=1, source_target_pairs={{0,4},{4,0},{1,5},{5,1},{2,6},{6,2},{3,7},{7,3},{8,12},{12,8},{9,1... | collective-permute-start | bytes 688136 | tf_op jit(solution)/shard_map/ppermute | solution.py:31
  13.1 26.1 %copy-start.7 = (f32[512]{0:T(512)S(1)}, f32[512]{0:T(512)}, u32[]{:S(2)}) copy-start(f32[512]{0:T(512)} %param.10) | copy-start | bytes 6148
  14.3 24.9 %all-to-all-start = ((f32[8,32,512]{2,1,0:T(8,128)}), f32[8,32,512]{2,1,0:T(8,128)S(1)}, u32[]{:S(2)}, u32[]{:S(2)}) async-start(f32[8,32,512]{2,1,0:T(8,128)} %bitcast), calls=%async_computation | async-start | bytes 1048576 | tf_op jit(solution)/shard_map/all_to_all | solution.py:51
  22.8 17.1 %collective-permute-start.6 = (bf16[512,464]{0,1:T(8,128)(2,1)}, bf16[512,464]{0,1:T(8,128)(2,1)}, u32[]{:S(2)}, u32[]{:S(2)}) collective-permute-start(bf16[512,464]{0,1:T(8,128)(2,1)} %get-tuple-element.24), channel_id=1, source_target_pairs={{0,64},{4,196},{64,128},{68,4},{128,192},{132,68},{192,0},{196,132... | collective-permute-start | bytes 1425416 | tf_op jit(solution)/shard_map/ppermute | solution.py:27
  23.1 16.8 %collective-permute-start.7 = (bf16[512,464]{0,1:T(8,128)(2,1)}, bf16[512,464]{0,1:T(8,128)(2,1)S(1)}, u32[]{:S(2)}, u32[]{:S(2)}) collective-permute-start(bf16[512,464]{0,1:T(8,128)(2,1)} %get-tuple-element.24), channel_id=1, source_target_pairs={{0,192},{4,68},{64,0},{68,132},{128,64},{132,196},{192,128},{196,4... | collective-permute-start | bytes 1425416 | tf_op jit(solution)/shard_map/ppermute | solution.py:27
  39.3 3.1 %collective-permute-start.5 = (bf16[32,512]{1,0:T(8,128)(2,1)S(1)}, bf16[32,512]{1,0:T(8,128)(2,1)S(1)}, u32[]{:S(2)}, u32[]{:S(2)}) collective-permute-start(bf16[32,512]{1,0:T(8,128)(2,1)S(1)} %maximum_convert_fusion), channel_id=1, source_target_pairs={{0,0},{4,132},{8,8},{12,140},{16,16},{20,148},{24,24},{28,156},{32... | collective-permute-start | bytes 98312 | tf_op jit(solution)/shard_map/ppermute | solution.py:43
  43.1 18.9 %all-to-all-start.1 = ((bf16[8,32,512]{2,1,0:T(8,128)(2,1)}), bf16[8,32,512]{2,1,0:T(8,128)(2,1)}, u32[]{:S(2)}, u32[]{:S(2)}) async-start(bf16[8,32,512]{2,1,0:T(8,128)(2,1)} %broadcast_in_dim.22), calls=%async_computation.1 | async-start | bytes 524288 | tf_op jit(solution)/shard_map/all_to_all | solution.py:51
  50.4 10.1 %collective-permute-start.10 = (bf16[512,240]{0,1:T(8,128)(2,1)}, bf16[512,240]{0,1:T(8,128)(2,1)S(1)}, u32[]{:S(2)}, u32[]{:S(2)}) collective-permute-start(bf16[512,240]{0,1:T(8,128)(2,1)} %slice.170), channel_id=1, source_target_pairs={{0,192},{4,68},{64,0},{68,132},{128,64},{132,196},{192,128},{196,4... | collective-permute-start | bytes 737288 | tf_op jit(solution)/shard_map/ppermute | solution.py:27
  50.9 9.5 %collective-permute-start.9 = (bf16[512,224]{0,1:T(8,128)(2,1)}, bf16[512,224]{0,1:T(8,128)(2,1)S(1)}, u32[]{:S(2)}, u32[]{:S(2)}) collective-permute-start(bf16[512,224]{0,1:T(8,128)(2,1)} %slice.169), channel_id=1, source_target_pairs={{0,64},{4,196},{64,128},{68,4},{128,192},{132,68},{192,0},{196,132... | collective-permute-start | bytes 688136 | tf_op jit(solution)/shard_map/ppermute | solution.py:27
  52.4 11.3 %copy-start = (bf16[128,2048]{1,0:T(8,128)(2,1)S(1)}, bf16[128,2048]{1,0:T(8,128)(2,1)}, u32[]{:S(2)}) copy-start(bf16[128,2048]{1,0:T(8,128)(2,1)} %shard_map.102) | copy-start | bytes 1572868
  61.9 1.7 %collective-permute-start.8 = (bf16[2,128,512]{2,1,0:T(8,128)(2,1)}, bf16[2,128,512]{2,1,0:T(8,128)(2,1)S(1)}, u32[]{:S(2)}, u32[]{:S(2)}) collective-permute-start(bf16[2,128,512]{2,1,0:T(8,128)(2,1)} %bitcast.4), channel_id=1, source_target_pairs={{0,4},{4,0},{1,5},{5,1},{2,6},{6,2},{3,7},{7,3},{8,12},{12,8},{9,1... | collective-permute-start | bytes 786440 | tf_op jit(solution)/shard_map/ppermute | solution.py:31
  63.9 0.8 copy-start.1
  64.0 1.0 copy-start.6
  65.6 1.6 %collective-permute-start.11 = (bf16[128,1024]{1,0:T(8,128)(2,1)S(1)}, bf16[128,1024]{1,0:T(8,128)(2,1)S(1)}, u32[]{:S(2)}, u32[]{:S(2)}) collective-permute-start(bf16[128,1024]{1,0:T(8,128)(2,1)S(1)} %fusion.5), channel_id=1, source_target_pairs={{0,4},{4,0},{1,5},{5,1},{2,6},{6,2},{3,7},{7,3},{8,12},{12,8},{9,1... | collective-permute-start | bytes 786440 | tf_op jit(solution)/shard_map/ppermute | solution.py:31
  67.4 6.8 %copy-start.2 = (bf16[128,2048]{1,0:T(8,128)(2,1)S(1)}, bf16[128,2048]{1,0:T(8,128)(2,1)}, u32[]{:S(2)}) copy-start(bf16[128,2048]{1,0:T(8,128)(2,1)} %copy-done.1) | copy-start | bytes 1572868
  68.3 18.0 %all-to-all-start.2 = ((bf16[8,32,640]{2,1,0:T(8,128)(2,1)}), bf16[8,32,640]{2,1,0:T(8,128)(2,1)S(1)}, u32[]{:S(2)}, u32[]{:S(2)}) async-start(bf16[8,32,640]{2,1,0:T(8,128)(2,1)} %pad_maximum_fusion.2), calls=%async_computation.2 | async-start | bytes 655360 | tf_op jit(solution)/shard_map/all_to_all | solution.py:192
  75.2 22.8 %collective-permute-start.15 = (bf16[112,2048]{1,0:T(8,128)(2,1)S(1)}, bf16[112,2048]{1,0:T(8,128)(2,1)}, u32[]{:S(2)}, u32[]{:S(2)}) collective-permute-start(bf16[112,2048]{1,0:T(8,128)(2,1)S(1)} %get-tuple-element.48), channel_id=1, source_target_pairs={{3,0},{0,1},{1,2},{2,3},{7,4},{4,5},{5,6},{6,7},{11,8},{8,9},{9,10... | collective-permute-start | bytes 1376264 | tf_op jit(solution)/shard_map/ppermute | solution.py:17
  76.9 21.2 %collective-permute-start.16 = (bf16[112,2048]{1,0:T(8,128)(2,1)S(1)}, bf16[112,2048]{1,0:T(8,128)(2,1)}, u32[]{:S(2)}, u32[]{:S(2)}) collective-permute-start(bf16[112,2048]{1,0:T(8,128)(2,1)S(1)} %get-tuple-element.47), channel_id=1, source_target_pairs={{1,0},{2,1},{3,2},{0,3},{5,4},{6,5},{7,6},{4,7},{9,8},{10,9},{11,1... | collective-permute-start | bytes 1376264 | tf_op jit(solution)/shard_map/ppermute | solution.py:17
  78.5 21.1 %collective-permute-start.17 = (bf16[112,2048]{1,0:T(8,128)(2,1)S(1)}, bf16[112,2048]{1,0:T(8,128)(2,1)}, u32[]{:S(2)}, u32[]{:S(2)}) collective-permute-start(bf16[112,2048]{1,0:T(8,128)(2,1)S(1)} %get-tuple-element.46), channel_id=1, source_target_pairs={{2,0},{3,1},{0,2},{1,3},{6,4},{7,5},{4,6},{5,7},{10,8},{11,9},{8,1... | collective-permute-start | bytes 1376264 | tf_op jit(solution)/shard_map/ppermute | solution.py:17
  86.4 0.7 collective-permute-start.12
  87.8 18.7 %all-to-all-start.3 = ((bf16[8,32,512]{2,1,0:T(8,128)(2,1)}), bf16[8,32,512]{2,1,0:T(8,128)(2,1)S(1)}, u32[]{:S(2)}, u32[]{:S(2)}) async-start(bf16[8,32,512]{2,1,0:T(8,128)(2,1)} %broadcast_in_dim.25), calls=%async_computation.3 | async-start | bytes 524288 | tf_op jit(solution)/shard_map/all_to_all | solution.py:51
  96.2 5.1 %collective-permute-start.14 = (f32[1,128]{1,0:T(1,128)S(1)}, f32[1,128]{1,0:T(1,128)S(1)}, u32[]{:S(2)}, u32[]{:S(2)}) collective-permute-start(f32[1,128]{1,0:T(1,128)S(1)} %slice_add_fusion.2), channel_id=1, source_target_pairs={{0,4},{4,0},{1,5},{5,1},{2,6},{6,2},{3,7},{7,3},{8,12},{12,8},{9,1... | collective-permute-start | bytes 1544 | tf_op jit(solution)/shard_map/ppermute | solution.py:31
  101.5 6.4 %collective-permute-start.18 = (bf16[120,512]{1,0:T(8,128)(2,1)S(1)}, bf16[120,512]{1,0:T(8,128)(2,1)S(1)}, u32[]{:S(2)}, u32[]{:S(2)}) collective-permute-start(bf16[120,512]{1,0:T(8,128)(2,1)S(1)} %get-tuple-element.69), channel_id=1, source_target_pairs={{0,192},{4,68},{64,0},{68,132},{128,64},{132,196},{192,128},{196,4... | collective-permute-start | bytes 368648 | tf_op jit(solution)/shard_map/ppermute | solution.py:27
  101.8 8.7 %collective-permute-start.19 = (bf16[120,512]{1,0:T(8,128)(2,1)S(1)}, bf16[120,512]{1,0:T(8,128)(2,1)S(1)}, u32[]{:S(2)}, u32[]{:S(2)}) collective-permute-start(bf16[120,512]{1,0:T(8,128)(2,1)S(1)} %get-tuple-element.70), channel_id=1, source_target_pairs={{0,64},{4,196},{64,128},{68,4},{128,192},{132,68},{192,0},{196,132... | collective-permute-start | bytes 368648 | tf_op jit(solution)/shard_map/ppermute | solution.py:27
  103.6 6.9 %collective-permute-start.20 = (bf16[120,512]{1,0:T(8,128)(2,1)S(1)}, bf16[120,512]{1,0:T(8,128)(2,1)S(1)}, u32[]{:S(2)}, u32[]{:S(2)}) collective-permute-start(bf16[120,512]{1,0:T(8,128)(2,1)S(1)} %get-tuple-element.68), channel_id=1, source_target_pairs={{128,0},{192,64},{0,128},{64,192},{129,1},{193,65},{1,129},{65,193... | collective-permute-start | bytes 368648 | tf_op jit(solution)/shard_map/ppermute | solution.py:17
  106.4 4.2 %collective-permute-start.13 = (bf16[256,512]{1,0:T(8,128)(2,1)S(1)}, bf16[256,512]{1,0:T(8,128)(2,1)S(1)}, u32[]{:S(2)}, u32[]{:S(2)}) collective-permute-start(bf16[256,512]{1,0:T(8,128)(2,1)S(1)} %bitcast.58), channel_id=1, source_target_pairs={{0,4},{4,0},{1,5},{5,1},{2,6},{6,2},{3,7},{7,3},{8,12},{12,8},{9,1... | collective-permute-start | bytes 786440 | tf_op jit(solution)/shard_map/ppermute | solution.py:31
  111.4 6.6 %collective-permute-start.21 = (bf16[120,512]{1,0:T(8,128)(2,1)S(1)}, bf16[120,512]{1,0:T(8,128)(2,1)S(1)}, u32[]{:S(2)}, u32[]{:S(2)}) collective-permute-start(bf16[120,512]{1,0:T(8,128)(2,1)S(1)} %get-tuple-element.56), channel_id=1, source_target_pairs={{3,0},{0,1},{1,2},{2,3},{7,4},{4,5},{5,6},{6,7},{11,8},{8,9},{9,10... | collective-permute-start | bytes 368648 | tf_op jit(solution)/shard_map/ppermute | solution.py:17
  112.6 6.8 %collective-permute-start.22 = (bf16[120,512]{1,0:T(8,128)(2,1)S(1)}, bf16[120,512]{1,0:T(8,128)(2,1)S(1)}, u32[]{:S(2)}, u32[]{:S(2)}) collective-permute-start(bf16[120,512]{1,0:T(8,128)(2,1)S(1)} %get-tuple-element.55), channel_id=1, source_target_pairs={{1,0},{2,1},{3,2},{0,3},{5,4},{6,5},{7,6},{4,7},{9,8},{10,9},{11,1... | collective-permute-start | bytes 368648 | tf_op jit(solution)/shard_map/ppermute | solution.py:17
  114.7 6.4 %collective-permute-start.23 = (bf16[120,512]{1,0:T(8,128)(2,1)S(1)}, bf16[120,512]{1,0:T(8,128)(2,1)S(1)}, u32[]{:S(2)}, u32[]{:S(2)}) collective-permute-start(bf16[120,512]{1,0:T(8,128)(2,1)S(1)} %get-tuple-element.54), channel_id=1, source_target_pairs={{2,0},{3,1},{0,2},{1,3},{6,4},{7,5},{4,6},{5,7},{10,8},{11,9},{8,1... | collective-permute-start | bytes 368648 | tf_op jit(solution)/shard_map/ppermute | solution.py:17

commit v5 on v4

--- a/solution.py
+++ b/solution.py
@@ -107,6 +107,23 @@
     return jnp.concatenate([body] + rows + [filler], 0)
 
 
+def last_rows(last, scale):
+    def kernel(last_ref, loss_ref, bias_ref):
+        bias_ref[...] = last_ref[0:1]
+        loss_ref[0, 0] = jnp.sum(last_ref[1:3]) * scale
+
+    vmem = pl.BlockSpec(memory_space=pltpu.VMEM)
+    return pl.pallas_call(
+        kernel,
+        out_shape=[
+            jax.ShapeDtypeStruct((1, 1), F32),
+            jax.ShapeDtypeStruct((1, last.shape[1]), F32),
+        ],
+        in_specs=[vmem],
+        out_specs=[pl.BlockSpec(memory_space=pltpu.SMEM), vmem],
+    )(last)
+
+
 def local(inputs, targets, enc_weight, enc_bias, dec_weight, dead_mask, aux_picks):
     blk, z_size, rep = lax.axis_size("blk"), lax.axis_size("z"), lax.axis_size("rep")
     core, blk_at, rep_at = lax.axis_index("core"), lax.axis_index("blk"), lax.axis_index("rep")
@@ -179,17 +196,13 @@
 
     got_pulled = swap_core(pulled_half(2 * lat).astype(BF16)).astype(F32)
     pulled_sum = pulled_half(0) + got_pulled
-    pulled_sum = jnp.stack([pulled_sum[:, :lat], pulled_sum[:, lat:]], 0).astype(BF16)
-    loss_rows = jnp.concatenate(two_halves(loss_part), 0)
-    loss_rows = jnp.pad(loss_rows, ((0, piece - 2), (0, 0)))
-    packet = jnp.concatenate(
-        [
-            pulled_sum.reshape(z_size, piece, lat),
-            jnp.broadcast_to(loss_rows[None], (z_size,) + loss_rows.shape),
-        ],
-        2,
-    )
-    arrived = lax.all_to_all(packet, "z", 0, 0, tiled=True).astype(F32)
+    quarters = rows // piece
+    pulled_sum = pulled_sum.astype(BF16).reshape(quarters, piece, 2, lat // 128, 128)
+    pulled_sum = jnp.transpose(pulled_sum, (2, 0, 3, 1, 4)).reshape(z_size, piece * lat // 128, 128)
+    loss_rows = jnp.concatenate(two_halves(loss_part) + [jnp.zeros((6, 128), BF16)], 0)
+    loss_rows = jnp.broadcast_to(loss_rows[None], (z_size,) + loss_rows.shape)
+    packet = jnp.concatenate([pulled_sum, loss_rows], 1)
+    arrived = exchange_z(packet).astype(F32)
 
     dec_term = lax.dot_general(
         after(grads, packet), both, (((0,), (0,)), ((), ())), preferred_element_type=F32
@@ -207,8 +220,10 @@
     dec_parts = rep_exchange(dec_term[:width].reshape(rep, share, lat_all))
 
     arrived = jnp.sum(arrived, axis=0)
-    grad_piece = jnp.where(lat_piece > 0, arrived[:, :lat], 0.0).astype(BF16)
-    loss_width = arrived[0:1, lat:] + arrived[1:2, lat:]
+    grad_piece = arrived[:-8].reshape(lat // 128, piece, 128)
+    grad_piece = jnp.concatenate([grad_piece[i] for i in range(lat // 128)], 1)
+    grad_piece = jnp.where(lat_piece > 0, grad_piece, 0.0).astype(BF16)
+    loss_width = arrived[-8:-7] + arrived[-7:-6]
     grad_piece = shift_pieces(grad_piece, -1)
     grad_copies = z_copies(grad_piece)
     loss_width = after(loss_width, grad_copies)
@@ -246,8 +261,8 @@
     parts = rep_exchange(jnp.concatenate([enc_term.reshape(rep, share, lat)] + more, 1))
     grad_enc = sum(part[:share].astype(F32) for part in parts)
     last = sum(part[share : share + 3, :quarter].astype(F32) for part in parts)
-    loss = jnp.sum(last[1:3]) / (total_tokens * width * 2 * z_size)
-    return (loss, grad_enc, last[0], grad_dec)
+    loss, bias = last_rows(last, 1.0 / (total_tokens * width * 2 * z_size))
+    return (loss.reshape(()), grad_enc, bias.reshape(quarter), grad_dec)
 
 
 def solution(mesh):

time: 127 us -> 125 us (0.984); the launches traced: 125 us -> 125 us
  between operations: 2.92 us -> 1.14 us
  Pallas kernels: 5.69 us -> 7.01 us
    all_to_all x3 -> x4, starting transfers between devices: 24.2 us -> 30.2 us  [exchange_z(): return lax.all_to_all(copies, 'z', 0, 0, tiled=True)]
    all_to_all x1 -> x0, starting transfers between devices: 5.91 us -> none  [local(): arrived = lax.all_to_all(packet, 'z', 0, 0, tiled=True).astype(F32)]
    all_to_all x1 -> x0, waiting for transfers between devices: 5.79 us -> none  [local(): arrived = lax.all_to_all(packet, 'z', 0, 0, tiled=True).astype(F32)]
    all_to_all x3 -> x4, waiting for transfers between devices: 11.5 us -> 14.8 us  [exchange_z(): return lax.all_to_all(copies, 'z', 0, 0, tiled=True)]
    ppermute x8, waiting for transfers between devices: 6.96 us -> 8.91 us  [from_ahead(): lax.ppermute(block, axis, [((i + distance) % size, i) for i in range(size)])]
    pallas_call x0 -> x1, Pallas kernels: none -> 1.32 us  [last_rows(): pl.pallas_call(kernel, out_shape=[jax.ShapeDtypeStruct((1, 1), F32), jax....]
  transfers between devices with their start and end apart: 28 -> 28, of which waited for: 16 -> 17; matrix products, arithmetic and copies ran while one was open for 9% -> 10% of each run, Pallas kernels for 5% -> 5%
where the time goes in v5:
time: 125 us
  starting transfers between devices  56.6 us (45%)
  waiting for transfers between devices  40 us (32%)
  other arithmetic  7.88 us (6%)
  local copies, waits for them, and re-layouts  7.8 us (6%)
  Pallas kernels  7.01 us (6%)
  matrix products  4.18 us (3%)
    all_to_all x4, starting transfers between devices, exchange_z(): return lax.all_to_all(copies, 'z', 0, 0, tiled=True)  30.2 us
    all_to_all x4, waiting for transfers between devices, exchange_z(): return lax.all_to_all(copies, 'z', 0, 0, tiled=True)  14.8 us
    ppermute x8, waiting for transfers between devices, blk_move(): return lax.ppermute(block, ('blk', 'core'), route)  13.5 us
    ppermute x8, starting transfers between devices, from_ahead(): lax.ppermute(block, axis, [((i + distance) % size, i) for i in range(size)])  11.9 us
    ppermute x8, starting transfers between devices, blk_move(): return lax.ppermute(block, ('blk', 'core'), route)  9.39 us
    ppermute x8, waiting for transfers between devices, from_ahead(): lax.ppermute(block, axis, [((i + distance) % size, i) for i in range(size)])  8.91 us
    pallas_call x1, Pallas kernels, picked_latents(): pl.pallas_call(pick_kernel, out_shape=jax.ShapeDtypeStruct((rows, lat_all...  5.69 us
    ppermute x6, starting transfers between devices, swap_core(): return lax.ppermute(block, 'core', [(0, 1), (1, 0)])  3.74 us
  transfers between devices with their start and end apart: 28, of which 17 were waited for; matrix products, arithmetic and copies ran while one was open for 10% of the time, Pallas kernels for 5%

profile of v5, /device:TPU:32, one launch (start us, length us, event | category | flops | bytes accessed | tf_op | source)
XLA Modules:
  0.0 124.6 jit_solution(6307415866294333996)
XLA Ops:
  0.6 3.1 %collective-permute-start.2 = (bf16[128,448]{0,1:T(8,128)(2,1)}, bf16[128,448]{0,1:T(8,128)(2,1)S(1)}, u32[]{:S(2)}, u32[]{:S(2)}) collective-permute-start(bf16[128,448]{0,1:T(8,128)(2,1)} %param.7), channel_id=1, source_target_pairs={{128,0},{192,64},{0,128},{64,192},{129,1},{193,65},{1,129},{65,193... | collective-permute-start | bytes 344072 | tf_op jit(solution)/shard_map/ppermute | solution.py:17
  3.8 1.1 collective-permute-start
  4.9 0.9 collective-permute-start.1
  6.0 0.7 convert_element_type.168
  6.9 0.9 constant_dynamic-update-slice_fusion.2
  8.0 1.9 %collective-permute-done = bf16[128,448]{0,1:T(8,128)(2,1)S(1)} collective-permute-done((bf16[128,448]{0,1:T(8,128)(2,1)}, bf16[128,448]{0,1:T(8,128)(2,1)S(1)}, u32[]{:S(2)}, u32[]{:S(2)}) %collective-permute-start) | collective-permute-done | bytes 114720 | tf_op jit(solution)/shard_map/ppermute | solution.py:27
  9.9 1.2 collective-permute-done.1
  11.3 1.5 %collective-permute-done.3 = bf16[256,448]{0,1:T(8,128)(2,1)S(1)} collective-permute-done((bf16[256,448]{0,1:T(8,128)(2,1)S(1)}, bf16[256,448]{0,1:T(8,128)(2,1)S(1)}, u32[]{:S(2)}, u32[]{:S(2)}) %collective-permute-start.3) | collective-permute-done | bytes 229408 | tf_op jit(solution)/shard_map/ppermute | solution.py:31
  13.1 1.1 convolution_add_fusion
  14.3 8.6 %all-to-all-start = ((f32[8,32,512]{2,1,0:T(8,128)}), f32[8,32,512]{2,1,0:T(8,128)S(1)}, u32[]{:S(2)}, u32[]{:S(2)}) async-start(f32[8,32,512]{2,1,0:T(8,128)} %bitcast), calls=%async_computation | async-start | bytes 1048576 | tf_op jit(solution)/shard_map/all_to_all | solution.py:51
  23.1 3.0 %collective-permute-start.7 = (bf16[512,464]{0,1:T(8,128)(2,1)}, bf16[512,464]{0,1:T(8,128)(2,1)S(1)}, u32[]{:S(2)}, u32[]{:S(2)}) collective-permute-start(bf16[512,464]{0,1:T(8,128)(2,1)} %get-tuple-element.26), channel_id=1, source_target_pairs={{0,192},{4,68},{64,0},{68,132},{128,64},{132,196},{192,128},{196,4... | collective-permute-start | bytes 1425416 | tf_op jit(solution)/shard_map/ppermute | solution.py:27
  26.1 5.7 %shard_map.102 = bf16[128,2048]{1,0:T(8,128)(2,1)} custom-call(s32[1]{0:T(128)} %bitcast.1.own_ref, s32[128,512]{1,0:T(8,128)} %picks_ref.1), custom_call_target="tpu_custom_call" | custom-call | flops 20000000 | bytes 1000000 | tf_op jit(solution)/shard_map/pallas_call | solution.py:82
  31.8 7.4 %all-to-all-done = f32[8,32,512]{2,1,0:T(8,128)S(1)} async-done(((f32[8,32,512]{2,1,0:T(8,128)}), f32[8,32,512]{2,1,0:T(8,128)S(1)}, u32[]{:S(2)}, u32[]{:S(2)}) %all-to-all-start) | async-done | bytes 524320 | tf_op jit(solution)/shard_map/all_to_all | solution.py:51
  39.9 0.7 slice.174
  40.7 1.6 %slice.173 = bf16[512,224]{0,1:T(8,128)(2,1)} slice(bf16[512,464]{0,1:T(8,128)(2,1)} %collective-permute-done.6), slice={[0:512], [0:224]} | slice | bytes 458752 | tf_op jit(solution)/shard_map/slice | solution.py:165
  42.3 0.7 broadcast_in_dim.24
  43.0 7.3 %all-to-all-start.1 = ((bf16[8,32,512]{2,1,0:T(8,128)(2,1)}), bf16[8,32,512]{2,1,0:T(8,128)(2,1)}, u32[]{:S(2)}, u32[]{:S(2)}) async-start(bf16[8,32,512]{2,1,0:T(8,128)(2,1)} %broadcast_in_dim.24), calls=%async_computation.1 | async-start | bytes 524288 | tf_op jit(solution)/shard_map/all_to_all | solution.py:51
  51.0 1.5 %collective-permute-start.9 = (bf16[512,224]{0,1:T(8,128)(2,1)}, bf16[512,224]{0,1:T(8,128)(2,1)S(1)}, u32[]{:S(2)}, u32[]{:S(2)}) collective-permute-start(bf16[512,224]{0,1:T(8,128)(2,1)} %slice.173), channel_id=1, source_target_pairs={{0,64},{4,196},{64,128},{68,4},{128,192},{132,68},{192,0},{196,132... | collective-permute-start | bytes 688136 | tf_op jit(solution)/shard_map/ppermute | solution.py:27
  52.5 1.1 constant_dynamic-update-slice_fusion.1
  53.7 6.8 %collective-permute-done.9 = bf16[512,224]{0,1:T(8,128)(2,1)S(1)} collective-permute-done((bf16[512,224]{0,1:T(8,128)(2,1)}, bf16[512,224]{0,1:T(8,128)(2,1)S(1)}, u32[]{:S(2)}, u32[]{:S(2)}) %collective-permute-start.9) | collective-permute-done | bytes 229408 | tf_op jit(solution)/shard_map/ppermute | solution.py:27
  60.6 1.3 %all-to-all-done.1 = bf16[8,32,512]{2,1,0:T(8,128)(2,1)} async-done(((bf16[8,32,512]{2,1,0:T(8,128)(2,1)}), bf16[8,32,512]{2,1,0:T(8,128)(2,1)}, u32[]{:S(2)}, u32[]{:S(2)}) %all-to-all-start.1) | async-done | bytes 262176 | tf_op jit(solution)/shard_map/all_to_all | solution.py:51
  62.1 1.0 fusion.35
  63.9 0.7 fusion.32
  65.5 0.7 fusion.18
  67.2 0.7 collective-permute-done.11
  68.3 0.7 pad_maximum_fusion.2
  69.1 6.0 %all-to-all-start.2 = ((bf16[8,136,128]{2,1,0:T(8,128)(2,1)}), bf16[8,136,128]{2,1,0:T(8,128)(2,1)S(1)}, u32[]{:S(2)}, u32[]{:S(2)}) async-start(bf16[8,136,128]{2,1,0:T(8,128)(2,1)} %pad_maximum_fusion.2), calls=%async_computation.2 | async-start | bytes 557056 | tf_op jit(solution)/shard_map/all_to_all | solution.py:51
  76.1 1.6 %collective-permute-start.15 = (bf16[112,2048]{1,0:T(8,128)(2,1)S(1)}, bf16[112,2048]{1,0:T(8,128)(2,1)}, u32[]{:S(2)}, u32[]{:S(2)}) collective-permute-start(bf16[112,2048]{1,0:T(8,128)(2,1)S(1)} %get-tuple-element.52), channel_id=1, source_target_pairs={{3,0},{0,1},{1,2},{2,3},{7,4},{4,5},{5,6},{6,7},{11,8},{8,9},{9,10... | collective-permute-start | bytes 1376264 | tf_op jit(solution)/shard_map/ppermute | solution.py:17
  77.7 1.7 %collective-permute-start.16 = (bf16[112,2048]{1,0:T(8,128)(2,1)S(1)}, bf16[112,2048]{1,0:T(8,128)(2,1)}, u32[]{:S(2)}, u32[]{:S(2)}) collective-permute-start(bf16[112,2048]{1,0:T(8,128)(2,1)S(1)} %get-tuple-element.51), channel_id=1, source_target_pairs={{1,0},{2,1},{3,2},{0,3},{5,4},{6,5},{7,6},{4,7},{9,8},{10,9},{11,1... | collective-permute-start | bytes 1376264 | tf_op jit(solution)/shard_map/ppermute | solution.py:17
  79.4 2.0 %collective-permute-start.17 = (bf16[112,2048]{1,0:T(8,128)(2,1)S(1)}, bf16[112,2048]{1,0:T(8,128)(2,1)}, u32[]{:S(2)}, u32[]{:S(2)}) collective-permute-start(bf16[112,2048]{1,0:T(8,128)(2,1)S(1)} %get-tuple-element.50), channel_id=1, source_target_pairs={{2,0},{3,1},{0,2},{1,3},{6,4},{7,5},{4,6},{5,7},{10,8},{11,9},{8,1... | collective-permute-start | bytes 1376264 | tf_op jit(solution)/shard_map/ppermute | solution.py:17
  81.4 4.8 %all-to-all-done.2 = bf16[8,136,128]{2,1,0:T(8,128)(2,1)S(1)} async-done(((bf16[8,136,128]{2,1,0:T(8,128)(2,1)}), bf16[8,136,128]{2,1,0:T(8,128)(2,1)S(1)}, u32[]{:S(2)}, u32[]{:S(2)}) %all-to-all-start.2) | async-done | bytes 278560 | tf_op jit(solution)/shard_map/all_to_all | solution.py:51
  86.9 0.7 broadcast_in_dim.28
  87.7 8.4 %all-to-all-start.3 = ((bf16[8,32,512]{2,1,0:T(8,128)(2,1)}), bf16[8,32,512]{2,1,0:T(8,128)(2,1)S(1)}, u32[]{:S(2)}, u32[]{:S(2)}) async-start(bf16[8,32,512]{2,1,0:T(8,128)(2,1)} %broadcast_in_dim.28), calls=%async_computation.3 | async-start | bytes 524288 | tf_op jit(solution)/shard_map/all_to_all | solution.py:51
  96.1 1.2 %collective-permute-start.14 = (f32[1,128]{1,0:T(1,128)S(1)}, f32[1,128]{1,0:T(1,128)S(1)}, u32[]{:S(2)}, u32[]{:S(2)}) collective-permute-start(f32[1,128]{1,0:T(1,128)S(1)} %slice_add_fusion.2), channel_id=1, source_target_pairs={{0,4},{4,0},{1,5},{5,1},{2,6},{6,2},{3,7},{7,3},{8,12},{12,8},{9,1... | collective-permute-start | bytes 1544 | tf_op jit(solution)/shard_map/ppermute | solution.py:31
  97.3 1.3 %collective-permute-done.16 = bf16[112,2048]{1,0:T(8,128)(2,1)} collective-permute-done((bf16[112,2048]{1,0:T(8,128)(2,1)S(1)}, bf16[112,2048]{1,0:T(8,128)(2,1)}, u32[]{:S(2)}, u32[]{:S(2)}) %collective-permute-start.16) | collective-permute-done | bytes 458784 | tf_op jit(solution)/shard_map/ppermute | solution.py:17
  98.7 1.9 %collective-permute-done.17 = bf16[112,2048]{1,0:T(8,128)(2,1)} collective-permute-done((bf16[112,2048]{1,0:T(8,128)(2,1)S(1)}, bf16[112,2048]{1,0:T(8,128)(2,1)}, u32[]{:S(2)}, u32[]{:S(2)}) %collective-permute-start.17) | collective-permute-done | bytes 458784 | tf_op jit(solution)/shard_map/ppermute | solution.py:17
  100.6 1.6 %add_convert_fusion = bf16[112,2048]{1,0:T(8,128)(2,1)S(1)} fusion(bf16[112,2048]{1,0:T(8,128)(2,1)} %collective-permute-done.17, bf16[112,2048]{1,0:T(8,128)(2,1)} %collective-permute-done.16, bf16[112,2048]{1,0:T(8,128)(2,1)} %collective-permute-done.15, bf16[112,2048]{1,0:T(8,128)(2,1)S(1)} %get-tuple-element.35), kind=kLoop, calls=%fused_computation.8 | loop fusion | flops 1835008 | bytes 2293760 | tf_op jit(solution)/shard_map/convert_element_type | solution.py:231
  102.6 1.9 %collective-permute-start.19 = (bf16[120,512]{1,0:T(8,128)(2,1)S(1)}, bf16[120,512]{1,0:T(8,128)(2,1)S(1)}, u32[]{:S(2)}, u32[]{:S(2)}) collective-permute-start(bf16[120,512]{1,0:T(8,128)(2,1)S(1)} %get-tuple-element.76), channel_id=1, source_target_pairs={{0,64},{4,196},{64,128},{68,4},{128,192},{132,68},{192,0},{196,132... | collective-permute-start | bytes 368648 | tf_op jit(solution)/shard_map/ppermute | solution.py:27
  104.6 1.3 %all-to-all-done.3 = bf16[8,32,512]{2,1,0:T(8,128)(2,1)S(1)} async-done(((bf16[8,32,512]{2,1,0:T(8,128)(2,1)}), bf16[8,32,512]{2,1,0:T(8,128)(2,1)S(1)}, u32[]{:S(2)}, u32[]{:S(2)}) %all-to-all-start.3) | async-done | bytes 262176 | tf_op jit(solution)/shard_map/all_to_all | solution.py:51
  105.9 1.8 %collective-permute-start.13 = (bf16[256,512]{1,0:T(8,128)(2,1)S(1)}, bf16[256,512]{1,0:T(8,128)(2,1)S(1)}, u32[]{:S(2)}, u32[]{:S(2)}) collective-permute-start(bf16[256,512]{1,0:T(8,128)(2,1)S(1)} %bitcast.56), channel_id=1, source_target_pairs={{0,4},{4,0},{1,5},{5,1},{2,6},{6,2},{3,7},{7,3},{8,12},{12,8},{9,1... | collective-permute-start | bytes 786440 | tf_op jit(solution)/shard_map/ppermute | solution.py:31
  108.1 3.2 %collective-permute-done.19 = bf16[120,512]{1,0:T(8,128)(2,1)S(1)} collective-permute-done((bf16[120,512]{1,0:T(8,128)(2,1)S(1)}, bf16[120,512]{1,0:T(8,128)(2,1)S(1)}, u32[]{:S(2)}, u32[]{:S(2)}) %collective-permute-start.19) | collective-permute-done | bytes 122912 | tf_op jit(solution)/shard_map/ppermute | solution.py:27
  112.2 1.2 collective-permute-start.21
  113.5 2.1 %collective-permute-start.22 = (bf16[120,512]{1,0:T(8,128)(2,1)S(1)}, bf16[120,512]{1,0:T(8,128)(2,1)S(1)}, u32[]{:S(2)}, u32[]{:S(2)}) collective-permute-start(bf16[120,512]{1,0:T(8,128)(2,1)S(1)} %get-tuple-element.59), channel_id=1, source_target_pairs={{1,0},{2,1},{3,2},{0,3},{5,4},{6,5},{7,6},{4,7},{9,8},{10,9},{11,1... | collective-permute-start | bytes 368648 | tf_op jit(solution)/shard_map/ppermute | solution.py:17
  115.6 0.7 add_bitcast_fusion
  116.4 3.3 %collective-permute-done.21 = bf16[120,512]{1,0:T(8,128)(2,1)S(1)} collective-permute-done((bf16[120,512]{1,0:T(8,128)(2,1)S(1)}, bf16[120,512]{1,0:T(8,128)(2,1)S(1)}, u32[]{:S(2)}, u32[]{:S(2)}) %collective-permute-start.21) | collective-permute-done | bytes 122912 | tf_op jit(solution)/shard_map/ppermute | solution.py:17
  119.7 2.2 %collective-permute-done.23 = bf16[120,512]{1,0:T(8,128)(2,1)S(1)} collective-permute-done((bf16[120,512]{1,0:T(8,128)(2,1)S(1)}, bf16[120,512]{1,0:T(8,128)(2,1)S(1)}, u32[]{:S(2)}, u32[]{:S(2)}) %collective-permute-start.23) | collective-permute-done | bytes 122912 | tf_op jit(solution)/shard_map/ppermute | solution.py:17
  122.5 1.3 %shard_map.103 = (f32[1,1]{1,0:T(1,128)}, f32[1,128]{1,0:T(1,128)}) custom-call(f32[3,128]{1,0:T(4,128)} %convert_add_fusion.1.last_ref), custom_call_target="tpu_custom_call" | custom-call | tf_op jit(solution)/shard_map/pallas_call | solution.py:116
  123.9 0.8 fusion.21
  (102 shorter events, 10.3 us)
Async XLA Ops:
  0.6 6.3 %copy-start.3 = (bf16[512,448]{0,1:T(8,128)(2,1)S(1)}, bf16[512,448]{0,1:T(8,128)(2,1)}, u32[]{:S(2)}) copy-start(bf16[512,448]{0,1:T(8,128)(2,1)} %param.11) | copy-start | bytes 1376260
  0.6 7.4 %collective-permute-start.2 = (bf16[128,448]{0,1:T(8,128)(2,1)}, bf16[128,448]{0,1:T(8,128)(2,1)S(1)}, u32[]{:S(2)}, u32[]{:S(2)}) collective-permute-start(bf16[128,448]{0,1:T(8,128)(2,1)} %param.7), channel_id=1, source_target_pairs={{128,0},{192,64},{0,128},{64,192},{129,1},{193,65},{1,129},{65,193... | collective-permute-start | bytes 344072 | tf_op jit(solution)/shard_map/ppermute | solution.py:17
  3.8 6.1 %collective-permute-start = (bf16[128,448]{0,1:T(8,128)(2,1)}, bf16[128,448]{0,1:T(8,128)(2,1)S(1)}, u32[]{:S(2)}, u32[]{:S(2)}) collective-permute-start(bf16[128,448]{0,1:T(8,128)(2,1)} %param.7), channel_id=1, source_target_pairs={{0,192},{4,68},{64,0},{68,132},{128,64},{132,196},{192,128},{196,4... | collective-permute-start | bytes 344072 | tf_op jit(solution)/shard_map/ppermute | solution.py:27
  4.9 6.2 %collective-permute-start.1 = (bf16[128,448]{0,1:T(8,128)(2,1)}, bf16[128,448]{0,1:T(8,128)(2,1)S(1)}, u32[]{:S(2)}, u32[]{:S(2)}) collective-permute-start(bf16[128,448]{0,1:T(8,128)(2,1)} %param.7), channel_id=1, source_target_pairs={{0,64},{4,196},{64,128},{68,4},{128,192},{132,68},{192,0},{196,132... | collective-permute-start | bytes 344072 | tf_op jit(solution)/shard_map/ppermute | solution.py:27
  5.8 7.0 %collective-permute-start.4 = (bf16[448,512]{1,0:T(8,128)(2,1)}, bf16[448,512]{1,0:T(8,128)(2,1)S(1)}, u32[]{:S(2)}, u32[]{:S(2)}) collective-permute-start(bf16[448,512]{1,0:T(8,128)(2,1)} %param.9), channel_id=1, source_target_pairs={{0,4},{4,0},{1,5},{5,1},{2,6},{6,2},{3,7},{7,3},{8,12},{12,8},{9,1... | collective-permute-start | bytes 1376264 | tf_op jit(solution)/shard_map/ppermute | solution.py:31
  6.7 1.2 copy-start.6
  6.9 6.2 %copy-start.4 = (bf16[448,512]{1,0:T(8,128)(2,1)S(1)}, bf16[448,512]{1,0:T(8,128)(2,1)}, u32[]{:S(2)}) copy-start(bf16[448,512]{1,0:T(8,128)(2,1)} %param.9) | copy-start | bytes 1376260
  11.2 1.6 %collective-permute-start.3 = (bf16[256,448]{0,1:T(8,128)(2,1)S(1)}, bf16[256,448]{0,1:T(8,128)(2,1)S(1)}, u32[]{:S(2)}, u32[]{:S(2)}) collective-permute-start(bf16[256,448]{0,1:T(8,128)(2,1)S(1)} %slice.224), channel_id=1, source_target_pairs={{0,4},{4,0},{1,5},{5,1},{2,6},{6,2},{3,7},{7,3},{8,12},{12,8},{9,1... | collective-permute-start | bytes 688136 | tf_op jit(solution)/shard_map/ppermute | solution.py:31
  13.1 26.1 %copy-start.8 = (f32[512]{0:T(512)S(1)}, f32[512]{0:T(512)}, u32[]{:S(2)}) copy-start(f32[512]{0:T(512)} %param.10) | copy-start | bytes 6148
  14.3 24.9 %all-to-all-start = ((f32[8,32,512]{2,1,0:T(8,128)}), f32[8,32,512]{2,1,0:T(8,128)S(1)}, u32[]{:S(2)}, u32[]{:S(2)}) async-start(f32[8,32,512]{2,1,0:T(8,128)} %bitcast), calls=%async_computation | async-start | bytes 1048576 | tf_op jit(solution)/shard_map/all_to_all | solution.py:51
  22.8 17.1 %collective-permute-start.6 = (bf16[512,464]{0,1:T(8,128)(2,1)}, bf16[512,464]{0,1:T(8,128)(2,1)}, u32[]{:S(2)}, u32[]{:S(2)}) collective-permute-start(bf16[512,464]{0,1:T(8,128)(2,1)} %get-tuple-element.26), channel_id=1, source_target_pairs={{0,64},{4,196},{64,128},{68,4},{128,192},{132,68},{192,0},{196,132... | collective-permute-start | bytes 1425416 | tf_op jit(solution)/shard_map/ppermute | solution.py:27
  23.1 16.8 %collective-permute-start.7 = (bf16[512,464]{0,1:T(8,128)(2,1)}, bf16[512,464]{0,1:T(8,128)(2,1)S(1)}, u32[]{:S(2)}, u32[]{:S(2)}) collective-permute-start(bf16[512,464]{0,1:T(8,128)(2,1)} %get-tuple-element.26), channel_id=1, source_target_pairs={{0,192},{4,68},{64,0},{68,132},{128,64},{132,196},{192,128},{196,4... | collective-permute-start | bytes 1425416 | tf_op jit(solution)/shard_map/ppermute | solution.py:27
  39.3 3.1 %collective-permute-start.5 = (bf16[32,512]{1,0:T(8,128)(2,1)S(1)}, bf16[32,512]{1,0:T(8,128)(2,1)S(1)}, u32[]{:S(2)}, u32[]{:S(2)}) collective-permute-start(bf16[32,512]{1,0:T(8,128)(2,1)S(1)} %maximum_convert_fusion), channel_id=1, source_target_pairs={{0,0},{4,132},{8,8},{12,140},{16,16},{20,148},{24,24},{28,156},{32... | collective-permute-start | bytes 98312 | tf_op jit(solution)/shard_map/ppermute | solution.py:43
  43.0 18.9 %all-to-all-start.1 = ((bf16[8,32,512]{2,1,0:T(8,128)(2,1)}), bf16[8,32,512]{2,1,0:T(8,128)(2,1)}, u32[]{:S(2)}, u32[]{:S(2)}) async-start(bf16[8,32,512]{2,1,0:T(8,128)(2,1)} %broadcast_in_dim.24), calls=%async_computation.1 | async-start | bytes 524288 | tf_op jit(solution)/shard_map/all_to_all | solution.py:51
  50.4 10.1 %collective-permute-start.10 = (bf16[512,240]{0,1:T(8,128)(2,1)}, bf16[512,240]{0,1:T(8,128)(2,1)S(1)}, u32[]{:S(2)}, u32[]{:S(2)}) collective-permute-start(bf16[512,240]{0,1:T(8,128)(2,1)} %slice.174), channel_id=1, source_target_pairs={{0,192},{4,68},{64,0},{68,132},{128,64},{132,196},{192,128},{196,4... | collective-permute-start | bytes 737288 | tf_op jit(solution)/shard_map/ppermute | solution.py:27
  51.0 9.6 %collective-permute-start.9 = (bf16[512,224]{0,1:T(8,128)(2,1)}, bf16[512,224]{0,1:T(8,128)(2,1)S(1)}, u32[]{:S(2)}, u32[]{:S(2)}) collective-permute-start(bf16[512,224]{0,1:T(8,128)(2,1)} %slice.173), channel_id=1, source_target_pairs={{0,64},{4,196},{64,128},{68,4},{128,192},{132,68},{192,0},{196,132... | collective-permute-start | bytes 688136 | tf_op jit(solution)/shard_map/ppermute | solution.py:27
  52.5 11.2 %copy-start = (bf16[128,2048]{1,0:T(8,128)(2,1)S(1)}, bf16[128,2048]{1,0:T(8,128)(2,1)}, u32[]{:S(2)}) copy-start(bf16[128,2048]{1,0:T(8,128)(2,1)} %shard_map.102) | copy-start | bytes 1572868
  61.9 1.7 %collective-permute-start.8 = (bf16[2,128,512]{2,1,0:T(8,128)(2,1)}, bf16[2,128,512]{2,1,0:T(8,128)(2,1)S(1)}, u32[]{:S(2)}, u32[]{:S(2)}) collective-permute-start(bf16[2,128,512]{2,1,0:T(8,128)(2,1)} %bitcast.4), channel_id=1, source_target_pairs={{0,4},{4,0},{1,5},{5,1},{2,6},{6,2},{3,7},{7,3},{8,12},{12,8},{9,1... | collective-permute-start | bytes 786440 | tf_op jit(solution)/shard_map/ppermute | solution.py:31
  63.9 0.8 copy-start.1
  63.9 1.0 copy-start.7
  66.3 1.6 %collective-permute-start.11 = (bf16[128,1024]{1,0:T(8,128)(2,1)S(1)}, bf16[128,1024]{1,0:T(8,128)(2,1)S(1)}, u32[]{:S(2)}, u32[]{:S(2)}) collective-permute-start(bf16[128,1024]{1,0:T(8,128)(2,1)S(1)} %fusion.5), channel_id=1, source_target_pairs={{0,4},{4,0},{1,5},{5,1},{2,6},{6,2},{3,7},{7,3},{8,12},{12,8},{9,1... | collective-permute-start | bytes 786440 | tf_op jit(solution)/shard_map/ppermute | solution.py:31
  67.2 7.9 %copy-start.2 = (bf16[128,2048]{1,0:T(8,128)(2,1)S(1)}, bf16[128,2048]{1,0:T(8,128)(2,1)}, u32[]{:S(2)}) copy-start(bf16[128,2048]{1,0:T(8,128)(2,1)} %copy-done.1) | copy-start | bytes 1572868
  67.2 7.9 %copy-start.5 = (bf16[256,464]{0,1:T(8,128)(2,1)S(1)}, bf16[256,464]{0,1:T(8,128)(2,1)}, u32[]{:S(2)}) copy-start(bf16[256,464]{0,1:T(8,128)(2,1)} %fusion.18) | copy-start | bytes 712708
  69.1 17.1 %all-to-all-start.2 = ((bf16[8,136,128]{2,1,0:T(8,128)(2,1)}), bf16[8,136,128]{2,1,0:T(8,128)(2,1)S(1)}, u32[]{:S(2)}, u32[]{:S(2)}) async-start(bf16[8,136,128]{2,1,0:T(8,128)(2,1)} %pad_maximum_fusion.2), calls=%async_computation.2 | async-start | bytes 557056 | tf_op jit(solution)/shard_map/all_to_all | solution.py:51
  76.1 21.2 %collective-permute-start.15 = (bf16[112,2048]{1,0:T(8,128)(2,1)S(1)}, bf16[112,2048]{1,0:T(8,128)(2,1)}, u32[]{:S(2)}, u32[]{:S(2)}) collective-permute-start(bf16[112,2048]{1,0:T(8,128)(2,1)S(1)} %get-tuple-element.52), channel_id=1, source_target_pairs={{3,0},{0,1},{1,2},{2,3},{7,4},{4,5},{5,6},{6,7},{11,8},{8,9},{9,10... | collective-permute-start | bytes 1376264 | tf_op jit(solution)/shard_map/ppermute | solution.py:17
  77.7 20.9 %collective-permute-start.16 = (bf16[112,2048]{1,0:T(8,128)(2,1)S(1)}, bf16[112,2048]{1,0:T(8,128)(2,1)}, u32[]{:S(2)}, u32[]{:S(2)}) collective-permute-start(bf16[112,2048]{1,0:T(8,128)(2,1)S(1)} %get-tuple-element.51), channel_id=1, source_target_pairs={{1,0},{2,1},{3,2},{0,3},{5,4},{6,5},{7,6},{4,7},{9,8},{10,9},{11,1... | collective-permute-start | bytes 1376264 | tf_op jit(solution)/shard_map/ppermute | solution.py:17
  79.4 21.1 %collective-permute-start.17 = (bf16[112,2048]{1,0:T(8,128)(2,1)S(1)}, bf16[112,2048]{1,0:T(8,128)(2,1)}, u32[]{:S(2)}, u32[]{:S(2)}) collective-permute-start(bf16[112,2048]{1,0:T(8,128)(2,1)S(1)} %get-tuple-element.50), channel_id=1, source_target_pairs={{2,0},{3,1},{0,2},{1,3},{6,4},{7,5},{4,6},{5,7},{10,8},{11,9},{8,1... | collective-permute-start | bytes 1376264 | tf_op jit(solution)/shard_map/ppermute | solution.py:17
  86.2 0.7 collective-permute-start.12
  87.7 18.2 %all-to-all-start.3 = ((bf16[8,32,512]{2,1,0:T(8,128)(2,1)}), bf16[8,32,512]{2,1,0:T(8,128)(2,1)S(1)}, u32[]{:S(2)}, u32[]{:S(2)}) async-start(bf16[8,32,512]{2,1,0:T(8,128)(2,1)} %broadcast_in_dim.28), calls=%async_computation.3 | async-start | bytes 524288 | tf_op jit(solution)/shard_map/all_to_all | solution.py:51
  96.1 6.1 %collective-permute-start.14 = (f32[1,128]{1,0:T(1,128)S(1)}, f32[1,128]{1,0:T(1,128)S(1)}, u32[]{:S(2)}, u32[]{:S(2)}) collective-permute-start(f32[1,128]{1,0:T(1,128)S(1)} %slice_add_fusion.2), channel_id=1, source_target_pairs={{0,4},{4,0},{1,5},{5,1},{2,6},{6,2},{3,7},{7,3},{8,12},{12,8},{9,1... | collective-permute-start | bytes 1544 | tf_op jit(solution)/shard_map/ppermute | solution.py:31
  102.3 5.8 %collective-permute-start.18 = (bf16[120,512]{1,0:T(8,128)(2,1)S(1)}, bf16[120,512]{1,0:T(8,128)(2,1)S(1)}, u32[]{:S(2)}, u32[]{:S(2)}) collective-permute-start(bf16[120,512]{1,0:T(8,128)(2,1)S(1)} %get-tuple-element.75), channel_id=1, source_target_pairs={{0,192},{4,68},{64,0},{68,132},{128,64},{132,196},{192,128},{196,4... | collective-permute-start | bytes 368648 | tf_op jit(solution)/shard_map/ppermute | solution.py:27
  102.6 8.7 %collective-permute-start.19 = (bf16[120,512]{1,0:T(8,128)(2,1)S(1)}, bf16[120,512]{1,0:T(8,128)(2,1)S(1)}, u32[]{:S(2)}, u32[]{:S(2)}) collective-permute-start(bf16[120,512]{1,0:T(8,128)(2,1)S(1)} %get-tuple-element.76), channel_id=1, source_target_pairs={{0,64},{4,196},{64,128},{68,4},{128,192},{132,68},{192,0},{196,132... | collective-permute-start | bytes 368648 | tf_op jit(solution)/shard_map/ppermute | solution.py:27
  104.4 6.9 %collective-permute-start.20 = (bf16[120,512]{1,0:T(8,128)(2,1)S(1)}, bf16[120,512]{1,0:T(8,128)(2,1)S(1)}, u32[]{:S(2)}, u32[]{:S(2)}) collective-permute-start(bf16[120,512]{1,0:T(8,128)(2,1)S(1)} %get-tuple-element.74), channel_id=1, source_target_pairs={{128,0},{192,64},{0,128},{64,192},{129,1},{193,65},{1,129},{65,193... | collective-permute-start | bytes 368648 | tf_op jit(solution)/shard_map/ppermute | solution.py:17
  105.9 5.5 %collective-permute-start.13 = (bf16[256,512]{1,0:T(8,128)(2,1)S(1)}, bf16[256,512]{1,0:T(8,128)(2,1)S(1)}, u32[]{:S(2)}, u32[]{:S(2)}) collective-permute-start(bf16[256,512]{1,0:T(8,128)(2,1)S(1)} %bitcast.56), channel_id=1, source_target_pairs={{0,4},{4,0},{1,5},{5,1},{2,6},{6,2},{3,7},{7,3},{8,12},{12,8},{9,1... | collective-permute-start | bytes 786440 | tf_op jit(solution)/shard_map/ppermute | solution.py:31
  112.2 7.5 %collective-permute-start.21 = (bf16[120,512]{1,0:T(8,128)(2,1)S(1)}, bf16[120,512]{1,0:T(8,128)(2,1)S(1)}, u32[]{:S(2)}, u32[]{:S(2)}) collective-permute-start(bf16[120,512]{1,0:T(8,128)(2,1)S(1)} %get-tuple-element.60), channel_id=1, source_target_pairs={{3,0},{0,1},{1,2},{2,3},{7,4},{4,5},{5,6},{6,7},{11,8},{8,9},{9,10... | collective-permute-start | bytes 368648 | tf_op jit(solution)/shard_map/ppermute | solution.py:17
  113.5 6.2 %collective-permute-start.22 = (bf16[120,512]{1,0:T(8,128)(2,1)S(1)}, bf16[120,512]{1,0:T(8,128)(2,1)S(1)}, u32[]{:S(2)}, u32[]{:S(2)}) collective-permute-start(bf16[120,512]{1,0:T(8,128)(2,1)S(1)} %get-tuple-element.59), channel_id=1, source_target_pairs={{1,0},{2,1},{3,2},{0,3},{5,4},{6,5},{7,6},{4,7},{9,8},{10,9},{11,1... | collective-permute-start | bytes 368648 | tf_op jit(solution)/shard_map/ppermute | solution.py:17
  115.6 6.4 %collective-permute-start.23 = (bf16[120,512]{1,0:T(8,128)(2,1)S(1)}, bf16[120,512]{1,0:T(8,128)(2,1)S(1)}, u32[]{:S(2)}, u32[]{:S(2)}) collective-permute-start(bf16[120,512]{1,0:T(8,128)(2,1)S(1)} %get-tuple-element.58), channel_id=1, source_target_pairs={{2,0},{3,1},{0,2},{1,3},{6,4},{7,5},{4,6},{5,7},{10,8},{11,9},{8,1... | collective-permute-start | bytes 368648 | tf_op jit(solution)/shard_map/ppermute | solution.py:17

commit v6 on v5

--- a/solution.py
+++ b/solution.py
@@ -159,16 +159,14 @@
     preact = jnp.sum(parts, axis=0) + enc_bias[None, :]
     lat_piece = jnp.maximum(preact, 0.0).astype(BF16)
     lat_piece, picked = lax.optimization_barrier((lat_piece, picked))
-    dec_1, dec_3 = after((dec_1, dec_3), lat_piece)
     lat_piece = shift_pieces(lat_piece, 1)
-    lat_piece, passed_1, passed_3 = lax.optimization_barrier(
-        (lat_piece, dec_1[:, :half], dec_3[:, half:])
-    )
-    dec_2 = [blk_move(passed_1, 1, 1), blk_move(passed_3, 3, 1)]
+    lat_copies = z_copies(lat_piece)
+    dec_1, dec_3 = after((dec_1, dec_3), lat_copies)
+    dec_2 = [blk_move(dec_1[:, :half], 1, 1), blk_move(dec_3[:, half:], 3, 1)]
     dec_all = in_slots(dec_own, dec_1, jnp.concatenate(dec_2, 1), dec_3)
     gate = picked * dec_all[:, width][None, :]
 
-    lat_mine = exchange_z(z_copies(lat_piece)).reshape(2, rows, lat)
+    lat_mine = exchange_z(lat_copies).reshape(2, rows, lat)
     lat_other = swap_core(lat_mine)
     latents = jnp.concatenate([lat_mine[0], lat_mine[1], lat_other[0], lat_other[1]], 1)
     both = jnp.concatenate([latents, latents * gate], 0)

time: 125 us -> 126 us (level)
  starting transfers between devices: 56.6 us -> 59.5 us
  local copies, waits for them, and re-layouts: 7.8 us -> 6.41 us
    all_to_all x4, starting transfers between devices: 30.2 us -> 32.5 us  [exchange_z(): return lax.all_to_all(copies, 'z', 0, 0, tiled=True)]
    slice x2, local copies, waits for them, and re-layouts: 2.36 us -> 0.97 us  [local(): dec_2 = [blk_move(dec_1[:, :half], 1, 1), blk_move(dec_3[:, half:], 3, 1)]]
  transfers between devices with their start and end apart: 28 -> 28, of which waited for: 17 -> 18; matrix products, arithmetic and copies ran while one was open for 10% -> 9% of each run, Pallas kernels for 5% -> 5%
where the time goes in v6:
time: 126 us; the launch traced here: 125 us
  starting transfers between devices  59.5 us (47%)
  waiting for transfers between devices  39 us (31%)
  other arithmetic  7.87 us (6%)
  Pallas kernels  7.01 us (6%)
  local copies, waits for them, and re-layouts  6.41 us (5%)
  matrix products  4.18 us (3%)
    all_to_all x4, starting transfers between devices, exchange_z(): return lax.all_to_all(copies, 'z', 0, 0, tiled=True)  32.5 us
    all_to_all x4, waiting for transfers between devices, exchange_z(): return lax.all_to_all(copies, 'z', 0, 0, tiled=True)  14.5 us
    ppermute x8, waiting for transfers between devices, blk_move(): return lax.ppermute(block, ('blk', 'core'), route)  12.7 us
    ppermute x8, starting transfers between devices, from_ahead(): lax.ppermute(block, axis, [((i + distance) % size, i) for i in range(size)])  12.3 us
    ppermute x8, starting transfers between devices, blk_move(): return lax.ppermute(block, ('blk', 'core'), route)  9.55 us
    ppermute x8, waiting for transfers between devices, from_ahead(): lax.ppermute(block, axis, [((i + distance) % size, i) for i in range(size)])  8.93 us
    pallas_call x1, Pallas kernels, picked_latents(): pl.pallas_call(pick_kernel, out_shape=jax.ShapeDtypeStruct((rows, lat_all...  5.69 us
    ppermute x6, starting transfers between devices, swap_core(): return lax.ppermute(block, 'core', [(0, 1), (1, 0)])  3.74 us
  transfers between devices with their start and end apart: 28, of which 18 were waited for; matrix products, arithmetic and copies ran while one was open for 9% of the time, Pallas kernels for 5%

profile of v6, /device:TPU:32, one launch (start us, length us, event | category | flops | bytes accessed | tf_op | source)
XLA Modules:
  0.0 125.0 jit_solution(1911277254704479847)
XLA Ops:
  0.6 3.1 %collective-permute-start.2 = (bf16[128,448]{0,1:T(8,128)(2,1)}, bf16[128,448]{0,1:T(8,128)(2,1)S(1)}, u32[]{:S(2)}, u32[]{:S(2)}) collective-permute-start(bf16[128,448]{0,1:T(8,128)(2,1)} %param.7), channel_id=1, source_target_pairs={{128,0},{192,64},{0,128},{64,192},{129,1},{193,65},{1,129},{65,193... | collective-permute-start | bytes 344072 | tf_op jit(solution)/shard_map/ppermute | solution.py:17
  3.8 1.1 collective-permute-start
  4.9 0.9 collective-permute-start.1
  6.0 0.7 convert_element_type.168
  6.9 0.9 constant_dynamic-update-slice_fusion.2
  8.0 1.9 %collective-permute-done = bf16[128,448]{0,1:T(8,128)(2,1)S(1)} collective-permute-done((bf16[128,448]{0,1:T(8,128)(2,1)}, bf16[128,448]{0,1:T(8,128)(2,1)S(1)}, u32[]{:S(2)}, u32[]{:S(2)}) %collective-permute-start) | collective-permute-done | bytes 114720 | tf_op jit(solution)/shard_map/ppermute | solution.py:27
  9.9 1.2 collective-permute-done.1
  11.3 1.5 %collective-permute-done.3 = bf16[256,448]{0,1:T(8,128)(2,1)S(1)} collective-permute-done((bf16[256,448]{0,1:T(8,128)(2,1)S(1)}, bf16[256,448]{0,1:T(8,128)(2,1)S(1)}, u32[]{:S(2)}, u32[]{:S(2)}) %collective-permute-start.3) | collective-permute-done | bytes 229408 | tf_op jit(solution)/shard_map/ppermute | solution.py:31
  13.1 1.1 convolution_add_fusion
  14.3 8.6 %all-to-all-start = ((f32[8,32,512]{2,1,0:T(8,128)}), f32[8,32,512]{2,1,0:T(8,128)S(1)}, u32[]{:S(2)}, u32[]{:S(2)}) async-start(f32[8,32,512]{2,1,0:T(8,128)} %bitcast), calls=%async_computation | async-start | bytes 1048576 | tf_op jit(solution)/shard_map/all_to_all | solution.py:51
  23.1 3.0 %collective-permute-start.8 = (bf16[512,464]{0,1:T(8,128)(2,1)}, bf16[512,464]{0,1:T(8,128)(2,1)S(1)}, u32[]{:S(2)}, u32[]{:S(2)}) collective-permute-start(bf16[512,464]{0,1:T(8,128)(2,1)} %get-tuple-element.24), channel_id=1, source_target_pairs={{0,192},{4,68},{64,0},{68,132},{128,64},{132,196},{192,128},{196,4... | collective-permute-start | bytes 1425416 | tf_op jit(solution)/shard_map/ppermute | solution.py:27
  26.1 5.7 %shard_map.102 = bf16[128,2048]{1,0:T(8,128)(2,1)} custom-call(s32[1]{0:T(128)} %bitcast.1.own_ref, s32[128,512]{1,0:T(8,128)} %picks_ref.1), custom_call_target="tpu_custom_call" | custom-call | flops 20000000 | bytes 1000000 | tf_op jit(solution)/shard_map/pallas_call | solution.py:82
  31.8 7.4 %all-to-all-done = f32[8,32,512]{2,1,0:T(8,128)S(1)} async-done(((f32[8,32,512]{2,1,0:T(8,128)}), f32[8,32,512]{2,1,0:T(8,128)S(1)}, u32[]{:S(2)}, u32[]{:S(2)}) %all-to-all-start) | async-done | bytes 524320 | tf_op jit(solution)/shard_map/all_to_all | solution.py:51
  39.9 0.7 broadcast_in_dim.24
  40.7 9.6 %all-to-all-start.1 = ((bf16[8,32,512]{2,1,0:T(8,128)(2,1)}), bf16[8,32,512]{2,1,0:T(8,128)(2,1)}, u32[]{:S(2)}, u32[]{:S(2)}) async-start(bf16[8,32,512]{2,1,0:T(8,128)(2,1)} %broadcast_in_dim.24), calls=%async_computation.1 | async-start | bytes 524288 | tf_op jit(solution)/shard_map/all_to_all | solution.py:51
  51.0 1.0 slice.177
  52.0 1.6 %collective-permute-start.9 = (bf16[512,224]{0,1:T(8,128)(2,1)S(1)}, bf16[512,224]{0,1:T(8,128)(2,1)S(1)}, u32[]{:S(2)}, u32[]{:S(2)}) collective-permute-start(bf16[512,224]{0,1:T(8,128)(2,1)S(1)} %slice.177), channel_id=1, source_target_pairs={{0,64},{4,196},{64,128},{68,4},{128,192},{132,68},{192,0},{196,132... | collective-permute-start | bytes 688136 | tf_op jit(solution)/shard_map/ppermute | solution.py:27
  53.6 1.1 constant_dynamic-update-slice_fusion.1
  54.8 5.6 %collective-permute-done.9 = bf16[512,224]{0,1:T(8,128)(2,1)S(1)} collective-permute-done((bf16[512,224]{0,1:T(8,128)(2,1)S(1)}, bf16[512,224]{0,1:T(8,128)(2,1)S(1)}, u32[]{:S(2)}, u32[]{:S(2)}) %collective-permute-start.9) | collective-permute-done | bytes 229408 | tf_op jit(solution)/shard_map/ppermute | solution.py:27
  60.5 1.4 %all-to-all-done.1 = bf16[8,32,512]{2,1,0:T(8,128)(2,1)} async-done(((bf16[8,32,512]{2,1,0:T(8,128)(2,1)}), bf16[8,32,512]{2,1,0:T(8,128)(2,1)}, u32[]{:S(2)}, u32[]{:S(2)}) %all-to-all-start.1) | async-done | bytes 262176 | tf_op jit(solution)/shard_map/all_to_all | solution.py:51
  62.1 1.0 fusion.35
  63.9 0.7 fusion.32
  65.5 0.7 fusion.18
  67.2 0.7 collective-permute-done.11
  68.3 0.7 pad_maximum_fusion.2
  69.1 5.9 %all-to-all-start.2 = ((bf16[8,136,128]{2,1,0:T(8,128)(2,1)}), bf16[8,136,128]{2,1,0:T(8,128)(2,1)S(1)}, u32[]{:S(2)}, u32[]{:S(2)}) async-start(bf16[8,136,128]{2,1,0:T(8,128)(2,1)} %pad_maximum_fusion.2), calls=%async_computation.2 | async-start | bytes 557056 | tf_op jit(solution)/shard_map/all_to_all | solution.py:51
  76.0 1.6 %collective-permute-start.15 = (bf16[112,2048]{1,0:T(8,128)(2,1)S(1)}, bf16[112,2048]{1,0:T(8,128)(2,1)}, u32[]{:S(2)}, u32[]{:S(2)}) collective-permute-start(bf16[112,2048]{1,0:T(8,128)(2,1)S(1)} %get-tuple-element.46), channel_id=1, source_target_pairs={{3,0},{0,1},{1,2},{2,3},{7,4},{4,5},{5,6},{6,7},{11,8},{8,9},{9,10... | collective-permute-start | bytes 1376264 | tf_op jit(solution)/shard_map/ppermute | solution.py:17
  77.6 1.7 %collective-permute-start.16 = (bf16[112,2048]{1,0:T(8,128)(2,1)S(1)}, bf16[112,2048]{1,0:T(8,128)(2,1)}, u32[]{:S(2)}, u32[]{:S(2)}) collective-permute-start(bf16[112,2048]{1,0:T(8,128)(2,1)S(1)} %get-tuple-element.45), channel_id=1, source_target_pairs={{1,0},{2,1},{3,2},{0,3},{5,4},{6,5},{7,6},{4,7},{9,8},{10,9},{11,1... | collective-permute-start | bytes 1376264 | tf_op jit(solution)/shard_map/ppermute | solution.py:17
  79.3 2.0 %collective-permute-start.17 = (bf16[112,2048]{1,0:T(8,128)(2,1)S(1)}, bf16[112,2048]{1,0:T(8,128)(2,1)}, u32[]{:S(2)}, u32[]{:S(2)}) collective-permute-start(bf16[112,2048]{1,0:T(8,128)(2,1)S(1)} %get-tuple-element.44), channel_id=1, source_target_pairs={{2,0},{3,1},{0,2},{1,3},{6,4},{7,5},{4,6},{5,7},{10,8},{11,9},{8,1... | collective-permute-start | bytes 1376264 | tf_op jit(solution)/shard_map/ppermute | solution.py:17
  81.3 4.8 %all-to-all-done.2 = bf16[8,136,128]{2,1,0:T(8,128)(2,1)S(1)} async-done(((bf16[8,136,128]{2,1,0:T(8,128)(2,1)}), bf16[8,136,128]{2,1,0:T(8,128)(2,1)S(1)}, u32[]{:S(2)}, u32[]{:S(2)}) %all-to-all-start.2) | async-done | bytes 278560 | tf_op jit(solution)/shard_map/all_to_all | solution.py:51
  86.8 0.7 broadcast_in_dim.28
  87.6 8.4 %all-to-all-start.3 = ((bf16[8,32,512]{2,1,0:T(8,128)(2,1)}), bf16[8,32,512]{2,1,0:T(8,128)(2,1)S(1)}, u32[]{:S(2)}, u32[]{:S(2)}) async-start(bf16[8,32,512]{2,1,0:T(8,128)(2,1)} %broadcast_in_dim.28), calls=%async_computation.3 | async-start | bytes 524288 | tf_op jit(solution)/shard_map/all_to_all | solution.py:51
  96.0 1.2 collective-permute-start.14
  97.2 1.3 %collective-permute-done.16 = bf16[112,2048]{1,0:T(8,128)(2,1)} collective-permute-done((bf16[112,2048]{1,0:T(8,128)(2,1)S(1)}, bf16[112,2048]{1,0:T(8,128)(2,1)}, u32[]{:S(2)}, u32[]{:S(2)}) %collective-permute-start.16) | collective-permute-done | bytes 458784 | tf_op jit(solution)/shard_map/ppermute | solution.py:17
  98.6 1.9 %collective-permute-done.17 = bf16[112,2048]{1,0:T(8,128)(2,1)} collective-permute-done((bf16[112,2048]{1,0:T(8,128)(2,1)S(1)}, bf16[112,2048]{1,0:T(8,128)(2,1)}, u32[]{:S(2)}, u32[]{:S(2)}) %collective-permute-start.17) | collective-permute-done | bytes 458784 | tf_op jit(solution)/shard_map/ppermute | solution.py:17
  100.4 1.6 %add_convert_fusion = bf16[112,2048]{1,0:T(8,128)(2,1)S(1)} fusion(bf16[112,2048]{1,0:T(8,128)(2,1)} %collective-permute-done.17, bf16[112,2048]{1,0:T(8,128)(2,1)} %collective-permute-done.16, bf16[112,2048]{1,0:T(8,128)(2,1)} %collective-permute-done.15, bf16[112,2048]{1,0:T(8,128)(2,1)S(1)} %get-tuple-element.29), kind=kLoop, calls=%fused_computation.8 | loop fusion | flops 1835008 | bytes 2293760 | tf_op jit(solution)/shard_map/convert_element_type | solution.py:229
  102.2 1.1 collective-permute-start.18
  103.3 1.0 collective-permute-start.19
  104.9 0.9 all-to-all-done.3
  105.8 1.8 %collective-permute-start.13 = (bf16[256,512]{1,0:T(8,128)(2,1)S(1)}, bf16[256,512]{1,0:T(8,128)(2,1)S(1)}, u32[]{:S(2)}, u32[]{:S(2)}) collective-permute-start(bf16[256,512]{1,0:T(8,128)(2,1)S(1)} %bitcast.56), channel_id=1, source_target_pairs={{0,4},{4,0},{1,5},{5,1},{2,6},{6,2},{3,7},{7,3},{8,12},{12,8},{9,1... | collective-permute-start | bytes 786440 | tf_op jit(solution)/shard_map/ppermute | solution.py:31
  108.0 3.7 %collective-permute-done.19 = bf16[120,512]{1,0:T(8,128)(2,1)S(1)} collective-permute-done((bf16[120,512]{1,0:T(8,128)(2,1)S(1)}, bf16[120,512]{1,0:T(8,128)(2,1)S(1)}, u32[]{:S(2)}, u32[]{:S(2)}) %collective-permute-start.19) | collective-permute-done | bytes 122912 | tf_op jit(solution)/shard_map/ppermute | solution.py:27
  112.6 1.2 collective-permute-start.21
  113.9 2.1 %collective-permute-start.22 = (bf16[120,512]{1,0:T(8,128)(2,1)S(1)}, bf16[120,512]{1,0:T(8,128)(2,1)S(1)}, u32[]{:S(2)}, u32[]{:S(2)}) collective-permute-start(bf16[120,512]{1,0:T(8,128)(2,1)S(1)} %get-tuple-element.53), channel_id=1, source_target_pairs={{1,0},{2,1},{3,2},{0,3},{5,4},{6,5},{7,6},{4,7},{9,8},{10,9},{11,1... | collective-permute-start | bytes 368648 | tf_op jit(solution)/shard_map/ppermute | solution.py:17
  116.0 0.7 add_bitcast_fusion
  116.8 2.9 %collective-permute-done.21 = bf16[120,512]{1,0:T(8,128)(2,1)S(1)} collective-permute-done((bf16[120,512]{1,0:T(8,128)(2,1)S(1)}, bf16[120,512]{1,0:T(8,128)(2,1)S(1)}, u32[]{:S(2)}, u32[]{:S(2)}) %collective-permute-start.21) | collective-permute-done | bytes 122912 | tf_op jit(solution)/shard_map/ppermute | solution.py:17
  119.7 2.6 %collective-permute-done.23 = bf16[120,512]{1,0:T(8,128)(2,1)S(1)} collective-permute-done((bf16[120,512]{1,0:T(8,128)(2,1)S(1)}, bf16[120,512]{1,0:T(8,128)(2,1)S(1)}, u32[]{:S(2)}, u32[]{:S(2)}) %collective-permute-start.23) | collective-permute-done | bytes 122912 | tf_op jit(solution)/shard_map/ppermute | solution.py:17
  122.9 1.3 %shard_map.103 = (f32[1,1]{1,0:T(1,128)}, f32[1,128]{1,0:T(1,128)}) custom-call(f32[3,128]{1,0:T(4,128)} %convert_add_fusion.1.last_ref), custom_call_target="tpu_custom_call" | custom-call | tf_op jit(solution)/shard_map/pallas_call | solution.py:116
  124.3 0.8 fusion.21
  (102 shorter events, 10.5 us)
Async XLA Ops:
  0.6 6.3 %copy-start.3 = (bf16[512,448]{0,1:T(8,128)(2,1)S(1)}, bf16[512,448]{0,1:T(8,128)(2,1)}, u32[]{:S(2)}) copy-start(bf16[512,448]{0,1:T(8,128)(2,1)} %param.11) | copy-start | bytes 1376260
  0.6 7.4 %collective-permute-start.2 = (bf16[128,448]{0,1:T(8,128)(2,1)}, bf16[128,448]{0,1:T(8,128)(2,1)S(1)}, u32[]{:S(2)}, u32[]{:S(2)}) collective-permute-start(bf16[128,448]{0,1:T(8,128)(2,1)} %param.7), channel_id=1, source_target_pairs={{128,0},{192,64},{0,128},{64,192},{129,1},{193,65},{1,129},{65,193... | collective-permute-start | bytes 344072 | tf_op jit(solution)/shard_map/ppermute | solution.py:17
  3.8 6.1 %collective-permute-start = (bf16[128,448]{0,1:T(8,128)(2,1)}, bf16[128,448]{0,1:T(8,128)(2,1)S(1)}, u32[]{:S(2)}, u32[]{:S(2)}) collective-permute-start(bf16[128,448]{0,1:T(8,128)(2,1)} %param.7), channel_id=1, source_target_pairs={{0,192},{4,68},{64,0},{68,132},{128,64},{132,196},{192,128},{196,4... | collective-permute-start | bytes 344072 | tf_op jit(solution)/shard_map/ppermute | solution.py:27
  4.9 6.2 %collective-permute-start.1 = (bf16[128,448]{0,1:T(8,128)(2,1)}, bf16[128,448]{0,1:T(8,128)(2,1)S(1)}, u32[]{:S(2)}, u32[]{:S(2)}) collective-permute-start(bf16[128,448]{0,1:T(8,128)(2,1)} %param.7), channel_id=1, source_target_pairs={{0,64},{4,196},{64,128},{68,4},{128,192},{132,68},{192,0},{196,132... | collective-permute-start | bytes 344072 | tf_op jit(solution)/shard_map/ppermute | solution.py:27
  5.8 7.0 %collective-permute-start.4 = (bf16[448,512]{1,0:T(8,128)(2,1)}, bf16[448,512]{1,0:T(8,128)(2,1)S(1)}, u32[]{:S(2)}, u32[]{:S(2)}) collective-permute-start(bf16[448,512]{1,0:T(8,128)(2,1)} %param.9), channel_id=1, source_target_pairs={{0,4},{4,0},{1,5},{5,1},{2,6},{6,2},{3,7},{7,3},{8,12},{12,8},{9,1... | collective-permute-start | bytes 1376264 | tf_op jit(solution)/shard_map/ppermute | solution.py:31
  6.7 1.2 copy-start.6
  6.9 6.2 %copy-start.4 = (bf16[448,512]{1,0:T(8,128)(2,1)S(1)}, bf16[448,512]{1,0:T(8,128)(2,1)}, u32[]{:S(2)}) copy-start(bf16[448,512]{1,0:T(8,128)(2,1)} %param.9) | copy-start | bytes 1376260
  11.2 1.6 %collective-permute-start.3 = (bf16[256,448]{0,1:T(8,128)(2,1)S(1)}, bf16[256,448]{0,1:T(8,128)(2,1)S(1)}, u32[]{:S(2)}, u32[]{:S(2)}) collective-permute-start(bf16[256,448]{0,1:T(8,128)(2,1)S(1)} %slice.224), channel_id=1, source_target_pairs={{0,4},{4,0},{1,5},{5,1},{2,6},{6,2},{3,7},{7,3},{8,12},{12,8},{9,1... | collective-permute-start | bytes 688136 | tf_op jit(solution)/shard_map/ppermute | solution.py:31
  13.1 26.1 %copy-start.8 = (f32[512]{0:T(512)S(1)}, f32[512]{0:T(512)}, u32[]{:S(2)}) copy-start(f32[512]{0:T(512)} %param.10) | copy-start | bytes 6148
  14.3 24.9 %all-to-all-start = ((f32[8,32,512]{2,1,0:T(8,128)}), f32[8,32,512]{2,1,0:T(8,128)S(1)}, u32[]{:S(2)}, u32[]{:S(2)}) async-start(f32[8,32,512]{2,1,0:T(8,128)} %bitcast), calls=%async_computation | async-start | bytes 1048576 | tf_op jit(solution)/shard_map/all_to_all | solution.py:51
  22.8 27.6 %collective-permute-start.7 = (bf16[512,464]{0,1:T(8,128)(2,1)}, bf16[512,464]{0,1:T(8,128)(2,1)}, u32[]{:S(2)}, u32[]{:S(2)}) collective-permute-start(bf16[512,464]{0,1:T(8,128)(2,1)} %get-tuple-element.24), channel_id=1, source_target_pairs={{0,64},{4,196},{64,128},{68,4},{128,192},{132,68},{192,0},{196,132... | collective-permute-start | bytes 1425416 | tf_op jit(solution)/shard_map/ppermute | solution.py:27
  23.1 27.4 %collective-permute-start.8 = (bf16[512,464]{0,1:T(8,128)(2,1)}, bf16[512,464]{0,1:T(8,128)(2,1)S(1)}, u32[]{:S(2)}, u32[]{:S(2)}) collective-permute-start(bf16[512,464]{0,1:T(8,128)(2,1)} %get-tuple-element.24), channel_id=1, source_target_pairs={{0,192},{4,68},{64,0},{68,132},{128,64},{132,196},{192,128},{196,4... | collective-permute-start | bytes 1425416 | tf_op jit(solution)/shard_map/ppermute | solution.py:27
  39.3 0.7 collective-permute-start.5
  40.7 21.3 %all-to-all-start.1 = ((bf16[8,32,512]{2,1,0:T(8,128)(2,1)}), bf16[8,32,512]{2,1,0:T(8,128)(2,1)}, u32[]{:S(2)}, u32[]{:S(2)}) async-start(bf16[8,32,512]{2,1,0:T(8,128)(2,1)} %broadcast_in_dim.24), calls=%async_computation.1 | async-start | bytes 524288 | tf_op jit(solution)/shard_map/all_to_all | solution.py:51
  50.5 10.0 %collective-permute-start.10 = (bf16[512,240]{0,1:T(8,128)(2,1)S(1)}, bf16[512,240]{0,1:T(8,128)(2,1)S(1)}, u32[]{:S(2)}, u32[]{:S(2)}) collective-permute-start(bf16[512,240]{0,1:T(8,128)(2,1)S(1)} %slice.178), channel_id=1, source_target_pairs={{0,192},{4,68},{64,0},{68,132},{128,64},{132,196},{192,128},{196,4... | collective-permute-start | bytes 737288 | tf_op jit(solution)/shard_map/ppermute | solution.py:27
  52.0 8.5 %collective-permute-start.9 = (bf16[512,224]{0,1:T(8,128)(2,1)S(1)}, bf16[512,224]{0,1:T(8,128)(2,1)S(1)}, u32[]{:S(2)}, u32[]{:S(2)}) collective-permute-start(bf16[512,224]{0,1:T(8,128)(2,1)S(1)} %slice.177), channel_id=1, source_target_pairs={{0,64},{4,196},{64,128},{68,4},{128,192},{132,68},{192,0},{196,132... | collective-permute-start | bytes 688136 | tf_op jit(solution)/shard_map/ppermute | solution.py:27
  53.6 10.1 %copy-start = (bf16[128,2048]{1,0:T(8,128)(2,1)S(1)}, bf16[128,2048]{1,0:T(8,128)(2,1)}, u32[]{:S(2)}) copy-start(bf16[128,2048]{1,0:T(8,128)(2,1)} %shard_map.102) | copy-start | bytes 1572868
  61.9 1.7 %collective-permute-start.6 = (bf16[2,128,512]{2,1,0:T(8,128)(2,1)}, bf16[2,128,512]{2,1,0:T(8,128)(2,1)S(1)}, u32[]{:S(2)}, u32[]{:S(2)}) collective-permute-start(bf16[2,128,512]{2,1,0:T(8,128)(2,1)} %bitcast.4), channel_id=1, source_target_pairs={{0,4},{4,0},{1,5},{5,1},{2,6},{6,2},{3,7},{7,3},{8,12},{12,8},{9,1... | collective-permute-start | bytes 786440 | tf_op jit(solution)/shard_map/ppermute | solution.py:31
  63.9 0.8 copy-start.1
  63.9 1.0 copy-start.7
  66.3 1.6 %collective-permute-start.11 = (bf16[128,1024]{1,0:T(8,128)(2,1)S(1)}, bf16[128,1024]{1,0:T(8,128)(2,1)S(1)}, u32[]{:S(2)}, u32[]{:S(2)}) collective-permute-start(bf16[128,1024]{1,0:T(8,128)(2,1)S(1)} %fusion.5), channel_id=1, source_target_pairs={{0,4},{4,0},{1,5},{5,1},{2,6},{6,2},{3,7},{7,3},{8,12},{12,8},{9,1... | collective-permute-start | bytes 786440 | tf_op jit(solution)/shard_map/ppermute | solution.py:31
  67.2 7.8 %copy-start.2 = (bf16[128,2048]{1,0:T(8,128)(2,1)S(1)}, bf16[128,2048]{1,0:T(8,128)(2,1)}, u32[]{:S(2)}) copy-start(bf16[128,2048]{1,0:T(8,128)(2,1)} %copy-done.1) | copy-start | bytes 1572868
  67.2 7.8 %copy-start.5 = (bf16[256,464]{0,1:T(8,128)(2,1)S(1)}, bf16[256,464]{0,1:T(8,128)(2,1)}, u32[]{:S(2)}) copy-start(bf16[256,464]{0,1:T(8,128)(2,1)} %fusion.18) | copy-start | bytes 712708
  69.1 17.0 %all-to-all-start.2 = ((bf16[8,136,128]{2,1,0:T(8,128)(2,1)}), bf16[8,136,128]{2,1,0:T(8,128)(2,1)S(1)}, u32[]{:S(2)}, u32[]{:S(2)}) async-start(bf16[8,136,128]{2,1,0:T(8,128)(2,1)} %pad_maximum_fusion.2), calls=%async_computation.2 | async-start | bytes 557056 | tf_op jit(solution)/shard_map/all_to_all | solution.py:51
  76.0 21.2 %collective-permute-start.15 = (bf16[112,2048]{1,0:T(8,128)(2,1)S(1)}, bf16[112,2048]{1,0:T(8,128)(2,1)}, u32[]{:S(2)}, u32[]{:S(2)}) collective-permute-start(bf16[112,2048]{1,0:T(8,128)(2,1)S(1)} %get-tuple-element.46), channel_id=1, source_target_pairs={{3,0},{0,1},{1,2},{2,3},{7,4},{4,5},{5,6},{6,7},{11,8},{8,9},{9,10... | collective-permute-start | bytes 1376264 | tf_op jit(solution)/shard_map/ppermute | solution.py:17
  77.6 20.9 %collective-permute-start.16 = (bf16[112,2048]{1,0:T(8,128)(2,1)S(1)}, bf16[112,2048]{1,0:T(8,128)(2,1)}, u32[]{:S(2)}, u32[]{:S(2)}) collective-permute-start(bf16[112,2048]{1,0:T(8,128)(2,1)S(1)} %get-tuple-element.45), channel_id=1, source_target_pairs={{1,0},{2,1},{3,2},{0,3},{5,4},{6,5},{7,6},{4,7},{9,8},{10,9},{11,1... | collective-permute-start | bytes 1376264 | tf_op jit(solution)/shard_map/ppermute | solution.py:17
  79.3 21.1 %collective-permute-start.17 = (bf16[112,2048]{1,0:T(8,128)(2,1)S(1)}, bf16[112,2048]{1,0:T(8,128)(2,1)}, u32[]{:S(2)}, u32[]{:S(2)}) collective-permute-start(bf16[112,2048]{1,0:T(8,128)(2,1)S(1)} %get-tuple-element.44), channel_id=1, source_target_pairs={{2,0},{3,1},{0,2},{1,3},{6,4},{7,5},{4,6},{5,7},{10,8},{11,9},{8,1... | collective-permute-start | bytes 1376264 | tf_op jit(solution)/shard_map/ppermute | solution.py:17
  86.1 0.7 collective-permute-start.12
  87.6 18.2 %all-to-all-start.3 = ((bf16[8,32,512]{2,1,0:T(8,128)(2,1)}), bf16[8,32,512]{2,1,0:T(8,128)(2,1)S(1)}, u32[]{:S(2)}, u32[]{:S(2)}) async-start(bf16[8,32,512]{2,1,0:T(8,128)(2,1)} %broadcast_in_dim.28), calls=%async_computation.3 | async-start | bytes 524288 | tf_op jit(solution)/shard_map/all_to_all | solution.py:51
  96.0 6.1 %collective-permute-start.14 = (f32[1,128]{1,0:T(1,128)S(1)}, f32[1,128]{1,0:T(1,128)S(1)}, u32[]{:S(2)}, u32[]{:S(2)}) collective-permute-start(f32[1,128]{1,0:T(1,128)S(1)} %slice_add_fusion.2), channel_id=1, source_target_pairs={{0,4},{4,0},{1,5},{5,1},{2,6},{6,2},{3,7},{7,3},{8,12},{12,8},{9,1... | collective-permute-start | bytes 1544 | tf_op jit(solution)/shard_map/ppermute | solution.py:31
  102.2 5.8 %collective-permute-start.18 = (bf16[120,512]{1,0:T(8,128)(2,1)S(1)}, bf16[120,512]{1,0:T(8,128)(2,1)S(1)}, u32[]{:S(2)}, u32[]{:S(2)}) collective-permute-start(bf16[120,512]{1,0:T(8,128)(2,1)S(1)} %get-tuple-element.69), channel_id=1, source_target_pairs={{0,192},{4,68},{64,0},{68,132},{128,64},{132,196},{192,128},{196,4... | collective-permute-start | bytes 368648 | tf_op jit(solution)/shard_map/ppermute | solution.py:27
  103.3 8.4 %collective-permute-start.19 = (bf16[120,512]{1,0:T(8,128)(2,1)S(1)}, bf16[120,512]{1,0:T(8,128)(2,1)S(1)}, u32[]{:S(2)}, u32[]{:S(2)}) collective-permute-start(bf16[120,512]{1,0:T(8,128)(2,1)S(1)} %get-tuple-element.70), channel_id=1, source_target_pairs={{0,64},{4,196},{64,128},{68,4},{128,192},{132,68},{192,0},{196,132... | collective-permute-start | bytes 368648 | tf_op jit(solution)/shard_map/ppermute | solution.py:27
  104.3 7.4 %collective-permute-start.20 = (bf16[120,512]{1,0:T(8,128)(2,1)S(1)}, bf16[120,512]{1,0:T(8,128)(2,1)S(1)}, u32[]{:S(2)}, u32[]{:S(2)}) collective-permute-start(bf16[120,512]{1,0:T(8,128)(2,1)S(1)} %get-tuple-element.68), channel_id=1, source_target_pairs={{128,0},{192,64},{0,128},{64,192},{129,1},{193,65},{1,129},{65,193... | collective-permute-start | bytes 368648 | tf_op jit(solution)/shard_map/ppermute | solution.py:17
  105.8 6.1 %collective-permute-start.13 = (bf16[256,512]{1,0:T(8,128)(2,1)S(1)}, bf16[256,512]{1,0:T(8,128)(2,1)S(1)}, u32[]{:S(2)}, u32[]{:S(2)}) collective-permute-start(bf16[256,512]{1,0:T(8,128)(2,1)S(1)} %bitcast.56), channel_id=1, source_target_pairs={{0,4},{4,0},{1,5},{5,1},{2,6},{6,2},{3,7},{7,3},{8,12},{12,8},{9,1... | collective-permute-start | bytes 786440 | tf_op jit(solution)/shard_map/ppermute | solution.py:31
  112.6 7.0 %collective-permute-start.21 = (bf16[120,512]{1,0:T(8,128)(2,1)S(1)}, bf16[120,512]{1,0:T(8,128)(2,1)S(1)}, u32[]{:S(2)}, u32[]{:S(2)}) collective-permute-start(bf16[120,512]{1,0:T(8,128)(2,1)S(1)} %get-tuple-element.54), channel_id=1, source_target_pairs={{3,0},{0,1},{1,2},{2,3},{7,4},{4,5},{5,6},{6,7},{11,8},{8,9},{9,10... | collective-permute-start | bytes 368648 | tf_op jit(solution)/shard_map/ppermute | solution.py:17
  113.9 5.8 %collective-permute-start.22 = (bf16[120,512]{1,0:T(8,128)(2,1)S(1)}, bf16[120,512]{1,0:T(8,128)(2,1)S(1)}, u32[]{:S(2)}, u32[]{:S(2)}) collective-permute-start(bf16[120,512]{1,0:T(8,128)(2,1)S(1)} %get-tuple-element.53), channel_id=1, source_target_pairs={{1,0},{2,1},{3,2},{0,3},{5,4},{6,5},{7,6},{4,7},{9,8},{10,9},{11,1... | collective-permute-start | bytes 368648 | tf_op jit(solution)/shard_map/ppermute | solution.py:17
  116.0 6.4 %collective-permute-start.23 = (bf16[120,512]{1,0:T(8,128)(2,1)S(1)}, bf16[120,512]{1,0:T(8,128)(2,1)S(1)}, u32[]{:S(2)}, u32[]{:S(2)}) collective-permute-start(bf16[120,512]{1,0:T(8,128)(2,1)S(1)} %get-tuple-element.52), channel_id=1, source_target_pairs={{2,0},{3,1},{0,2},{1,3},{6,4},{7,5},{4,6},{5,7},{10,8},{11,9},{8,1... | collective-permute-start | bytes 368648 | tf_op jit(solution)/shard_map/ppermute | solution.py:17

commit v7 on v5

--- a/solution.py
+++ b/solution.py
@@ -152,7 +152,8 @@
     half = dec_own.shape[1] // 32 * 16
     picked = picked_latents(aux_picks, blk_at + 2 * core, lat_all)
 
-    x_far = swap_core(x_all[2 * rows :])
+    far_2, far_3 = swap_core(x_all[2 * rows : 3 * rows]), swap_core(x_3)
+    x_far = jnp.concatenate([far_2, far_3], 0)
     summed = jnp.dot(x_all[: 2 * rows], enc_weight, preferred_element_type=F32)
     summed = summed + jnp.dot(x_far, enc_far, preferred_element_type=F32)
     parts = exchange_z(summed.reshape(z_size, piece, lat))

time: 125 us -> 126 us (level)
    ppermute x6 -> x7, waiting for transfers between devices: 2.79 us -> 2.29 us  [swap_core(): return lax.ppermute(block, 'core', [(0, 1), (1, 0)])]
    ppermute x6 -> x7, starting transfers between devices: 3.74 us -> 4.24 us  [swap_core(): return lax.ppermute(block, 'core', [(0, 1), (1, 0)])]
  transfers between devices with their start and end apart: 28 -> 29, of which waited for: 17 -> 18; matrix products, arithmetic and copies ran while one was open for 10% -> 9% of each run, Pallas kernels for 5% -> 5%
where the time goes in v7:
time: 126 us; the launch traced here: 125 us
  starting transfers between devices  57.1 us (45%)
  waiting for transfers between devices  39.7 us (32%)
  other arithmetic  7.9 us (6%)
  local copies, waits for them, and re-layouts  7.79 us (6%)
  Pallas kernels  7 us (6%)
  matrix products  4.19 us (3%)
    all_to_all x4, starting transfers between devices, exchange_z(): return lax.all_to_all(copies, 'z', 0, 0, tiled=True)  30.2 us
    all_to_all x4, waiting for transfers between devices, exchange_z(): return lax.all_to_all(copies, 'z', 0, 0, tiled=True)  15 us
    ppermute x8, waiting for transfers between devices, blk_move(): return lax.ppermute(block, ('blk', 'core'), route)  13.5 us
    ppermute x8, starting transfers between devices, from_ahead(): lax.ppermute(block, axis, [((i + distance) % size, i) for i in range(size)])  12 us
    ppermute x8, starting transfers between devices, blk_move(): return lax.ppermute(block, ('blk', 'core'), route)  9.39 us
    ppermute x8, waiting for transfers between devices, from_ahead(): lax.ppermute(block, axis, [((i + distance) % size, i) for i in range(size)])  8.92 us
    pallas_call x1, Pallas kernels, picked_latents(): pl.pallas_call(pick_kernel, out_shape=jax.ShapeDtypeStruct((rows, lat_all...  5.69 us
    ppermute x7, starting transfers between devices, swap_core(): return lax.ppermute(block, 'core', [(0, 1), (1, 0)])  4.24 us
  transfers between devices with their start and end apart: 29, of which 18 were waited for; matrix products, arithmetic and copies ran while one was open for 9% of the time, Pallas kernels for 5%

profile of v7, /device:TPU:32, one launch (start us, length us, event | category | flops | bytes accessed | tf_op | source)
XLA Modules:
  0.0 124.9 jit_solution(7233988514609084881)
XLA Ops:
  0.6 3.1 %collective-permute-start.2 = (bf16[128,448]{0,1:T(8,128)(2,1)}, bf16[128,448]{0,1:T(8,128)(2,1)S(1)}, u32[]{:S(2)}, u32[]{:S(2)}) collective-permute-start(bf16[128,448]{0,1:T(8,128)(2,1)} %param.7), channel_id=1, source_target_pairs={{128,0},{192,64},{0,128},{64,192},{129,1},{193,65},{1,129},{65,193... | collective-permute-start | bytes 344072 | tf_op jit(solution)/shard_map/ppermute | solution.py:17
  3.8 1.1 collective-permute-start
  4.9 0.9 collective-permute-start.1
  6.0 0.7 convert_element_type.168
  6.9 0.9 constant_dynamic-update-slice_fusion.2
  8.0 1.9 %collective-permute-done = bf16[128,448]{0,1:T(8,128)(2,1)S(1)} collective-permute-done((bf16[128,448]{0,1:T(8,128)(2,1)}, bf16[128,448]{0,1:T(8,128)(2,1)S(1)}, u32[]{:S(2)}, u32[]{:S(2)}) %collective-permute-start) | collective-permute-done | bytes 114720 | tf_op jit(solution)/shard_map/ppermute | solution.py:27
  9.9 1.2 collective-permute-done.1
  11.8 0.8 collective-permute-done.3
  13.1 1.1 convolution_add_fusion
  14.3 8.6 %all-to-all-start = ((f32[8,32,512]{2,1,0:T(8,128)}), f32[8,32,512]{2,1,0:T(8,128)S(1)}, u32[]{:S(2)}, u32[]{:S(2)}) async-start(f32[8,32,512]{2,1,0:T(8,128)} %bitcast), calls=%async_computation | async-start | bytes 1048576 | tf_op jit(solution)/shard_map/all_to_all | solution.py:51
  23.1 3.0 %collective-permute-start.8 = (bf16[512,464]{0,1:T(8,128)(2,1)}, bf16[512,464]{0,1:T(8,128)(2,1)S(1)}, u32[]{:S(2)}, u32[]{:S(2)}) collective-permute-start(bf16[512,464]{0,1:T(8,128)(2,1)} %get-tuple-element.26), channel_id=1, source_target_pairs={{0,192},{4,68},{64,0},{68,132},{128,64},{132,196},{192,128},{196,4... | collective-permute-start | bytes 1425416 | tf_op jit(solution)/shard_map/ppermute | solution.py:27
  26.1 5.7 %shard_map.102 = bf16[128,2048]{1,0:T(8,128)(2,1)} custom-call(s32[1]{0:T(128)} %bitcast.1.own_ref, s32[128,512]{1,0:T(8,128)} %picks_ref.1), custom_call_target="tpu_custom_call" | custom-call | flops 20000000 | bytes 1000000 | tf_op jit(solution)/shard_map/pallas_call | solution.py:82
  31.8 7.6 %all-to-all-done = f32[8,32,512]{2,1,0:T(8,128)S(1)} async-done(((f32[8,32,512]{2,1,0:T(8,128)}), f32[8,32,512]{2,1,0:T(8,128)S(1)}, u32[]{:S(2)}, u32[]{:S(2)}) %all-to-all-start) | async-done | bytes 524320 | tf_op jit(solution)/shard_map/all_to_all | solution.py:51
  40.2 0.7 slice.174
  40.9 1.6 %slice.173 = bf16[512,224]{0,1:T(8,128)(2,1)} slice(bf16[512,464]{0,1:T(8,128)(2,1)} %collective-permute-done.7), slice={[0:512], [0:224]} | slice | bytes 458752 | tf_op jit(solution)/shard_map/slice | solution.py:166
  42.6 0.7 broadcast_in_dim.24
  43.3 7.3 %all-to-all-start.1 = ((bf16[8,32,512]{2,1,0:T(8,128)(2,1)}), bf16[8,32,512]{2,1,0:T(8,128)(2,1)}, u32[]{:S(2)}, u32[]{:S(2)}) async-start(bf16[8,32,512]{2,1,0:T(8,128)(2,1)} %broadcast_in_dim.24), calls=%async_computation.1 | async-start | bytes 524288 | tf_op jit(solution)/shard_map/all_to_all | solution.py:51
  51.2 1.5 %collective-permute-start.10 = (bf16[512,224]{0,1:T(8,128)(2,1)}, bf16[512,224]{0,1:T(8,128)(2,1)S(1)}, u32[]{:S(2)}, u32[]{:S(2)}) collective-permute-start(bf16[512,224]{0,1:T(8,128)(2,1)} %slice.173), channel_id=1, source_target_pairs={{0,64},{4,196},{64,128},{68,4},{128,192},{132,68},{192,0},{196,132... | collective-permute-start | bytes 688136 | tf_op jit(solution)/shard_map/ppermute | solution.py:27
  52.7 1.1 constant_dynamic-update-slice_fusion.1
  53.9 6.8 %collective-permute-done.10 = bf16[512,224]{0,1:T(8,128)(2,1)S(1)} collective-permute-done((bf16[512,224]{0,1:T(8,128)(2,1)}, bf16[512,224]{0,1:T(8,128)(2,1)S(1)}, u32[]{:S(2)}, u32[]{:S(2)}) %collective-permute-start.10) | collective-permute-done | bytes 229408 | tf_op jit(solution)/shard_map/ppermute | solution.py:27
  60.8 1.3 %all-to-all-done.1 = bf16[8,32,512]{2,1,0:T(8,128)(2,1)} async-done(((bf16[8,32,512]{2,1,0:T(8,128)(2,1)}), bf16[8,32,512]{2,1,0:T(8,128)(2,1)}, u32[]{:S(2)}, u32[]{:S(2)}) %all-to-all-start.1) | async-done | bytes 262176 | tf_op jit(solution)/shard_map/all_to_all | solution.py:51
  62.3 1.0 fusion.40
  64.2 0.7 fusion.37
  65.7 0.7 fusion.18
  67.5 0.7 collective-permute-done.12
  68.6 0.8 pad_maximum_fusion.2
  69.3 6.0 %all-to-all-start.2 = ((bf16[8,136,128]{2,1,0:T(8,128)(2,1)}), bf16[8,136,128]{2,1,0:T(8,128)(2,1)S(1)}, u32[]{:S(2)}, u32[]{:S(2)}) async-start(bf16[8,136,128]{2,1,0:T(8,128)(2,1)} %pad_maximum_fusion.2), calls=%async_computation.2 | async-start | bytes 557056 | tf_op jit(solution)/shard_map/all_to_all | solution.py:51
  76.3 1.7 %collective-permute-start.16 = (bf16[112,2048]{1,0:T(8,128)(2,1)S(1)}, bf16[112,2048]{1,0:T(8,128)(2,1)}, u32[]{:S(2)}, u32[]{:S(2)}) collective-permute-start(bf16[112,2048]{1,0:T(8,128)(2,1)S(1)} %get-tuple-element.52), channel_id=1, source_target_pairs={{3,0},{0,1},{1,2},{2,3},{7,4},{4,5},{5,6},{6,7},{11,8},{8,9},{9,10... | collective-permute-start | bytes 1376264 | tf_op jit(solution)/shard_map/ppermute | solution.py:17
  78.0 1.7 %collective-permute-start.17 = (bf16[112,2048]{1,0:T(8,128)(2,1)S(1)}, bf16[112,2048]{1,0:T(8,128)(2,1)}, u32[]{:S(2)}, u32[]{:S(2)}) collective-permute-start(bf16[112,2048]{1,0:T(8,128)(2,1)S(1)} %get-tuple-element.51), channel_id=1, source_target_pairs={{1,0},{2,1},{3,2},{0,3},{5,4},{6,5},{7,6},{4,7},{9,8},{10,9},{11,1... | collective-permute-start | bytes 1376264 | tf_op jit(solution)/shard_map/ppermute | solution.py:17
  79.6 2.0 %collective-permute-start.18 = (bf16[112,2048]{1,0:T(8,128)(2,1)S(1)}, bf16[112,2048]{1,0:T(8,128)(2,1)}, u32[]{:S(2)}, u32[]{:S(2)}) collective-permute-start(bf16[112,2048]{1,0:T(8,128)(2,1)S(1)} %get-tuple-element.50), channel_id=1, source_target_pairs={{2,0},{3,1},{0,2},{1,3},{6,4},{7,5},{4,6},{5,7},{10,8},{11,9},{8,1... | collective-permute-start | bytes 1376264 | tf_op jit(solution)/shard_map/ppermute | solution.py:17
  81.6 4.8 %all-to-all-done.2 = bf16[8,136,128]{2,1,0:T(8,128)(2,1)S(1)} async-done(((bf16[8,136,128]{2,1,0:T(8,128)(2,1)}), bf16[8,136,128]{2,1,0:T(8,128)(2,1)S(1)}, u32[]{:S(2)}, u32[]{:S(2)}) %all-to-all-start.2) | async-done | bytes 278560 | tf_op jit(solution)/shard_map/all_to_all | solution.py:51
  87.2 0.7 broadcast_in_dim.28
  87.9 8.4 %all-to-all-start.3 = ((bf16[8,32,512]{2,1,0:T(8,128)(2,1)}), bf16[8,32,512]{2,1,0:T(8,128)(2,1)S(1)}, u32[]{:S(2)}, u32[]{:S(2)}) async-start(bf16[8,32,512]{2,1,0:T(8,128)(2,1)} %broadcast_in_dim.28), calls=%async_computation.3 | async-start | bytes 524288 | tf_op jit(solution)/shard_map/all_to_all | solution.py:51
  96.3 1.2 %collective-permute-start.15 = (f32[1,128]{1,0:T(1,128)S(1)}, f32[1,128]{1,0:T(1,128)S(1)}, u32[]{:S(2)}, u32[]{:S(2)}) collective-permute-start(f32[1,128]{1,0:T(1,128)S(1)} %slice_add_fusion.2), channel_id=1, source_target_pairs={{0,4},{4,0},{1,5},{5,1},{2,6},{6,2},{3,7},{7,3},{8,12},{12,8},{9,1... | collective-permute-start | bytes 1544 | tf_op jit(solution)/shard_map/ppermute | solution.py:31
  97.6 1.3 %collective-permute-done.17 = bf16[112,2048]{1,0:T(8,128)(2,1)} collective-permute-done((bf16[112,2048]{1,0:T(8,128)(2,1)S(1)}, bf16[112,2048]{1,0:T(8,128)(2,1)}, u32[]{:S(2)}, u32[]{:S(2)}) %collective-permute-start.17) | collective-permute-done | bytes 458784 | tf_op jit(solution)/shard_map/ppermute | solution.py:17
  98.9 1.9 %collective-permute-done.18 = bf16[112,2048]{1,0:T(8,128)(2,1)} collective-permute-done((bf16[112,2048]{1,0:T(8,128)(2,1)S(1)}, bf16[112,2048]{1,0:T(8,128)(2,1)}, u32[]{:S(2)}, u32[]{:S(2)}) %collective-permute-start.18) | collective-permute-done | bytes 458784 | tf_op jit(solution)/shard_map/ppermute | solution.py:17
  100.8 1.6 %add_convert_fusion = bf16[112,2048]{1,0:T(8,128)(2,1)S(1)} fusion(bf16[112,2048]{1,0:T(8,128)(2,1)} %collective-permute-done.18, bf16[112,2048]{1,0:T(8,128)(2,1)} %collective-permute-done.17, bf16[112,2048]{1,0:T(8,128)(2,1)} %collective-permute-done.16, bf16[112,2048]{1,0:T(8,128)(2,1)S(1)} %get-tuple-element.35), kind=kLoop, calls=%fused_computation.8 | loop fusion | flops 1835008 | bytes 2293760 | tf_op jit(solution)/shard_map/convert_element_type | solution.py:232
  102.8 1.8 %collective-permute-start.20 = (bf16[120,512]{1,0:T(8,128)(2,1)S(1)}, bf16[120,512]{1,0:T(8,128)(2,1)S(1)}, u32[]{:S(2)}, u32[]{:S(2)}) collective-permute-start(bf16[120,512]{1,0:T(8,128)(2,1)S(1)} %get-tuple-element.76), channel_id=1, source_target_pairs={{0,64},{4,196},{64,128},{68,4},{128,192},{132,68},{192,0},{196,132... | collective-permute-start | bytes 368648 | tf_op jit(solution)/shard_map/ppermute | solution.py:27
  104.9 1.3 %all-to-all-done.3 = bf16[8,32,512]{2,1,0:T(8,128)(2,1)S(1)} async-done(((bf16[8,32,512]{2,1,0:T(8,128)(2,1)}), bf16[8,32,512]{2,1,0:T(8,128)(2,1)S(1)}, u32[]{:S(2)}, u32[]{:S(2)}) %all-to-all-start.3) | async-done | bytes 262176 | tf_op jit(solution)/shard_map/all_to_all | solution.py:51
  106.1 1.8 %collective-permute-start.14 = (bf16[256,512]{1,0:T(8,128)(2,1)S(1)}, bf16[256,512]{1,0:T(8,128)(2,1)S(1)}, u32[]{:S(2)}, u32[]{:S(2)}) collective-permute-start(bf16[256,512]{1,0:T(8,128)(2,1)S(1)} %bitcast.55), channel_id=1, source_target_pairs={{0,4},{4,0},{1,5},{5,1},{2,6},{6,2},{3,7},{7,3},{8,12},{12,8},{9,1... | collective-permute-start | bytes 786440 | tf_op jit(solution)/shard_map/ppermute | solution.py:31
  108.3 3.2 %collective-permute-done.20 = bf16[120,512]{1,0:T(8,128)(2,1)S(1)} collective-permute-done((bf16[120,512]{1,0:T(8,128)(2,1)S(1)}, bf16[120,512]{1,0:T(8,128)(2,1)S(1)}, u32[]{:S(2)}, u32[]{:S(2)}) %collective-permute-start.20) | collective-permute-done | bytes 122912 | tf_op jit(solution)/shard_map/ppermute | solution.py:27
  112.5 1.2 collective-permute-start.22
  113.7 2.1 %collective-permute-start.23 = (bf16[120,512]{1,0:T(8,128)(2,1)S(1)}, bf16[120,512]{1,0:T(8,128)(2,1)S(1)}, u32[]{:S(2)}, u32[]{:S(2)}) collective-permute-start(bf16[120,512]{1,0:T(8,128)(2,1)S(1)} %get-tuple-element.59), channel_id=1, source_target_pairs={{1,0},{2,1},{3,2},{0,3},{5,4},{6,5},{7,6},{4,7},{9,8},{10,9},{11,1... | collective-permute-start | bytes 368648 | tf_op jit(solution)/shard_map/ppermute | solution.py:17
  115.9 0.7 add_bitcast_fusion
  116.6 3.3 %collective-permute-done.22 = bf16[120,512]{1,0:T(8,128)(2,1)S(1)} collective-permute-done((bf16[120,512]{1,0:T(8,128)(2,1)S(1)}, bf16[120,512]{1,0:T(8,128)(2,1)S(1)}, u32[]{:S(2)}, u32[]{:S(2)}) %collective-permute-start.22) | collective-permute-done | bytes 122912 | tf_op jit(solution)/shard_map/ppermute | solution.py:17
  119.9 2.3 %collective-permute-done.24 = bf16[120,512]{1,0:T(8,128)(2,1)S(1)} collective-permute-done((bf16[120,512]{1,0:T(8,128)(2,1)S(1)}, bf16[120,512]{1,0:T(8,128)(2,1)S(1)}, u32[]{:S(2)}, u32[]{:S(2)}) %collective-permute-start.24) | collective-permute-done | bytes 122912 | tf_op jit(solution)/shard_map/ppermute | solution.py:17
  122.8 1.3 %shard_map.103 = (f32[1,1]{1,0:T(1,128)}, f32[1,128]{1,0:T(1,128)}) custom-call(f32[3,128]{1,0:T(4,128)} %convert_add_fusion.1.last_ref), custom_call_target="tpu_custom_call" | custom-call | tf_op jit(solution)/shard_map/pallas_call | solution.py:116
  124.1 0.8 fusion.25
  (104 shorter events, 11.0 us)
Async XLA Ops:
  0.6 6.3 %copy-start.3 = (bf16[512,448]{0,1:T(8,128)(2,1)S(1)}, bf16[512,448]{0,1:T(8,128)(2,1)}, u32[]{:S(2)}) copy-start(bf16[512,448]{0,1:T(8,128)(2,1)} %param.11) | copy-start | bytes 1376260
  0.6 7.4 %collective-permute-start.2 = (bf16[128,448]{0,1:T(8,128)(2,1)}, bf16[128,448]{0,1:T(8,128)(2,1)S(1)}, u32[]{:S(2)}, u32[]{:S(2)}) collective-permute-start(bf16[128,448]{0,1:T(8,128)(2,1)} %param.7), channel_id=1, source_target_pairs={{128,0},{192,64},{0,128},{64,192},{129,1},{193,65},{1,129},{65,193... | collective-permute-start | bytes 344072 | tf_op jit(solution)/shard_map/ppermute | solution.py:17
  3.8 6.1 %collective-permute-start = (bf16[128,448]{0,1:T(8,128)(2,1)}, bf16[128,448]{0,1:T(8,128)(2,1)S(1)}, u32[]{:S(2)}, u32[]{:S(2)}) collective-permute-start(bf16[128,448]{0,1:T(8,128)(2,1)} %param.7), channel_id=1, source_target_pairs={{0,192},{4,68},{64,0},{68,132},{128,64},{132,196},{192,128},{196,4... | collective-permute-start | bytes 344072 | tf_op jit(solution)/shard_map/ppermute | solution.py:27
  4.9 6.2 %collective-permute-start.1 = (bf16[128,448]{0,1:T(8,128)(2,1)}, bf16[128,448]{0,1:T(8,128)(2,1)S(1)}, u32[]{:S(2)}, u32[]{:S(2)}) collective-permute-start(bf16[128,448]{0,1:T(8,128)(2,1)} %param.7), channel_id=1, source_target_pairs={{0,64},{4,196},{64,128},{68,4},{128,192},{132,68},{192,0},{196,132... | collective-permute-start | bytes 344072 | tf_op jit(solution)/shard_map/ppermute | solution.py:27
  5.8 7.0 %collective-permute-start.5 = (bf16[448,512]{1,0:T(8,128)(2,1)}, bf16[448,512]{1,0:T(8,128)(2,1)S(1)}, u32[]{:S(2)}, u32[]{:S(2)}) collective-permute-start(bf16[448,512]{1,0:T(8,128)(2,1)} %param.9), channel_id=1, source_target_pairs={{0,4},{4,0},{1,5},{5,1},{2,6},{6,2},{3,7},{7,3},{8,12},{12,8},{9,1... | collective-permute-start | bytes 1376264 | tf_op jit(solution)/shard_map/ppermute | solution.py:31
  6.7 1.2 copy-start.6
  6.9 6.2 %copy-start.4 = (bf16[448,512]{1,0:T(8,128)(2,1)S(1)}, bf16[448,512]{1,0:T(8,128)(2,1)}, u32[]{:S(2)}) copy-start(bf16[448,512]{1,0:T(8,128)(2,1)} %param.9) | copy-start | bytes 1376260
  11.2 1.4 %collective-permute-start.3 = (bf16[128,448]{0,1:T(8,128)(2,1)S(1)}, bf16[128,448]{0,1:T(8,128)(2,1)S(1)}, u32[]{:S(2)}, u32[]{:S(2)}) collective-permute-start(bf16[128,448]{0,1:T(8,128)(2,1)S(1)} %slice.224), channel_id=1, source_target_pairs={{0,4},{4,0},{1,5},{5,1},{2,6},{6,2},{3,7},{7,3},{8,12},{12,8},{9,1... | collective-permute-start | bytes 344072 | tf_op jit(solution)/shard_map/ppermute | solution.py:31
  11.3 1.5 %collective-permute-start.4 = (bf16[128,448]{0,1:T(8,128)(2,1)S(1)}, bf16[128,448]{0,1:T(8,128)(2,1)S(1)}, u32[]{:S(2)}, u32[]{:S(2)}) collective-permute-start(bf16[128,448]{0,1:T(8,128)(2,1)S(1)} %collective-permute-done.1), channel_id=1, source_target_pairs={{0,4},{4,0},{1,5},{5,1},{2,6},{6,2},{3,7},{7,3},{8,12},{12,8},{9,1... | collective-permute-start | bytes 344072 | tf_op jit(solution)/shard_map/ppermute | solution.py:31
  13.1 26.3 %copy-start.8 = (f32[512]{0:T(512)S(1)}, f32[512]{0:T(512)}, u32[]{:S(2)}) copy-start(f32[512]{0:T(512)} %param.10) | copy-start | bytes 6148
  14.3 25.1 %all-to-all-start = ((f32[8,32,512]{2,1,0:T(8,128)}), f32[8,32,512]{2,1,0:T(8,128)S(1)}, u32[]{:S(2)}, u32[]{:S(2)}) async-start(f32[8,32,512]{2,1,0:T(8,128)} %bitcast), calls=%async_computation | async-start | bytes 1048576 | tf_op jit(solution)/shard_map/all_to_all | solution.py:51
  22.9 17.3 %collective-permute-start.7 = (bf16[512,464]{0,1:T(8,128)(2,1)}, bf16[512,464]{0,1:T(8,128)(2,1)}, u32[]{:S(2)}, u32[]{:S(2)}) collective-permute-start(bf16[512,464]{0,1:T(8,128)(2,1)} %get-tuple-element.26), channel_id=1, source_target_pairs={{0,64},{4,196},{64,128},{68,4},{128,192},{132,68},{192,0},{196,132... | collective-permute-start | bytes 1425416 | tf_op jit(solution)/shard_map/ppermute | solution.py:27
  23.1 17.1 %collective-permute-start.8 = (bf16[512,464]{0,1:T(8,128)(2,1)}, bf16[512,464]{0,1:T(8,128)(2,1)S(1)}, u32[]{:S(2)}, u32[]{:S(2)}) collective-permute-start(bf16[512,464]{0,1:T(8,128)(2,1)} %get-tuple-element.26), channel_id=1, source_target_pairs={{0,192},{4,68},{64,0},{68,132},{128,64},{132,196},{192,128},{196,4... | collective-permute-start | bytes 1425416 | tf_op jit(solution)/shard_map/ppermute | solution.py:27
  39.5 3.1 %collective-permute-start.6 = (bf16[32,512]{1,0:T(8,128)(2,1)S(1)}, bf16[32,512]{1,0:T(8,128)(2,1)S(1)}, u32[]{:S(2)}, u32[]{:S(2)}) collective-permute-start(bf16[32,512]{1,0:T(8,128)(2,1)S(1)} %maximum_convert_fusion), channel_id=1, source_target_pairs={{0,0},{4,132},{8,8},{12,140},{16,16},{20,148},{24,24},{28,156},{32... | collective-permute-start | bytes 98312 | tf_op jit(solution)/shard_map/ppermute | solution.py:43
  43.3 18.9 %all-to-all-start.1 = ((bf16[8,32,512]{2,1,0:T(8,128)(2,1)}), bf16[8,32,512]{2,1,0:T(8,128)(2,1)}, u32[]{:S(2)}, u32[]{:S(2)}) async-start(bf16[8,32,512]{2,1,0:T(8,128)(2,1)} %broadcast_in_dim.24), calls=%async_computation.1 | async-start | bytes 524288 | tf_op jit(solution)/shard_map/all_to_all | solution.py:51
  50.7 10.1 %collective-permute-start.11 = (bf16[512,240]{0,1:T(8,128)(2,1)}, bf16[512,240]{0,1:T(8,128)(2,1)S(1)}, u32[]{:S(2)}, u32[]{:S(2)}) collective-permute-start(bf16[512,240]{0,1:T(8,128)(2,1)} %slice.174), channel_id=1, source_target_pairs={{0,192},{4,68},{64,0},{68,132},{128,64},{132,196},{192,128},{196,4... | collective-permute-start | bytes 737288 | tf_op jit(solution)/shard_map/ppermute | solution.py:27
  51.2 9.5 %collective-permute-start.10 = (bf16[512,224]{0,1:T(8,128)(2,1)}, bf16[512,224]{0,1:T(8,128)(2,1)S(1)}, u32[]{:S(2)}, u32[]{:S(2)}) collective-permute-start(bf16[512,224]{0,1:T(8,128)(2,1)} %slice.173), channel_id=1, source_target_pairs={{0,64},{4,196},{64,128},{68,4},{128,192},{132,68},{192,0},{196,132... | collective-permute-start | bytes 688136 | tf_op jit(solution)/shard_map/ppermute | solution.py:27
  52.7 11.2 %copy-start = (bf16[128,2048]{1,0:T(8,128)(2,1)S(1)}, bf16[128,2048]{1,0:T(8,128)(2,1)}, u32[]{:S(2)}) copy-start(bf16[128,2048]{1,0:T(8,128)(2,1)} %shard_map.102) | copy-start | bytes 1572868
  62.2 1.7 %collective-permute-start.9 = (bf16[2,128,512]{2,1,0:T(8,128)(2,1)}, bf16[2,128,512]{2,1,0:T(8,128)(2,1)S(1)}, u32[]{:S(2)}, u32[]{:S(2)}) collective-permute-start(bf16[2,128,512]{2,1,0:T(8,128)(2,1)} %bitcast.4), channel_id=1, source_target_pairs={{0,4},{4,0},{1,5},{5,1},{2,6},{6,2},{3,7},{7,3},{8,12},{12,8},{9,1... | collective-permute-start | bytes 786440 | tf_op jit(solution)/shard_map/ppermute | solution.py:31
  64.1 0.8 copy-start.1
  64.2 1.0 copy-start.7
  66.6 1.6 %collective-permute-start.12 = (bf16[128,1024]{1,0:T(8,128)(2,1)S(1)}, bf16[128,1024]{1,0:T(8,128)(2,1)S(1)}, u32[]{:S(2)}, u32[]{:S(2)}) collective-permute-start(bf16[128,1024]{1,0:T(8,128)(2,1)S(1)} %fusion.5), channel_id=1, source_target_pairs={{0,4},{4,0},{1,5},{5,1},{2,6},{6,2},{3,7},{7,3},{8,12},{12,8},{9,1... | collective-permute-start | bytes 786440 | tf_op jit(solution)/shard_map/ppermute | solution.py:31
  67.4 7.9 %copy-start.2 = (bf16[128,2048]{1,0:T(8,128)(2,1)S(1)}, bf16[128,2048]{1,0:T(8,128)(2,1)}, u32[]{:S(2)}) copy-start(bf16[128,2048]{1,0:T(8,128)(2,1)} %copy-done.1) | copy-start | bytes 1572868
  67.5 7.9 %copy-start.5 = (bf16[256,464]{0,1:T(8,128)(2,1)S(1)}, bf16[256,464]{0,1:T(8,128)(2,1)}, u32[]{:S(2)}) copy-start(bf16[256,464]{0,1:T(8,128)(2,1)} %fusion.18) | copy-start | bytes 712708
  69.3 17.1 %all-to-all-start.2 = ((bf16[8,136,128]{2,1,0:T(8,128)(2,1)}), bf16[8,136,128]{2,1,0:T(8,128)(2,1)S(1)}, u32[]{:S(2)}, u32[]{:S(2)}) async-start(bf16[8,136,128]{2,1,0:T(8,128)(2,1)} %pad_maximum_fusion.2), calls=%async_computation.2 | async-start | bytes 557056 | tf_op jit(solution)/shard_map/all_to_all | solution.py:51
  76.3 21.2 %collective-permute-start.16 = (bf16[112,2048]{1,0:T(8,128)(2,1)S(1)}, bf16[112,2048]{1,0:T(8,128)(2,1)}, u32[]{:S(2)}, u32[]{:S(2)}) collective-permute-start(bf16[112,2048]{1,0:T(8,128)(2,1)S(1)} %get-tuple-element.52), channel_id=1, source_target_pairs={{3,0},{0,1},{1,2},{2,3},{7,4},{4,5},{5,6},{6,7},{11,8},{8,9},{9,10... | collective-permute-start | bytes 1376264 | tf_op jit(solution)/shard_map/ppermute | solution.py:17
  78.0 20.9 %collective-permute-start.17 = (bf16[112,2048]{1,0:T(8,128)(2,1)S(1)}, bf16[112,2048]{1,0:T(8,128)(2,1)}, u32[]{:S(2)}, u32[]{:S(2)}) collective-permute-start(bf16[112,2048]{1,0:T(8,128)(2,1)S(1)} %get-tuple-element.51), channel_id=1, source_target_pairs={{1,0},{2,1},{3,2},{0,3},{5,4},{6,5},{7,6},{4,7},{9,8},{10,9},{11,1... | collective-permute-start | bytes 1376264 | tf_op jit(solution)/shard_map/ppermute | solution.py:17
  79.6 21.2 %collective-permute-start.18 = (bf16[112,2048]{1,0:T(8,128)(2,1)S(1)}, bf16[112,2048]{1,0:T(8,128)(2,1)}, u32[]{:S(2)}, u32[]{:S(2)}) collective-permute-start(bf16[112,2048]{1,0:T(8,128)(2,1)S(1)} %get-tuple-element.50), channel_id=1, source_target_pairs={{2,0},{3,1},{0,2},{1,3},{6,4},{7,5},{4,6},{5,7},{10,8},{11,9},{8,1... | collective-permute-start | bytes 1376264 | tf_op jit(solution)/shard_map/ppermute | solution.py:17
  86.5 0.7 collective-permute-start.13
  87.9 18.2 %all-to-all-start.3 = ((bf16[8,32,512]{2,1,0:T(8,128)(2,1)}), bf16[8,32,512]{2,1,0:T(8,128)(2,1)S(1)}, u32[]{:S(2)}, u32[]{:S(2)}) async-start(bf16[8,32,512]{2,1,0:T(8,128)(2,1)} %broadcast_in_dim.28), calls=%async_computation.3 | async-start | bytes 524288 | tf_op jit(solution)/shard_map/all_to_all | solution.py:51
  96.3 6.1 %collective-permute-start.15 = (f32[1,128]{1,0:T(1,128)S(1)}, f32[1,128]{1,0:T(1,128)S(1)}, u32[]{:S(2)}, u32[]{:S(2)}) collective-permute-start(f32[1,128]{1,0:T(1,128)S(1)} %slice_add_fusion.2), channel_id=1, source_target_pairs={{0,4},{4,0},{1,5},{5,1},{2,6},{6,2},{3,7},{7,3},{8,12},{12,8},{9,1... | collective-permute-start | bytes 1544 | tf_op jit(solution)/shard_map/ppermute | solution.py:31
  102.6 5.8 %collective-permute-start.19 = (bf16[120,512]{1,0:T(8,128)(2,1)S(1)}, bf16[120,512]{1,0:T(8,128)(2,1)S(1)}, u32[]{:S(2)}, u32[]{:S(2)}) collective-permute-start(bf16[120,512]{1,0:T(8,128)(2,1)S(1)} %get-tuple-element.75), channel_id=1, source_target_pairs={{0,192},{4,68},{64,0},{68,132},{128,64},{132,196},{192,128},{196,4... | collective-permute-start | bytes 368648 | tf_op jit(solution)/shard_map/ppermute | solution.py:27
  102.8 8.7 %collective-permute-start.20 = (bf16[120,512]{1,0:T(8,128)(2,1)S(1)}, bf16[120,512]{1,0:T(8,128)(2,1)S(1)}, u32[]{:S(2)}, u32[]{:S(2)}) collective-permute-start(bf16[120,512]{1,0:T(8,128)(2,1)S(1)} %get-tuple-element.76), channel_id=1, source_target_pairs={{0,64},{4,196},{64,128},{68,4},{128,192},{132,68},{192,0},{196,132... | collective-permute-start | bytes 368648 | tf_op jit(solution)/shard_map/ppermute | solution.py:27
  104.7 6.9 %collective-permute-start.21 = (bf16[120,512]{1,0:T(8,128)(2,1)S(1)}, bf16[120,512]{1,0:T(8,128)(2,1)S(1)}, u32[]{:S(2)}, u32[]{:S(2)}) collective-permute-start(bf16[120,512]{1,0:T(8,128)(2,1)S(1)} %get-tuple-element.74), channel_id=1, source_target_pairs={{128,0},{192,64},{0,128},{64,192},{129,1},{193,65},{1,129},{65,193... | collective-permute-start | bytes 368648 | tf_op jit(solution)/shard_map/ppermute | solution.py:17
  106.1 5.6 %collective-permute-start.14 = (bf16[256,512]{1,0:T(8,128)(2,1)S(1)}, bf16[256,512]{1,0:T(8,128)(2,1)S(1)}, u32[]{:S(2)}, u32[]{:S(2)}) collective-permute-start(bf16[256,512]{1,0:T(8,128)(2,1)S(1)} %bitcast.55), channel_id=1, source_target_pairs={{0,4},{4,0},{1,5},{5,1},{2,6},{6,2},{3,7},{7,3},{8,12},{12,8},{9,1... | collective-permute-start | bytes 786440 | tf_op jit(solution)/shard_map/ppermute | solution.py:31
  112.5 7.4 %collective-permute-start.22 = (bf16[120,512]{1,0:T(8,128)(2,1)S(1)}, bf16[120,512]{1,0:T(8,128)(2,1)S(1)}, u32[]{:S(2)}, u32[]{:S(2)}) collective-permute-start(bf16[120,512]{1,0:T(8,128)(2,1)S(1)} %get-tuple-element.60), channel_id=1, source_target_pairs={{3,0},{0,1},{1,2},{2,3},{7,4},{4,5},{5,6},{6,7},{11,8},{8,9},{9,10... | collective-permute-start | bytes 368648 | tf_op jit(solution)/shard_map/ppermute | solution.py:17
  113.7 6.2 %collective-permute-start.23 = (bf16[120,512]{1,0:T(8,128)(2,1)S(1)}, bf16[120,512]{1,0:T(8,128)(2,1)S(1)}, u32[]{:S(2)}, u32[]{:S(2)}) collective-permute-start(bf16[120,512]{1,0:T(8,128)(2,1)S(1)} %get-tuple-element.59), channel_id=1, source_target_pairs={{1,0},{2,1},{3,2},{0,3},{5,4},{6,5},{7,6},{4,7},{9,8},{10,9},{11,1... | collective-permute-start | bytes 368648 | tf_op jit(solution)/shard_map/ppermute | solution.py:17
  115.8 6.4 %collective-permute-start.24 = (bf16[120,512]{1,0:T(8,128)(2,1)S(1)}, bf16[120,512]{1,0:T(8,128)(2,1)S(1)}, u32[]{:S(2)}, u32[]{:S(2)}) collective-permute-start(bf16[120,512]{1,0:T(8,128)(2,1)S(1)} %get-tuple-element.58), channel_id=1, source_target_pairs={{2,0},{3,1},{0,2},{1,3},{6,4},{7,5},{4,6},{5,7},{10,8},{11,9},{8,1... | collective-permute-start | bytes 368648 | tf_op jit(solution)/shard_map/ppermute | solution.py:17
